TPU v7x, 512 devices: a whole 4x8x8 slice. The times are simulated.
512 devices in a mesh: blk: 64 (over y_lo, z, core), uly: 8 (over x, y_hi).
Axes of the slice: x: 4, y: 8 (y_hi: 2, y_lo: 4; y = y_hi * 4 + y_lo), z: 8, core: 2. Of those that a mesh axis runs over, the one named last changes fastest.
Arguments:
- queries: bfloat16 [65536, 2048], P(('blk', 'uly')), may hold values from -6.5 to 6.5
- key_rows: bfloat16 [65536, 256], P(('blk', 'uly')), may hold values from -6.5 to 6.5
- value_rows: bfloat16 [65536, 256], P(('blk', 'uly')), may hold values from -6 to 6
- span_place: int32 [65536], P(('blk', 'uly')), may hold values from 0 to 65535
- span_offset: int32 [65536], P(('blk', 'uly')), may hold values from 0 to 511
- segment_number: int32 [65536], replicated, may hold values from 0 to 4095, never falling along the last dimension, each value on 1 to 32 neighbouring positions
- block_class: int32 [64], replicated, may hold values from 0 to 2
Outputs:
- attended: bfloat16 [65536, 2048], P(('blk', 'uly'))
Inputs may be any that keep to these rules, and one draw needn't show every extreme that they name: `segment_number`: segment numbers never fall along the sequence.
All inputs are finite; a program needn't handle non-finite values.
Results may differ from a plain program's by a relative error of at most 0.009.
Values may be sent and summed in bfloat16 or wider, within the bound.
No kernel may reach another device: no remote copies, remote signals or barrier semaphores. Data moves between devices by JAX's collectives and lax.ppermute only.
A program may use at most 64 MiB of HBM per device.

v0:
```python
import jax
import jax.numpy as jnp
from jax import lax
from jax.sharding import PartitionSpec as P

HEAD_DIM = 128
KV_GROUPS = 2


def from_behind(block, axis, distance):
    devices = range(lax.axis_size(axis))
    route = [(i - distance, i) for i in devices if i - distance in devices]
    return lax.ppermute(block, axis, route)


def rope_pair(part, where):
    half_width = part.shape[-1] // 2
    inverse = 10000.0 ** (-jnp.arange(half_width, dtype=jnp.float32) / half_width)
    angle = where.astype(jnp.float32)[:, None] * inverse[None, :]
    cosine = jnp.cos(angle)[:, None, :]
    sine = jnp.sin(angle)[:, None, :]
    first = part[..., :half_width]
    second = part[..., half_width:]
    return jnp.concatenate(
        [first * cosine - second * sine, second * cosine + first * sine], axis=-1
    )


def rotary(rows, major, minor):
    count = rows.shape[0]
    heads = rows.reshape(count, -1, HEAD_DIM).astype(jnp.float32)
    quarter = HEAD_DIM // 4
    turned = jnp.concatenate(
        [
            rope_pair(heads[..., :quarter], major),
            rope_pair(heads[..., quarter : 2 * quarter], minor),
            heads[..., 2 * quarter :],
        ],
        axis=-1,
    )
    return turned.reshape(count, -1).astype(jnp.bfloat16)


def visible(klass, query_pos, key_pos, query_ctx, key_ctx, limit):
    valid = (key_pos >= 0) & (key_pos < limit)
    earlier = key_pos[None, :] <= query_pos[:, None]
    infill = key_ctx[None, :] | jnp.logical_not(query_ctx)[:, None] & earlier
    rule = jnp.where(klass == 0, True, jnp.where(klass == 1, earlier, infill))
    return valid[None, :] & rule


def softmax_rows(query_block, keys, values, allowed):
    scores = lax.dot_general(
        query_block, keys, (((1,), (1,)), ((), ())), preferred_element_type=jnp.float32
    ) * HEAD_DIM ** (-0.5)
    scores = jnp.where(allowed, scores, -1e30)
    top = jnp.max(scores, axis=1, keepdims=True)
    expon = jnp.exp(scores - top)
    total = jnp.sum(expon, axis=1, keepdims=True)
    weights = (expon / total).astype(jnp.bfloat16)
    return jnp.dot(weights, values, preferred_element_type=jnp.float32).astype(jnp.bfloat16)


def shards(queries, key_rows, value_rows, span_place, span_offset, segment_number, block_class):
    local_rows = queries.shape[0]
    ulysses = lax.axis_size("uly")
    blocks = lax.axis_size("blk")
    block = local_rows * ulysses
    margin = 2 * block
    q_rot = rotary(queries, span_place, span_offset)
    k_rot = rotary(key_rows, span_place, span_offset)
    head_major = lax.all_to_all(q_rot, "uly", split_axis=1, concat_axis=0, tiled=True)
    head_count = head_major.shape[1] // HEAD_DIM
    group = lax.axis_index("uly") // (ulysses // KV_GROUPS)
    block_index = lax.axis_index("blk")
    paired = jnp.stack([k_rot, value_rows])
    whole = lax.all_gather(paired, "uly", axis=1, tiled=True)
    mine = lax.dynamic_slice_in_dim(whole, group * HEAD_DIM, HEAD_DIM, 2)
    pieces = []
    for offset in (2, 1, 0, -1, -2):
        if offset == 0:
            pieces.append(mine)
        else:
            pieces.append(from_behind(mine, "blk", offset))
    window = jnp.stack(pieces)
    keys = window[:, 0].reshape(5 * block, HEAD_DIM)
    values = window[:, 1].reshape(5 * block, HEAD_DIM)
    context = segment_number % 2 == 0
    c_pad = jnp.pad(context, (margin, margin))
    start = block_index * block
    key_ctx = lax.dynamic_slice_in_dim(c_pad, start, 5 * block, 0)
    query_ctx = lax.dynamic_slice_in_dim(context, start, block, 0)
    klass = lax.dynamic_index_in_dim(block_class, block_index, 0, False)
    width_q = min(512, block)
    parts = block // width_q
    limit = block * blocks
    key_count = 5 * block

    def item(number):
        head = number // parts
        first = number % parts * width_q
        q_part = lax.dynamic_slice(head_major, (first, head * HEAD_DIM), (width_q, HEAD_DIM))
        query_pos = start + first + jnp.arange(width_q, dtype=jnp.int32)
        key_pos = start - margin + jnp.arange(key_count, dtype=jnp.int32)
        own_ctx = lax.dynamic_slice_in_dim(query_ctx, first, width_q, 0)
        allowed = visible(klass, query_pos, key_pos, own_ctx, key_ctx, limit)
        return softmax_rows(q_part, keys, values, allowed)

    outs = lax.map(item, jnp.arange(head_count * parts, dtype=jnp.int32))
    outs = outs.reshape(head_count, parts, width_q, HEAD_DIM)
    attended = jnp.transpose(outs, (1, 2, 0, 3)).reshape(block, head_count * HEAD_DIM)
    return lax.all_to_all(attended, "uly", split_axis=0, concat_axis=1, tiled=True)


def solution(mesh):
    in_specs = (
        P(("blk", "uly"), None),
        P(("blk", "uly"), None),
        P(("blk", "uly"), None),
        P(("blk", "uly")),
        P(("blk", "uly")),
        P(),
        P(),
    )
    out_specs = P(("blk", "uly"), None)
    return jax.shard_map(shards, mesh=mesh, in_specs=in_specs, out_specs=out_specs, check_vma=False)
```

profile of v0, /device:TPU:8, one launch (start us, length us, event | category | flops | bytes accessed | tf_op | source)
XLA Modules:
  0.0 201.0 jit_solution(14325300874380217707)
XLA Ops:
  6.5 0.9 convert_element_type.55
  7.5 0.1 slice.71
  7.7 0.7 convert_element_type.52
  8.3 0.7 convert_element_type.53
  9.0 0.1 multiply_cosine_fusion
  9.1 0.1 copy.16
  9.2 0.1 copy.17
  9.3 0.1 copy.18
  9.4 0.1 copy.19
  9.5 0.5 add_convert_fusion
  10.0 1.0 concatenate.9
  11.1 1.5 pad_maximum_fusion
  12.6 0.3 copy.14
  12.9 0.1 convert_element_type.51
  13.0 0.7 fusion.11
  13.7 0.7 fusion.12
  14.4 0.7 fusion.13
  15.0 0.7 fusion.14
  15.7 0.7 slice_dynamic-update-slice_fusion
  16.4 8.7 %all-to-all-start = ((bf16[128,8,256]{0,2,1:T(8,128)(2,1)}), bf16[128,8,256]{0,2,1:T(8,128)(2,1)S(1)}, u32[]{:S(2)}, u32[]{:S(2)}) async-start(bf16[128,8,256]{0,2,1:T(8,128)(2,1)} %bitcast.5), calls=%async_computation | async-start | bytes 1048576 | tf_op jit(solution)/shard_map/all_to_all | solution.py:72
  25.1 62.1 %all-gather.2.cloned.1.call-done = bf16[2,1024,256]{2,1,0:T(8,128)(2,1)} async-done(((bf16[2,128,256]{2,1,0:T(8,128)(2,1)}), bf16[2,1024,256]{2,1,0:T(8,128)(2,1)}) %all-gather.2.cloned.1.call-update) | async-done | bytes 1048592 | tf_op jit(solution)/shard_map/all_gather | solution.py:77
  87.2 2.0 constant_dynamic-slice_fusion
  89.2 3.5 %collective-permute-start = (bf16[2,1024,128]{2,1,0:T(8,128)(2,1)}, bf16[2,1024,128]{2,1,0:T(8,128)(2,1)S(1)}, u32[]{:S(2)}, u32[]{:S(2)}) collective-permute-start(bf16[2,1024,128]{2,1,0:T(8,128)(2,1)} %constant_dynamic-slice_fusion), channel_id=1, source_target_pairs={{0,16},{8,24},{16,32},{24,40},{32,48},{40,56},{48,64},{56,72},{64,... | collective-permute-start | bytes 1572872 | tf_op jit(solution)/shard_map/ppermute | solution.py:13
  92.8 1.9 collective-permute-start.1
  94.7 0.1 fusion.10
  94.9 0.6 dynamic_slice.32
  96.8 0.2 copy.15
  97.0 5.8 %collective-permute-start.2 = (bf16[2,1024,128]{2,1,0:T(8,128)(2,1)}, bf16[2,1024,128]{2,1,0:T(8,128)(2,1)S(1)}, u32[]{:S(2)}, u32[]{:S(2)}) collective-permute-start(bf16[2,1024,128]{2,1,0:T(8,128)(2,1)} %constant_dynamic-slice_fusion), channel_id=1, source_target_pairs={{8,0},{16,8},{24,16},{32,24},{40,32},{48,40},{56,48},{64,56},{72,6... | collective-permute-start | bytes 1572872 | tf_op jit(solution)/shard_map/ppermute | solution.py:13
  102.7 2.3 %collective-permute-start.3 = (bf16[2,1024,128]{2,1,0:T(8,128)(2,1)}, bf16[2,1024,128]{2,1,0:T(8,128)(2,1)S(1)}, u32[]{:S(2)}, u32[]{:S(2)}) collective-permute-start(bf16[2,1024,128]{2,1,0:T(8,128)(2,1)} %constant_dynamic-slice_fusion), channel_id=1, source_target_pairs={{16,0},{24,8},{32,16},{40,24},{48,32},{56,40},{64,48},{72,56},{80,... | collective-permute-start | bytes 1572872 | tf_op jit(solution)/shard_map/ppermute | solution.py:13
  105.0 3.2 %collective-permute-done = bf16[2,1024,128]{2,1,0:T(8,128)(2,1)S(1)} collective-permute-done((bf16[2,1024,128]{2,1,0:T(8,128)(2,1)}, bf16[2,1024,128]{2,1,0:T(8,128)(2,1)S(1)}, u32[]{:S(2)}, u32[]{:S(2)}) %collective-permute-start) | collective-permute-done | bytes 524320 | tf_op jit(solution)/shard_map/ppermute | solution.py:13
  108.3 3.2 %collective-permute-done.1 = bf16[2,1024,128]{2,1,0:T(8,128)(2,1)S(1)} collective-permute-done((bf16[2,1024,128]{2,1,0:T(8,128)(2,1)}, bf16[2,1024,128]{2,1,0:T(8,128)(2,1)S(1)}, u32[]{:S(2)}, u32[]{:S(2)}) %collective-permute-start.1) | collective-permute-done | bytes 524320 | tf_op jit(solution)/shard_map/ppermute | solution.py:13
  111.6 0.1 bitcast_dynamic-update-slice_fusion.2
  111.7 2.2 %collective-permute-done.2 = bf16[2,1024,128]{2,1,0:T(8,128)(2,1)S(1)} collective-permute-done((bf16[2,1024,128]{2,1,0:T(8,128)(2,1)}, bf16[2,1024,128]{2,1,0:T(8,128)(2,1)S(1)}, u32[]{:S(2)}, u32[]{:S(2)}) %collective-permute-start.2) | collective-permute-done | bytes 524320 | tf_op jit(solution)/shard_map/ppermute | solution.py:13
  114.0 0.1 bitcast_dynamic-update-slice_fusion.1
  114.0 6.9 %collective-permute-done.3 = bf16[2,1024,128]{2,1,0:T(8,128)(2,1)S(1)} collective-permute-done((bf16[2,1024,128]{2,1,0:T(8,128)(2,1)}, bf16[2,1024,128]{2,1,0:T(8,128)(2,1)S(1)}, u32[]{:S(2)}, u32[]{:S(2)}) %collective-permute-start.3) | collective-permute-done | bytes 524320 | tf_op jit(solution)/shard_map/ppermute | solution.py:13
  121.0 0.1 bitcast_dynamic-update-slice_fusion
  121.1 0.2 fusion.16
  121.3 0.5 dynamic-slice-done
  121.7 49.3 %while.12 = (s32[]{:T(128)}, bf16[4,512,128]{2,1,0:T(8,128)(2,1)}, s32[]{:T(128)}, pred[]{:T(512)}, pred[]{:T(512)}, /*index=5*/s32[4]{0:T(128)S(1)}, s32[]{:T(1...) while((s32[]{:T(128)}, bf16[4,512,128]{2,1,0:T(8,128)(2,1)}, ...), condition=%wide.region_3.4_spmd, body=%wide.region_0.3_spmd.sunk | while | flops 1378968576 | bytes 34414076 | solution.py:109
  121.7 0.6 dynamic_slice.50
  124.9 0.1 dynamic-slice_not_fusion.2
  125.0 4.2 %fusion.26 = (f32[512]{0:T(512)S(1)}, f32[512,5120]{1,0:T(8,128)S(1)}) fusion(bf16[5120,128]{1,0:T(8,128)(2,1)S(1)} %get-tuple-element.315, bf16[1024,256]{1,0:T(8,128)(2,1)S(1)} %get-tuple-element.314, s32[]{:T(128)S(6)} %select_n.118, s32[]{:T(128)S(6)} %select_n.120, pred[512]{0:T(512)(128)(4,1)S(1)} %dynamic-slice_not_fusion.2, ...), kind=kOutput, calls=%fused_computation.50.clone.1 | convolution fusion | flops 694681088 | bytes 11962890 | tf_op jit(solution)/shard_map/while/body/eval_jaxpr/dot_general | solution.py:53
  129.2 1.6 fusion.27
  130.8 3.3 %fusion.28 = bf16[4,512,128]{2,1,0:T(8,128)(2,1)} fusion(bf16[4,512,128]{2,1,0:T(8,128)(2,1)} %get-tuple-element.286, s32[]{:T(128)} %get-tuple-element.285, bf16[5120,128]{1,0:T(8,128)(2,1)S(1)} %get-tuple-element.316, f32[512,5120]{1,0:T(8,128)S(1)} %get-tuple-element.263, f32[512]{0:T(512)S(1)} %fusion.27, f32[512]{0:T(512)S(1)} %get-tuple-element.264), kind=kOutput, calls=%fused_computation.12.clone.1 | convolution fusion | flops 679018496 | bytes 11932160 | tf_op jit(solution)/shard_map/while/body/eval_jaxpr/dot_general | solution.py:61
  134.1 0.6 dynamic_slice.50
  137.2 0.1 dynamic-slice_not_fusion.2
  137.3 4.2 %fusion.26 = (f32[512]{0:T(512)S(1)}, f32[512,5120]{1,0:T(8,128)S(1)}) fusion(bf16[5120,128]{1,0:T(8,128)(2,1)S(1)} %get-tuple-element.315, bf16[1024,256]{1,0:T(8,128)(2,1)S(1)} %get-tuple-element.314, s32[]{:T(128)S(6)} %select_n.118, s32[]{:T(128)S(6)} %select_n.120, pred[512]{0:T(512)(128)(4,1)S(1)} %dynamic-slice_not_fusion.2, ...), kind=kOutput, calls=%fused_computation.50.clone.1 | convolution fusion | flops 694681088 | bytes 11962890 | tf_op jit(solution)/shard_map/while/body/eval_jaxpr/dot_general | solution.py:53
  141.5 1.6 fusion.27
  143.1 3.3 %fusion.28 = bf16[4,512,128]{2,1,0:T(8,128)(2,1)} fusion(bf16[4,512,128]{2,1,0:T(8,128)(2,1)} %get-tuple-element.286, s32[]{:T(128)} %get-tuple-element.285, bf16[5120,128]{1,0:T(8,128)(2,1)S(1)} %get-tuple-element.316, f32[512,5120]{1,0:T(8,128)S(1)} %get-tuple-element.263, f32[512]{0:T(512)S(1)} %fusion.27, f32[512]{0:T(512)S(1)} %get-tuple-element.264), kind=kOutput, calls=%fused_computation.12.clone.1 | convolution fusion | flops 679018496 | bytes 11932160 | tf_op jit(solution)/shard_map/while/body/eval_jaxpr/dot_general | solution.py:61
  146.4 0.6 dynamic_slice.50
  149.6 0.1 dynamic-slice_not_fusion.2
  149.7 4.2 %fusion.26 = (f32[512]{0:T(512)S(1)}, f32[512,5120]{1,0:T(8,128)S(1)}) fusion(bf16[5120,128]{1,0:T(8,128)(2,1)S(1)} %get-tuple-element.315, bf16[1024,256]{1,0:T(8,128)(2,1)S(1)} %get-tuple-element.314, s32[]{:T(128)S(6)} %select_n.118, s32[]{:T(128)S(6)} %select_n.120, pred[512]{0:T(512)(128)(4,1)S(1)} %dynamic-slice_not_fusion.2, ...), kind=kOutput, calls=%fused_computation.50.clone.1 | convolution fusion | flops 694681088 | bytes 11962890 | tf_op jit(solution)/shard_map/while/body/eval_jaxpr/dot_general | solution.py:53
  153.9 1.6 fusion.27
  155.4 3.3 %fusion.28 = bf16[4,512,128]{2,1,0:T(8,128)(2,1)} fusion(bf16[4,512,128]{2,1,0:T(8,128)(2,1)} %get-tuple-element.286, s32[]{:T(128)} %get-tuple-element.285, bf16[5120,128]{1,0:T(8,128)(2,1)S(1)} %get-tuple-element.316, f32[512,5120]{1,0:T(8,128)S(1)} %get-tuple-element.263, f32[512]{0:T(512)S(1)} %fusion.27, f32[512]{0:T(512)S(1)} %get-tuple-element.264), kind=kOutput, calls=%fused_computation.12.clone.1 | convolution fusion | flops 679018496 | bytes 11932160 | tf_op jit(solution)/shard_map/while/body/eval_jaxpr/dot_general | solution.py:61
  158.7 0.6 dynamic_slice.50
  161.9 0.1 dynamic-slice_not_fusion.2
  162.0 4.2 %fusion.26 = (f32[512]{0:T(512)S(1)}, f32[512,5120]{1,0:T(8,128)S(1)}) fusion(bf16[5120,128]{1,0:T(8,128)(2,1)S(1)} %get-tuple-element.315, bf16[1024,256]{1,0:T(8,128)(2,1)S(1)} %get-tuple-element.314, s32[]{:T(128)S(6)} %select_n.118, s32[]{:T(128)S(6)} %select_n.120, pred[512]{0:T(512)(128)(4,1)S(1)} %dynamic-slice_not_fusion.2, ...), kind=kOutput, calls=%fused_computation.50.clone.1 | convolution fusion | flops 694681088 | bytes 11962890 | tf_op jit(solution)/shard_map/while/body/eval_jaxpr/dot_general | solution.py:53
  166.2 1.6 fusion.27
  167.8 3.3 %fusion.28 = bf16[4,512,128]{2,1,0:T(8,128)(2,1)} fusion(bf16[4,512,128]{2,1,0:T(8,128)(2,1)} %get-tuple-element.286, s32[]{:T(128)} %get-tuple-element.285, bf16[5120,128]{1,0:T(8,128)(2,1)S(1)} %get-tuple-element.316, f32[512,5120]{1,0:T(8,128)S(1)} %get-tuple-element.263, f32[512]{0:T(512)S(1)} %fusion.27, f32[512]{0:T(512)S(1)} %get-tuple-element.264), kind=kOutput, calls=%fused_computation.12.clone.1 | convolution fusion | flops 679018496 | bytes 11932160 | tf_op jit(solution)/shard_map/while/body/eval_jaxpr/dot_general | solution.py:61
  171.0 1.6 copy.24
  172.6 0.3 all_to_all.29
  173.0 19.9 %all_to_all.35 = bf16[8,128,256]{2,1,0:T(8,128)(2,1)S(1)} all-to-all(bf16[8,128,256]{2,1,0:T(8,128)(2,1)S(1)} %all_to_all.29), channel_id=1, replica_groups=mesh['blk'=64,'uly'=8] {'uly'}, dimensions={0} | all-to-all | bytes 1048576 | tf_op jit(solution)/shard_map/all_to_all | solution.py:112
  192.9 0.3 copy.21
  193.2 1.0 copy.22
  (34 shorter events, 0.4 us)
Async XLA Ops:
  6.5 6.1 %copy-start.1 = (bf16[128,2048]{1,0:T(8,128)(2,1)S(1)}, bf16[128,2048]{1,0:T(8,128)(2,1)}, u32[]{:S(2)}) copy-start(bf16[128,2048]{1,0:T(8,128)(2,1)} %param.9) | copy-start | bytes 1572868
  6.5 80.7 %all-gather.2.cloned.1.call-start = ((), (), s32[]{:S(2)}) async-start(), calls=%async_computation.2 | async-start | bytes 1179648 | tf_op jit(solution)/shard_map/all_gather | solution.py:77
  12.9 81.8 %copy-start.3 = (s32[65536]{0:T(1024)S(1)}, s32[65536]{0:T(1024)}, u32[]{:S(2)}) copy-start(s32[65536]{0:T(1024)} %param.14) | copy-start | bytes 786436
  12.9 81.9 %copy-start.4 = (s32[64]{0:T(128)S(1)}, s32[64]{0:T(128)}, u32[]{:S(2)}) copy-start(s32[64]{0:T(128)} %param.15) | copy-start | bytes 772
  16.4 80.3 %all-to-all-start = ((bf16[128,8,256]{0,2,1:T(8,128)(2,1)}), bf16[128,8,256]{0,2,1:T(8,128)(2,1)S(1)}, u32[]{:S(2)}, u32[]{:S(2)}) async-start(bf16[128,8,256]{0,2,1:T(8,128)(2,1)} %bitcast.5), calls=%async_computation | async-start | bytes 1048576 | tf_op jit(solution)/shard_map/all_to_all | solution.py:72
  87.2 24.4 %copy-start = (bf16[2,1024,256]{2,1,0:T(8,128)(2,1)S(1)}, bf16[2,1024,256]{2,1,0:T(8,128)(2,1)}, u32[]{:S(2)}) copy-start(bf16[2,1024,256]{2,1,0:T(8,128)(2,1)} %all-gather.2.cloned.1.call-done) | copy-start | bytes 3145732
  89.2 19.1 %collective-permute-start = (bf16[2,1024,128]{2,1,0:T(8,128)(2,1)}, bf16[2,1024,128]{2,1,0:T(8,128)(2,1)S(1)}, u32[]{:S(2)}, u32[]{:S(2)}) collective-permute-start(bf16[2,1024,128]{2,1,0:T(8,128)(2,1)} %constant_dynamic-slice_fusion), channel_id=1, source_target_pairs={{0,16},{8,24},{16,32},{24,40},{32,48},{40,56},{48,64},{56,72},{64,... | collective-permute-start | bytes 1572872 | tf_op jit(solution)/shard_map/ppermute | solution.py:13
  92.8 18.8 %collective-permute-start.1 = (bf16[2,1024,128]{2,1,0:T(8,128)(2,1)}, bf16[2,1024,128]{2,1,0:T(8,128)(2,1)S(1)}, u32[]{:S(2)}, u32[]{:S(2)}) collective-permute-start(bf16[2,1024,128]{2,1,0:T(8,128)(2,1)} %constant_dynamic-slice_fusion), channel_id=1, source_target_pairs={{0,8},{8,16},{16,24},{24,32},{32,40},{40,48},{48,56},{56,64},{64,7... | collective-permute-start | bytes 1572872 | tf_op jit(solution)/shard_map/ppermute | solution.py:13
  94.8 19.2 %copy-start.2 = (pred[65536]{0:T(1024)(128)(4,1)}, pred[65536]{0:T(1024)(128)(4,1)S(1)}, u32[]{:S(2)}) copy-start(pred[65536]{0:T(1024)(128)(4,1)S(1)} %fusion.10) | copy-start | bytes 196612
  97.0 17.0 %collective-permute-start.2 = (bf16[2,1024,128]{2,1,0:T(8,128)(2,1)}, bf16[2,1024,128]{2,1,0:T(8,128)(2,1)S(1)}, u32[]{:S(2)}, u32[]{:S(2)}) collective-permute-start(bf16[2,1024,128]{2,1,0:T(8,128)(2,1)} %constant_dynamic-slice_fusion), channel_id=1, source_target_pairs={{8,0},{16,8},{24,16},{32,24},{40,32},{48,40},{56,48},{64,56},{72,6... | collective-permute-start | bytes 1572872 | tf_op jit(solution)/shard_map/ppermute | solution.py:13
  102.7 18.2 %collective-permute-start.3 = (bf16[2,1024,128]{2,1,0:T(8,128)(2,1)}, bf16[2,1024,128]{2,1,0:T(8,128)(2,1)S(1)}, u32[]{:S(2)}, u32[]{:S(2)}) collective-permute-start(bf16[2,1024,128]{2,1,0:T(8,128)(2,1)} %constant_dynamic-slice_fusion), channel_id=1, source_target_pairs={{16,0},{24,8},{32,16},{40,24},{48,32},{56,40},{64,48},{72,56},{80,... | collective-permute-start | bytes 1572872 | tf_op jit(solution)/shard_map/ppermute | solution.py:13
  121.0 0.7 dynamic-slice-start
Sparse Core Ops, SparseCore 0:
  12.8 74.4 all-gather.1
where the time goes:
time: 202 us; the launch traced here: 201 us
  waiting for transfers between devices  77.8 us (39%)
  matrix products  29.9 us (15%)
  starting transfers between devices  22.2 us (11%)
  blocking collectives  19.9 us (10%)
  between operations  14.9 us (7%)
  local copies, waits for them, and re-layouts  13.1 us (6%)
  other arithmetic  13.1 us (6%)
  loops' own time  10.2 us (5%)
    all_gather x1, waiting for transfers between devices, shards(): whole = lax.all_gather(paired, 'uly', axis=1, tiled=True)  62.1 us
    all_to_all x1, blocking collectives, shards(): lax.all_to_all(attended, 'uly', split_axis=0, concat_axis=1, tiled=True)  19.9 us
    dot_general x4, matrix products, softmax_rows(): lax.dot_general(query_block, keys, (((1,), (1,)), ((), ())), preferred_el...  16.7 us
    ppermute x4, waiting for transfers between devices, from_behind(): return lax.ppermute(block, axis, route)  15.6 us
    ppermute x4, starting transfers between devices, from_behind(): return lax.ppermute(block, axis, route)  13.5 us
    dot_general x4, matrix products, softmax_rows(): jnp.dot(weights, values, preferred_element_type=jnp.float32)  13.1 us
    another operation x1, loops' own time, shards(): outs = lax.map(item, jnp.arange(head_count * parts, dtype=jnp.int32))  10.2 us
    all_to_all x1, starting transfers between devices, shards(): lax.all_to_all(q_rot, 'uly', split_axis=1, concat_axis=0, tiled=True)  8.66 us
  transfers between devices with their start and end apart: 6, of which 5 were waited for; matrix products, arithmetic and copies ran while one was open for 3% of the time, Pallas kernels for 0%

commit v1 on v0

v1 whole, which is shorter than its diff:
```python
import functools

import jax
import jax.numpy as jnp
import numpy as np
from jax import lax
from jax.experimental import pallas as pl
from jax.experimental.pallas import tpu as pltpu
from jax.sharding import PartitionSpec as P

HEAD_DIM = 128
HEADS_PER_GROUP = 8
WIDTH = HEADS_PER_GROUP * HEAD_DIM
ROWS = 128
SHARDS = 8
BLOCK = ROWS * SHARDS
BLOCKS = 64
STACK = 4
NEGATIVE = -1e30
SCALE = HEAD_DIM**-0.5 * 1.4426950408889634
VMEM = pltpu.CompilerParams(vmem_limit_bytes=48 * 2**20)


def lane_frequencies():
    one = 10000.0 ** (-np.arange(16, dtype=np.float64) / 16)
    return np.concatenate([one, one, one, one, np.zeros(64)]).astype(np.float32)[None, :]


def rotate(x, cosine, minus, plus):
    return (
        x * cosine
        + pltpu.roll(x, HEAD_DIM - 16, axis=1) * minus
        + pltpu.roll(x, 16, axis=1) * plus
    )


def keys_kernel(place, offset, frequency, keys, values, payload, tables):
    shape = (ROWS, HEAD_DIM)
    lane = lax.broadcasted_iota(jnp.int32, shape, 1)
    by_place = jnp.broadcast_to(place[...].astype(jnp.float32), shape).T
    by_offset = jnp.broadcast_to(offset[...].astype(jnp.float32), shape).T
    angle = jnp.where(lane < 32, by_place, by_offset) * frequency[...]
    cosine, sine = jnp.cos(angle), jnp.sin(angle)
    first = lane % 32 < 16
    minus = jnp.where(first, -sine, 0.0)
    plus = jnp.where(first, 0.0, sine)
    tables[0], tables[1], tables[2] = cosine, minus, plus
    for group in range(2):
        lanes = slice(group * HEAD_DIM, (group + 1) * HEAD_DIM)
        turned = rotate(keys[:, lanes].astype(jnp.float32), cosine, minus, plus).T.astype(jnp.bfloat16)
        for x in (group, group + 2):
            for half in range(2):
                payload[2 * x + half, :ROWS, :] = turned
                payload[2 * x + half, ROWS:, :] = values[:, lanes]


def queries_kernel(queries, tables, own, other):
    group = lax.axis_index("uly") // 2 % 2
    cosine, minus, plus = tables[0], tables[1], tables[2]
    for out, which in ((other, 1 - group), (own, group)):
        for head in range(HEADS_PER_GROUP):
            start = pl.multiple_of(which * WIDTH + head * HEAD_DIM, HEAD_DIM)
            x = queries[:, pl.ds(start, HEAD_DIM)].astype(jnp.float32)
            out[:, head * HEAD_DIM : (head + 1) * HEAD_DIM] = rotate(x, cosine, minus, plus).astype(jnp.bfloat16)


def attend_kernel(sets, roles, fresh, final, *refs):
    refs = list(refs)
    classes, segments = refs.pop(0), refs.pop(0)
    count = len(sets)
    queries = [refs.pop(0) for _ in range(count)]
    blocks = [refs.pop(0) for _ in roles]
    before = [] if fresh else [(refs.pop(0), refs.pop(0)) for _ in range(count)]
    if final:
        outs = [refs.pop(0) for _ in range(count)]
    else:
        after = [(refs.pop(0), refs.pop(0)) for _ in range(count)]
    split, across, down, total, top, bias = refs

    me, uly = lax.axis_index("blk"), lax.axis_index("uly")
    step = 1 - 2 * (me % 2)
    distance_of = {"own": 0, "near": step, "far": 2 * step, "late": -step, "back": -2 * step}
    klass = classes[me]
    base = jnp.clip(me - 2, 0, BLOCKS - 5)

    for s in range(count):
        for head in range(HEADS_PER_GROUP):
            rows = slice(head * ROWS, (head + 1) * ROWS)
            x = queries[s][:, head * HEAD_DIM : (head + 1) * HEAD_DIM].astype(jnp.float32) * SCALE
            high = x.astype(jnp.bfloat16)
            split[s, rows, :HEAD_DIM] = high
            split[s, rows, HEAD_DIM:] = (x - high.astype(jnp.float32)).astype(jnp.bfloat16)
        if fresh:
            total[s] = jnp.zeros_like(total[s])
            top[s] = jnp.full_like(top[s], NEGATIVE)
        else:
            total[s] = before[s][0][...]
            top[s] = before[s][1][...]
    for j, block in enumerate(blocks):
        down[j, :, HEAD_DIM:] = jnp.ones((BLOCK, HEAD_DIM), jnp.bfloat16)
        for c in range(SHARDS):
            cols = slice(c * ROWS, (c + 1) * ROWS)
            across[j, :HEAD_DIM, cols] = block[c, :ROWS, :]
            across[j, HEAD_DIM:, cols] = block[c, :ROWS, :]
            down[j, cols, :HEAD_DIM] = block[c, ROWS:, :]

    tall = STACK * ROWS
    tiles = HEADS_PER_GROUP // STACK

    def one(s, j, masked):
        def scores(tile):
            return jnp.dot(split[s, tile * tall : (tile + 1) * tall, :], across[j], preferred_element_type=jnp.float32)

        ahead = scores(0)
        for tile in range(tiles):
            now, ahead = ahead, scores(tile + 1) if tile + 1 < tiles else None
            rows = slice(tile * tall, (tile + 1) * tall)
            if masked:
                now = now + jnp.concatenate([bias[...]] * STACK, axis=0)
            old = top[s, rows, :]
            new = jnp.maximum(old, jnp.max(now, axis=1, keepdims=True))
            weights = jnp.exp2(now - jnp.concatenate([new] * SHARDS, axis=1)).astype(jnp.bfloat16)
            part = jnp.dot(weights, down[j], preferred_element_type=jnp.float32)
            decay = jnp.exp2(old - new)
            total[s, rows, :] = total[s, rows, :] * jnp.concatenate([decay, decay], axis=1) + part
            top[s, rows, :] = new

    def block_step(j, carry):
        distance = distance_of[roles[-1]]
        for i in reversed(range(len(roles) - 1)):
            distance = jnp.where(j == i, distance_of[roles[i]], distance)
        there = me + distance
        seen = (there >= 0) & (there < BLOCKS) & ((klass != 1) | (distance <= 0))
        plain = (klass == 0) | ((klass == 1) & (distance < 0))

        @pl.when(seen & plain)
        def _():
            for s in range(count):
                one(s, j, False)

        @pl.when(seen & jnp.logical_not(plain))
        def _():
            row = jnp.clip(there - base, 0, 4)
            key_segment = jnp.concatenate([segments[row * SHARDS + c] for c in range(SHARDS)], axis=1)
            key_context = ((key_segment & 1) == 0) & (klass == 2)
            for s in range(count):
                chunk = uly ^ 2 if sets[s] else uly
                own_segment = segments[(me - base) * SHARDS + chunk]
                odd = jnp.broadcast_to((own_segment & 1).astype(jnp.float32), (ROWS, ROWS)).T
                odd = jnp.where(klass == 1, 1.0, odd)
                causal = jnp.concatenate([odd] * SHARDS, axis=1) > 0.5
                key_at = distance * BLOCK + lax.broadcasted_iota(jnp.int32, (ROWS, BLOCK), 1)
                own_at = chunk * ROWS + lax.broadcasted_iota(jnp.int32, (ROWS, BLOCK), 0)
                allowed = key_context | (causal & (key_at <= own_at))
                bias[...] = jnp.where(allowed, 0.0, NEGATIVE)
                one(s, j, True)

        return carry

    lax.fori_loop(0, len(roles), block_step, 0)
    for s in range(count):
        if final:
            wide = outs[s].shape[1] > WIDTH
            for head in range(HEADS_PER_GROUP):
                state = total[s, head * ROWS : (head + 1) * ROWS, :]
                value = (state[:, :HEAD_DIM] / state[:, HEAD_DIM:]).astype(jnp.bfloat16)
                start = head * HEAD_DIM
                if wide:
                    start = pl.multiple_of(uly // 2 % 2 * WIDTH + start, HEAD_DIM)
                outs[s][:, pl.ds(start, HEAD_DIM)] = value
        else:
            after[s][0][...] = total[s]
            after[s][1][...] = top[s]


def attend(name, classes, segments, sets, queries, blocks, state=None, out=None):
    roles = tuple(blocks)
    count, number = len(sets), len(roles)
    whole = pl.BlockSpec(memory_space=pltpu.VMEM)
    shapes = [
        jax.ShapeDtypeStruct((WIDTH, 2 * HEAD_DIM), jnp.float32),
        jax.ShapeDtypeStruct((WIDTH, HEAD_DIM), jnp.float32),
    ]
    given = [] if state is None else [x for pair in state for x in pair]
    out_shape = shapes * count if out is None else [jax.ShapeDtypeStruct((ROWS, w), jnp.bfloat16) for w in out]
    pairs = count * number * HEADS_PER_GROUP * ROWS * BLOCK
    results = pl.pallas_call(
        functools.partial(attend_kernel, sets, roles, state is None, out is not None),
        out_shape=out_shape,
        in_specs=[pl.BlockSpec(memory_space=pltpu.SMEM)] + [whole] * (1 + count + number + len(given)),
        out_specs=[whole] * len(out_shape),
        scratch_shapes=[
            pltpu.VMEM((count, WIDTH, 2 * HEAD_DIM), jnp.bfloat16),
            pltpu.VMEM((number, 2 * HEAD_DIM, BLOCK), jnp.bfloat16),
            pltpu.VMEM((number, BLOCK, 2 * HEAD_DIM), jnp.bfloat16),
            pltpu.VMEM((count, WIDTH, 2 * HEAD_DIM), jnp.float32),
            pltpu.VMEM((count, WIDTH, HEAD_DIM), jnp.float32),
            pltpu.VMEM((ROWS, BLOCK), jnp.float32),
        ],
        compiler_params=VMEM,
        cost_estimate=pl.CostEstimate(flops=8 * pairs * HEAD_DIM, bytes_accessed=2**20, transcendentals=pairs),
        name=name,
    )(classes, segments, *queries, *blocks.values(), *given)
    if out is not None:
        return results
    return [tuple(results[2 * s : 2 * s + 2]) for s in range(count)]


def shards(queries, key_rows, value_rows, span_place, span_offset, segment_number, block_class):
    me, uly = lax.axis_index("blk"), lax.axis_index("uly")
    payload, tables = pl.pallas_call(
        keys_kernel,
        out_shape=[
            jax.ShapeDtypeStruct((SHARDS, 2 * ROWS, HEAD_DIM), jnp.bfloat16),
            jax.ShapeDtypeStruct((3, ROWS, HEAD_DIM), jnp.float32),
        ],
        compiler_params=VMEM,
        name="rotate_keys",
    )(span_place[None, :], span_offset[None, :], lane_frequencies(), key_rows, value_rows)
    own = lax.all_to_all(payload, "uly", split_axis=0, concat_axis=0, tiled=True)

    q_own, q_other = pl.pallas_call(
        queries_kernel,
        out_shape=[jax.ShapeDtypeStruct((ROWS, WIDTH), jnp.bfloat16)] * 2,
        compiler_params=VMEM,
        name="rotate_queries",
    )(queries, tables)
    partner = [(i, i ^ 2) for i in range(SHARDS)]
    q_partner = lax.ppermute(q_other, "uly", partner)
    first = jnp.clip(me - 2, 0, BLOCKS - 5) * BLOCK
    segments = lax.dynamic_slice(segment_number, (first,), (5 * BLOCK,)).reshape(5 * SHARDS, 1, ROWS)

    within = range(BLOCKS)
    ahead = [(i + 2 - 4 * (i % 2), i) for i in within if i + 2 - 4 * (i % 2) in within]
    behind = [(i - 2 + 4 * (i % 2), i) for i in within if i - 2 + 4 * (i % 2) in within]
    cores = [(i, i ^ 1) for i in within]
    far = lax.ppermute(own, "blk", ahead)
    back = lax.ppermute(own, "blk", behind)
    near, late = lax.ppermute(own, "blk", cores), lax.ppermute(far, "blk", cores)

    run = functools.partial(attend, classes=block_class, segments=segments)
    state = run("attend_own", sets=(True, False), queries=(q_partner, q_own), blocks={"own": own, "near": near})
    (to_send,) = run(
        "attend_partner",
        sets=(True,),
        queries=(q_partner,),
        blocks={"far": far, "late": late, "back": back},
        state=state[:1],
        out=(WIDTH,),
    )
    (mine,) = run(
        "attend_rest",
        sets=(False,),
        queries=(q_own,),
        blocks={"far": far, "late": late, "back": back},
        state=state[1:],
        out=(2 * WIDTH,),
    )
    others = lax.ppermute(to_send, "uly", partner)
    group = uly // 2 % 2
    return lax.dynamic_update_slice(mine, others, (0, (1 - group) * WIDTH))


def solution(mesh):
    rows = P(("blk", "uly"), None)
    line = P(("blk", "uly"))
    return jax.shard_map(
        shards,
        mesh=mesh,
        in_specs=(rows, rows, rows, line, line, P(), P()),
        out_specs=rows,
        check_vma=False,
    )
```

time: 202 us -> 84.2 us (0.42)
  the two profiles are of different devices: /device:TPU:8 before, /device:TPU:19 now
where the time goes in v1:
time: 84.2 us; the launch traced here: 83.8 us
  starting transfers between devices  27.3 us (32%)
  Pallas kernels  26.2 us (31%)
  blocking collectives  23.9 us (28%)
  local copies, waits for them, and re-layouts  4.48 us (5%)
  waiting for transfers between devices  1.75 us (2%)
    pallas_call x3, Pallas kernels, attend(): pl.pallas_call(functools.partial(attend_kernel, sets, roles, state is Non...  25.2 us
    all_to_all x1, blocking collectives, shards(): lax.all_to_all(payload, 'uly', split_axis=0, concat_axis=0, tiled=True)  23.9 us
    ppermute x1, starting transfers between devices, shards(): lax.ppermute(own, 'blk', cores)  12.1 us
    ppermute x1, starting transfers between devices, shards(): far = lax.ppermute(own, 'blk', ahead)  3.99 us
    ppermute x1, starting transfers between devices, shards(): q_partner = lax.ppermute(q_other, 'uly', partner)  3.78 us
    ppermute x1, starting transfers between devices, shards(): others = lax.ppermute(to_send, 'uly', partner)  3.34 us
    unnamed x14, local copies, waits for them, and re-layouts  3.02 us
    ppermute x1, starting transfers between devices, shards(): back = lax.ppermute(own, 'blk', behind)  2.18 us
  transfers between devices with their start and end apart: 6, of which 1 were waited for; matrix products, arithmetic and copies ran while one was open for 1% of the time, Pallas kernels for 21%

profile of v1, /device:TPU:19, one launch (start us, length us, event | category | flops | bytes accessed | tf_op | source)
XLA Modules:
  0.0 83.8 jit_solution(337328678623872741)
XLA Ops:
  0.0 0.0 copy-start.3
  0.0 0.0 copy-start.4
  0.0 0.0 copy-start.5
  0.0 0.6 copy-done.3
  0.7 0.0 copy-done.4
  0.7 0.0 copy-done.5
  0.7 0.0 copy-start.1
  0.7 0.8 copy-done.1
  1.5 0.0 copy-start.2
  1.5 0.8 copy-done.2
  2.4 0.4 rotate_keys.1
  2.8 0.0 copy-start
  2.8 23.9 %all_to_all.5.refs_4_ = bf16[8,256,128]{2,1,0:T(8,128)(2,1)S(1)} all-to-all(bf16[8,256,128]{2,1,0:T(8,128)(2,1)S(1)} %get-tuple-element.15), channel_id=1, replica_groups=mesh['blk'=64,'uly'=8] {'uly'}, dimensions={0} | all-to-all | bytes 1048576 | tf_op jit(solution)/shard_map/all_to_all | solution.py:220
  26.7 4.0 %collective-permute-start = (bf16[8,256,128]{2,1,0:T(8,128)(2,1)S(1)}, bf16[8,256,128]{2,1,0:T(8,128)(2,1)S(1)}, u32[]{:S(2)}, u32[]{:S(2)}) collective-permute-start(bf16[8,256,128]{2,1,0:T(8,128)(2,1)S(1)} %all_to_all.5.refs_4_), channel_id=1, source_target_pairs={{16,0},{32,16},{8,24},{48,32},{24,40},{64,48},{40,56},{80,64},{56,... | collective-permute-start | bytes 1572872 | tf_op jit(solution)/shard_map/ppermute | solution.py:237
  30.7 12.1 %collective-permute-start.4 = (bf16[8,256,128]{2,1,0:T(8,128)(2,1)S(1)}, bf16[8,256,128]{2,1,0:T(8,128)(2,1)S(1)}, u32[]{:S(2)}, u32[]{:S(2)}) collective-permute-start(bf16[8,256,128]{2,1,0:T(8,128)(2,1)S(1)} %all_to_all.5.refs_4_), channel_id=1, source_target_pairs={{0,8},{8,0},{16,24},{24,16},{32,40},{40,32},{48,56},{56,48},{64,72... | collective-permute-start | bytes 1572872 | tf_op jit(solution)/shard_map/ppermute | solution.py:239
  42.8 0.0 copy-done
  42.8 0.5 rotate_queries.1
  43.3 3.8 %collective-permute-start.3 = (bf16[128,1024]{1,0:T(8,128)(2,1)S(1)}, bf16[128,1024]{1,0:T(8,128)(2,1)S(1)}, u32[]{:S(2)}, u32[]{:S(2)}) collective-permute-start(bf16[128,1024]{1,0:T(8,128)(2,1)S(1)} %get-tuple-element.16), channel_id=1, source_target_pairs={{0,2},{1,3},{2,0},{3,1},{4,6},{5,7},{6,4},{7,5},{8,10},{9,11},{10,... | collective-permute-start | bytes 786440 | tf_op jit(solution)/shard_map/ppermute | solution.py:229
  47.1 2.2 %collective-permute-start.2 = (bf16[8,256,128]{2,1,0:T(8,128)(2,1)S(1)}, bf16[8,256,128]{2,1,0:T(8,128)(2,1)S(1)}, u32[]{:S(2)}, u32[]{:S(2)}) collective-permute-start(bf16[8,256,128]{2,1,0:T(8,128)(2,1)S(1)} %all_to_all.5.refs_4_), channel_id=1, source_target_pairs={{24,8},{0,16},{40,24},{16,32},{56,40},{32,48},{72,56},{48,64},{88,... | collective-permute-start | bytes 1572872 | tf_op jit(solution)/shard_map/ppermute | solution.py:238
  49.3 0.0 collective-permute-done.refs_3_
  49.3 1.9 %collective-permute-start.1 = (bf16[8,256,128]{2,1,0:T(8,128)(2,1)S(1)}, bf16[8,256,128]{2,1,0:T(8,128)(2,1)S(1)}, u32[]{:S(2)}, u32[]{:S(2)}) collective-permute-start(bf16[8,256,128]{2,1,0:T(8,128)(2,1)S(1)} %collective-permute-done.refs_3_), channel_id=1, source_target_pairs={{0,8},{8,0},{16,24},{24,16},{32,40},{40,32},{48,56},{56,48},{64,72... | collective-permute-start | bytes 1572872 | tf_op jit(solution)/shard_map/ppermute | solution.py:239
  51.3 0.7 dynamic_slice.3
  52.0 1.7 %collective-permute-done.3.refs_2_ = bf16[128,1024]{1,0:T(8,128)(2,1)S(1)} collective-permute-done((bf16[128,1024]{1,0:T(8,128)(2,1)S(1)}, bf16[128,1024]{1,0:T(8,128)(2,1)S(1)}, u32[]{:S(2)}, u32[]{:S(2)}) %collective-permute-start.3) | collective-permute-done | bytes 262176 | tf_op jit(solution)/shard_map/ppermute | solution.py:229
  53.8 0.0 collective-permute-done.4.refs_5_
  53.8 0.0 copy-start.6
  53.8 0.7 copy-done.6
  54.4 8.8 %attend_own.1 = (f32[1024,256]{1,0:T(8,128)S(1)}, f32[1024,128]{1,0:T(8,128)S(1)}, f32[1024,256]{1,0:T(8,128)S(1)}, f32[1024,128]{1,0:T(8,128)S(1)}) custom-call(s32[64]{0:T(128)S(1)} %copy-done.6, s32[40,1,128]{2,1,0:T(1,128)S(1)} %bitcast.3, bf16[128,1024]{1,0:T(8,128)(2,1)S(1)} %collective-permute-done.3.refs_2_, ...), custom_call_target="tpu_custom_call" | custom-call | flops 4294967296 | bytes 1048576 | tf_op jit(solution)/shard_map/attend_own/pallas_call | solution.py:187
  63.2 0.0 collective-permute-done.2.refs_5_
  63.2 0.0 collective-permute-done.1.refs_4_
  63.2 7.8 %attend_partner.1 = bf16[128,1024]{1,0:T(8,128)(2,1)S(1)} custom-call(s32[64]{0:T(128)S(1)} %copy-done.6, s32[40,1,128]{2,1,0:T(1,128)S(1)} %bitcast.4, bf16[128,1024]{1,0:T(8,128)(2,1)S(1)} %collective-permute-done.3.refs_2_, bf16[8,256,128]{2,1,0:T(8,128)(2,1)S(1)} %collective-permute-done.refs_3_, ...), custom_call_target="tpu_custom_call" | custom-call | flops 3221225472 | bytes 1048576 | tf_op jit(solution)/shard_map/attend_partner/pallas_call | solution.py:187
  71.1 3.3 %collective-permute-start.5 = (bf16[128,1024]{1,0:T(8,128)(2,1)S(1)}, bf16[128,1024]{1,0:T(8,128)(2,1)S(1)}, u32[]{:S(2)}, u32[]{:S(2)}) collective-permute-start(bf16[128,1024]{1,0:T(8,128)(2,1)S(1)} %attend_partner.1), channel_id=1, source_target_pairs={{0,2},{1,3},{2,0},{3,1},{4,6},{5,7},{6,4},{7,5},{8,10},{9,11},{10,... | collective-permute-start | bytes 786440 | tf_op jit(solution)/shard_map/ppermute | solution.py:259
  74.4 8.6 %attend_rest.1 = bf16[128,2048]{1,0:T(8,128)(2,1)} custom-call(s32[64]{0:T(128)S(1)} %copy-done.6, s32[40,1,128]{2,1,0:T(1,128)S(1)} %bitcast.5, bf16[128,1024]{1,0:T(8,128)(2,1)S(1)} %get-tuple-element.14.refs_3_.refs_2_, bf16[8,256,128]{2,1,0:T(8,128)(2,1)S(1)} %collective-permute-done.refs_3_, bf16[8,256,128]{2,1,0:T(8,128)(2,1)S(1)} %collective-permute-done.1.refs_4_, ...), custom_call_target="tpu_custom_call" | custom-call | flops 3221225472 | bytes 1048576 | tf_op jit(solution)/shard_map/attend_rest/pallas_call | solution.py:187
  83.0 0.0 collective-permute-done.5
  83.0 0.7 constant_dynamic-update-slice_fusion
Async XLA Ops:
  0.0 0.7 copy-start.3
  0.0 0.7 copy-start.4
  0.0 0.7 copy-start.5
  0.7 0.8 %copy-start.1 = (bf16[128,256]{1,0:T(8,128)(2,1)S(1)}, bf16[128,256]{1,0:T(8,128)(2,1)}, u32[]{:S(2)}) copy-start(bf16[128,256]{1,0:T(8,128)(2,1)} %keys.1) | copy-start | bytes 196612
  1.5 0.8 %copy-start.2 = (bf16[128,256]{1,0:T(8,128)(2,1)S(1)}, bf16[128,256]{1,0:T(8,128)(2,1)}, u32[]{:S(2)}) copy-start(bf16[128,256]{1,0:T(8,128)(2,1)} %values.1) | copy-start | bytes 196612
  2.8 40.0 %copy-start = (bf16[128,2048]{1,0:T(8,128)(2,1)S(1)}, bf16[128,2048]{1,0:T(8,128)(2,1)}, u32[]{:S(2)}) copy-start(bf16[128,2048]{1,0:T(8,128)(2,1)} %queries.1) | copy-start | bytes 1572868
  26.7 22.6 %collective-permute-start = (bf16[8,256,128]{2,1,0:T(8,128)(2,1)S(1)}, bf16[8,256,128]{2,1,0:T(8,128)(2,1)S(1)}, u32[]{:S(2)}, u32[]{:S(2)}) collective-permute-start(bf16[8,256,128]{2,1,0:T(8,128)(2,1)S(1)} %all_to_all.5.refs_4_), channel_id=1, source_target_pairs={{16,0},{32,16},{8,24},{48,32},{24,40},{64,48},{40,56},{80,64},{56,... | collective-permute-start | bytes 1572872 | tf_op jit(solution)/shard_map/ppermute | solution.py:237
  30.7 23.1 %collective-permute-start.4 = (bf16[8,256,128]{2,1,0:T(8,128)(2,1)S(1)}, bf16[8,256,128]{2,1,0:T(8,128)(2,1)S(1)}, u32[]{:S(2)}, u32[]{:S(2)}) collective-permute-start(bf16[8,256,128]{2,1,0:T(8,128)(2,1)S(1)} %all_to_all.5.refs_4_), channel_id=1, source_target_pairs={{0,8},{8,0},{16,24},{24,16},{32,40},{40,32},{48,56},{56,48},{64,72... | collective-permute-start | bytes 1572872 | tf_op jit(solution)/shard_map/ppermute | solution.py:239
  43.3 10.4 %collective-permute-start.3 = (bf16[128,1024]{1,0:T(8,128)(2,1)S(1)}, bf16[128,1024]{1,0:T(8,128)(2,1)S(1)}, u32[]{:S(2)}, u32[]{:S(2)}) collective-permute-start(bf16[128,1024]{1,0:T(8,128)(2,1)S(1)} %get-tuple-element.16), channel_id=1, source_target_pairs={{0,2},{1,3},{2,0},{3,1},{4,6},{5,7},{6,4},{7,5},{8,10},{9,11},{10,... | collective-permute-start | bytes 786440 | tf_op jit(solution)/shard_map/ppermute | solution.py:229
  47.1 16.1 %collective-permute-start.2 = (bf16[8,256,128]{2,1,0:T(8,128)(2,1)S(1)}, bf16[8,256,128]{2,1,0:T(8,128)(2,1)S(1)}, u32[]{:S(2)}, u32[]{:S(2)}) collective-permute-start(bf16[8,256,128]{2,1,0:T(8,128)(2,1)S(1)} %all_to_all.5.refs_4_), channel_id=1, source_target_pairs={{24,8},{0,16},{40,24},{16,32},{56,40},{32,48},{72,56},{48,64},{88,... | collective-permute-start | bytes 1572872 | tf_op jit(solution)/shard_map/ppermute | solution.py:238
  49.3 13.9 %collective-permute-start.1 = (bf16[8,256,128]{2,1,0:T(8,128)(2,1)S(1)}, bf16[8,256,128]{2,1,0:T(8,128)(2,1)S(1)}, u32[]{:S(2)}, u32[]{:S(2)}) collective-permute-start(bf16[8,256,128]{2,1,0:T(8,128)(2,1)S(1)} %collective-permute-done.refs_3_), channel_id=1, source_target_pairs={{0,8},{8,0},{16,24},{24,16},{32,40},{40,32},{48,56},{56,48},{64,72... | collective-permute-start | bytes 1572872 | tf_op jit(solution)/shard_map/ppermute | solution.py:239
  53.8 0.7 copy-start.6
  71.1 12.0 %collective-permute-start.5 = (bf16[128,1024]{1,0:T(8,128)(2,1)S(1)}, bf16[128,1024]{1,0:T(8,128)(2,1)S(1)}, u32[]{:S(2)}, u32[]{:S(2)}) collective-permute-start(bf16[128,1024]{1,0:T(8,128)(2,1)S(1)} %attend_partner.1), channel_id=1, source_target_pairs={{0,2},{1,3},{2,0},{3,1},{4,6},{5,7},{6,4},{7,5},{8,10},{9,11},{10,... | collective-permute-start | bytes 786440 | tf_op jit(solution)/shard_map/ppermute | solution.py:259

commit v2 on v1

v2 whole, which is shorter than its diff:
```python
import functools

import jax
import jax.numpy as jnp
import numpy as np
from jax import lax
from jax.experimental import pallas as pl
from jax.experimental.pallas import tpu as pltpu
from jax.sharding import PartitionSpec as P

HEAD_DIM = 128
HEADS_PER_GROUP = 8
WIDTH = HEADS_PER_GROUP * HEAD_DIM
ROWS = 128
SHARDS = 8
BLOCK = ROWS * SHARDS
BLOCKS = 64
STACK = 4
NEGATIVE = -1e30
SCALE = HEAD_DIM**-0.5 * 1.4426950408889634
MAXIMUM = HEAD_DIM + 8
VMEM = pltpu.CompilerParams(vmem_limit_bytes=16 * 2**20)
KEYS_VMEM = 60 * 2**20


def lane_frequencies():
    one = 10000.0 ** (-np.arange(16, dtype=np.float64) / 16)
    return np.concatenate([one, one, one, one, np.zeros(64)]).astype(np.float32)[None, :]


def rotate(x, cosine, minus, plus):
    return (
        x * cosine
        + pltpu.roll(x, HEAD_DIM - 16, axis=1) * minus
        + pltpu.roll(x, 16, axis=1) * plus
    )


def keys_kernel(place_in, offset_in, frequency, keys_in, values_in, payload, tables, place, offset, keys, values, sems):
    copies = [
        pltpu.make_async_copy(source, target, sems.at[i])
        for i, (source, target) in enumerate(
            ((place_in, place), (offset_in, offset), (keys_in, keys), (values_in, values))
        )
    ]
    for copy in copies:
        copy.start()
    copies[0].wait()
    copies[1].wait()
    shape = (ROWS, HEAD_DIM)
    lane = lax.broadcasted_iota(jnp.int32, shape, 1)
    by_place = jnp.broadcast_to(place[...].astype(jnp.float32), shape).T
    by_offset = jnp.broadcast_to(offset[...].astype(jnp.float32), shape).T
    angle = jnp.where(lane < 32, by_place, by_offset) * frequency[...]
    cosine, sine = jnp.cos(angle), jnp.sin(angle)
    first = lane % 32 < 16
    minus = jnp.where(first, -sine, 0.0)
    plus = jnp.where(first, 0.0, sine)
    tables[0], tables[1], tables[2] = cosine, minus, plus
    copies[2].wait()
    copies[3].wait()
    for group in range(2):
        lanes = slice(group * HEAD_DIM, (group + 1) * HEAD_DIM)
        turned = rotate(keys[:, lanes].astype(jnp.float32), cosine, minus, plus).astype(jnp.bfloat16)
        across = values[:, lanes].astype(jnp.float32).T.astype(jnp.bfloat16)
        for x in (group, group + 2):
            for half in range(2):
                payload[2 * x + half, :ROWS, :] = turned
                payload[2 * x + half, ROWS:, :] = across


def split_queries(x, odd, tip):
    x = x * SCALE
    high = x.astype(jnp.bfloat16)
    guard = jnp.where(tip == HEAD_DIM - 1, NEGATIVE, jnp.where(odd > 0.5, 0.0, NEGATIVE))
    low = jnp.where(tip < HEAD_DIM - 2, x - high.astype(jnp.float32), guard)
    return high, low.astype(jnp.bfloat16)


def turn_queries(queries, tables, group, head):
    start = pl.multiple_of(group * WIDTH + head * HEAD_DIM, HEAD_DIM)
    x = queries[:, pl.ds(start, HEAD_DIM)].astype(jnp.float32)
    return rotate(x, tables[0], tables[1], tables[2]).astype(jnp.bfloat16).astype(jnp.float32).T


def other_queries_kernel(queries, tables, other):
    group = 1 - lax.axis_index("uly") // 2 % 2
    for head in range(HEADS_PER_GROUP):
        cols = slice(head * ROWS, (head + 1) * ROWS)
        other[:, cols] = turn_queries(queries, tables, group, head).astype(jnp.bfloat16)


def own_queries_kernel(queries, tables, all_segments, own, odds, segments, sem):
    me, uly = lax.axis_index("blk"), lax.axis_index("uly")
    square = (ROWS, ROWS)
    tip = lax.broadcasted_iota(jnp.int32, square, 0)
    base = jnp.clip(me - 2, 0, BLOCKS - 5)
    copy = pltpu.make_async_copy(all_segments.at[pl.ds(base * SHARDS, 5 * SHARDS)], segments, sem)
    copy.start()
    copy.wait()
    odd = jnp.broadcast_to((segments[(me - base) * SHARDS + uly] & 1).astype(jnp.float32), square)
    for head in range(HEADS_PER_GROUP):
        cols = slice(head * ROWS, (head + 1) * ROWS)
        high, low = split_queries(turn_queries(queries, tables, uly // 2 % 2, head), odd, tip)
        own[:HEAD_DIM, cols] = high
        own[HEAD_DIM:, cols] = low

    def chunk_step(c, carry):
        start = pl.multiple_of(c * ROWS, ROWS)
        column = jnp.broadcast_to((segments[c] & 1).astype(jnp.float32), square).T
        odds[pl.ds(start, ROWS), :] = column.astype(jnp.bfloat16)
        return carry

    lax.fori_loop(0, 5 * SHARDS, chunk_step, 0, unroll=4)


def attend_kernel(sets, roles, pairs, start, final, *refs):
    refs = list(refs)
    classes, segments, odds = refs.pop(0), refs.pop(0), refs.pop(0)
    count = len(sets)
    laid = [(refs.pop(0), refs.pop(0)) for _ in range(pairs)]
    if start:
        arrived = refs.pop(0)
        splits = [None, refs.pop(0)]
    else:
        splits = [refs.pop(0) for _ in range(count)]
    blocks = [] if pairs else [refs.pop(0) for _ in roles]
    given = [] if start else [refs.pop(0) for _ in range(count)]
    states = [refs.pop(0) for _ in range(count)]
    if start:
        splits[0] = refs.pop(0)
    outs = [refs.pop(0) for _ in range(count)] if final else []
    if not pairs:
        laid = [(refs.pop(0), refs.pop(0))]
    (bias,) = refs
    keys = [pair[0].at[i] for pair in laid for i in range(pair[0].shape[0])]
    values = [pair[1].at[i] for pair in laid for i in range(pair[1].shape[0])]

    me, uly = lax.axis_index("blk"), lax.axis_index("uly")
    step = 1 - 2 * (me % 2)
    distance_of = {"own": 0, "near": step, "far": 2 * step, "late": -step, "back": -2 * step}
    klass = classes[me]
    base = jnp.clip(me - 2, 0, BLOCKS - 5)
    square = (ROWS, ROWS)
    lane = lax.broadcasted_iota(jnp.int32, square, 1)
    tip = lax.broadcasted_iota(jnp.int32, square, 0)
    chunks = [uly ^ 2 if theirs else uly for theirs in sets]

    def odd_tokens(s, shape):
        segment = segments[(me - base) * SHARDS + chunks[s]]
        return jnp.broadcast_to((segment & 1).astype(jnp.float32), shape)

    def hidden(s, first, number):
        shape = (number, ROWS)
        at = pl.multiple_of((me - base) * BLOCK + first, ROWS)
        context = (odds[pl.ds(at, number), :].astype(jnp.float32) < 0.5) & (klass == 2)
        follows = (odd_tokens(s, shape) > 0.5) | (klass != 2)
        key_at = first + lax.broadcasted_iota(jnp.int32, shape, 0)
        token_at = chunks[s] * ROWS + lax.broadcasted_iota(jnp.int32, shape, 1)
        return jnp.where(context | (follows & (key_at <= token_at)), 0.0, NEGATIVE)

    facts = []
    for role in roles:
        distance = distance_of[role]
        there = me + distance
        seen = (there >= 0) & (there < BLOCKS) & ((klass != 1) | (distance <= 0))
        facts.append((distance, there, seen))

    def lay_out(j):
        distance, there, _ = facts[j]
        before = jnp.where((klass == 2) & (distance < 0), 1.0, 0.0)
        after = jnp.where((klass == 2) & (distance > 0), 1.0, 0.0)
        guard = jnp.where(lane == HEAD_DIM - 2, before, jnp.where(lane == HEAD_DIM - 1, after, 0.0))
        place = jnp.clip(there - base, 0, 4) * SHARDS
        for c in range(SHARDS):
            rows = slice(c * ROWS, (c + 1) * ROWS)
            part = blocks[j][c, :ROWS, :]
            keys[j][rows, :HEAD_DIM] = part
            odd = odds[pl.ds(pl.multiple_of((place + c) * ROWS, ROWS), ROWS), :].astype(jnp.float32)
            part = jnp.where(lane < HEAD_DIM - 2, part.astype(jnp.float32), odd * guard)
            keys[j][rows, HEAD_DIM:] = part.astype(jnp.bfloat16)
            values[j][:, rows] = blocks[j][c, ROWS:, :]

    wide = STACK * ROWS
    items = [
        (s, slice(tile * wide, (tile + 1) * wide)) for s in range(count) for tile in range(HEADS_PER_GROUP // STACK)
    ]

    def scores(j, s, cols):
        return jnp.dot(keys[j][...], splits[s][:, cols], preferred_element_type=jnp.float32)

    def take(which, masked):
        steps = [(j, s, cols) for j in which for s, cols in items]
        ahead = scores(*steps[0])
        for i, (j, s, cols) in enumerate(steps):
            now, ahead = ahead, scores(*steps[i + 1]) if i + 1 < len(steps) else None
            if masked:
                now = now + jnp.concatenate([bias[s]] * STACK, axis=1)
            weights = jnp.exp2(now - states[s][MAXIMUM : MAXIMUM + 1, cols])
            part = jnp.dot(values[j][...], weights.astype(jnp.bfloat16), preferred_element_type=jnp.float32)
            states[s][:HEAD_DIM, cols] += part
            states[s][HEAD_DIM : HEAD_DIM + 1, cols] += jnp.sum(weights, axis=0, keepdims=True)

    def take_largest(which, masked):
        def head_step(head, carry):
            cols = pl.ds(pl.multiple_of(head * ROWS, ROWS), ROWS)
            for s in range(count):
                now = scores(which[0], s, cols)
                if masked:
                    now = now + bias[s]
                old = states[s][MAXIMUM : MAXIMUM + 1, cols]
                new = jnp.maximum(old, jnp.max(now, axis=0, keepdims=True))
                decay = jnp.exp2(old - new)
                weights = jnp.exp2(now - new)
                part = jnp.dot(values[which[0]][...], weights.astype(jnp.bfloat16), preferred_element_type=jnp.float32)
                states[s][:HEAD_DIM, cols] = states[s][:HEAD_DIM, cols] * decay + part
                total = states[s][HEAD_DIM : HEAD_DIM + 1, cols] * decay + jnp.sum(weights, axis=0, keepdims=True)
                states[s][HEAD_DIM : HEAD_DIM + 1, cols] = total
                states[s][MAXIMUM : MAXIMUM + 1, cols] = new
            return carry

        lax.fori_loop(0, HEADS_PER_GROUP, head_step, 0)

    def each_block(how):
        for j in range(len(roles)):

            @pl.when(facts[j][2])
            def _(j=j):
                how([j], False)

    def own_block(how):
        @pl.when(klass == 0)
        def _():
            how([0], False)

        @pl.when(klass != 0)
        def _():
            how([0], True)

    if start:
        odd = odd_tokens(0, square)
        for head in range(HEADS_PER_GROUP):
            cols = slice(head * ROWS, (head + 1) * ROWS)
            high, low = split_queries(arrived[:, cols].astype(jnp.float32), odd, tip)
            splits[0][:HEAD_DIM, cols] = high
            splits[0][HEAD_DIM:, cols] = low
        lay_out(0)
        for s in range(count):
            rows = pl.ds(pl.multiple_of(chunks[s] * ROWS, ROWS), ROWS)
            near = jnp.dot(keys[0][rows, :], splits[s][...], preferred_element_type=jnp.float32)
            near = near + jnp.concatenate([hidden(s, chunks[s] * ROWS, ROWS)] * HEADS_PER_GROUP, axis=1)
            states[s][:MAXIMUM, :] = jnp.zeros((MAXIMUM, WIDTH), jnp.float32)
            states[s][MAXIMUM : MAXIMUM + 1, :] = jnp.max(near, axis=0, keepdims=True)

        @pl.when(klass != 0)
        def _():
            for s in range(count):
                bias[s] = hidden(s, 0, BLOCK)

        own_block(take)
    else:
        for j in range(len(blocks)):
            lay_out(j)
        for s in range(count):
            states[s][...] = given[s][...]
        every = facts[0][2]
        for fact in facts[1:]:
            every = every & fact[2]

        @pl.when(every)
        def _():
            take(list(range(len(roles))), False)

        @pl.when(jnp.logical_not(every))
        def _():
            each_block(take)

    largest = states[0][HEAD_DIM : HEAD_DIM + 1, :]
    for s in range(1, count):
        largest = jnp.maximum(largest, states[s][HEAD_DIM : HEAD_DIM + 1, :])

    @pl.when(jnp.logical_not(jnp.max(largest) < 2.0**100))
    def _():
        for s in range(count):
            if start:
                states[s][:MAXIMUM, :] = jnp.zeros((MAXIMUM, WIDTH), jnp.float32)
            else:
                states[s][...] = given[s][...]
        if start:
            own_block(take_largest)
        else:
            each_block(take_largest)

    for s, out in enumerate(outs):
        for head in range(HEADS_PER_GROUP):
            cols = slice(head * ROWS, (head + 1) * ROWS)
            value = states[s][:HEAD_DIM, cols] / states[s][HEAD_DIM : HEAD_DIM + 1, cols]
            out[:, cols] = value.T.astype(jnp.bfloat16)


def combine_kernel(mine, others, out, sems):
    group = lax.axis_index("uly") // 2 % 2
    copies = [
        pltpu.make_async_copy(source, out.at[:, pl.ds(pl.multiple_of(which * WIDTH, WIDTH), WIDTH)], sems.at[i])
        for i, (source, which) in enumerate(((mine, group), (others, 1 - group)))
    ]
    for copy in copies:
        copy.start()
    for copy in copies:
        copy.wait()


def attend(name, classes, segments, odds, sets, splits, blocks=None, laid=(), state=None, final=False):
    roles = tuple(blocks) if blocks else tuple(role for group in laid for role in group[0])
    count, number = len(sets), len(roles)
    start = state is None
    whole = pl.BlockSpec(memory_space=pltpu.VMEM)
    shapes = [jax.ShapeDtypeStruct((MAXIMUM + 8, WIDTH), jnp.float32)] * count
    if start:
        shapes.append(jax.ShapeDtypeStruct((2 * HEAD_DIM, WIDTH), jnp.bfloat16))
    if final:
        shapes.append(jax.ShapeDtypeStruct((ROWS, WIDTH), jnp.bfloat16))
    if blocks:
        shapes.append(jax.ShapeDtypeStruct((number, BLOCK, 2 * HEAD_DIM), jnp.bfloat16))
        shapes.append(jax.ShapeDtypeStruct((number, HEAD_DIM, BLOCK), jnp.bfloat16))
    given = [odds, *(x for group in laid for x in group[1:]), *splits, *(blocks or {}).values(), *(state or ())]
    pairs = count * number * HEADS_PER_GROUP * ROWS * BLOCK
    results = list(
        pl.pallas_call(
            functools.partial(attend_kernel, sets, roles, len(laid), start, final),
            out_shape=shapes,
            in_specs=[pl.BlockSpec(memory_space=pltpu.SMEM)] + [whole] * (1 + len(given)),
            out_specs=[whole] * len(shapes),
            scratch_shapes=[pltpu.VMEM((count, BLOCK if start else 8, ROWS), jnp.float32)],
            compiler_params=VMEM,
            cost_estimate=pl.CostEstimate(flops=8 * pairs * HEAD_DIM, bytes_accessed=2**20, transcendentals=pairs),
            name=name,
        )(classes, segments, *given)
    )
    if blocks:
        laid = (roles, *results[-2:])
    states = results[:count]
    if start:
        splits = [results[count], splits[1]]
    return splits, states, laid, results[count] if final else None


def shards(queries, key_rows, value_rows, span_place, span_offset, segment_number, block_class):
    vmem, hbm = pl.BlockSpec(memory_space=pltpu.VMEM), pl.BlockSpec(memory_space=pl.ANY)
    payload, tables = pl.pallas_call(
        keys_kernel,
        out_shape=[
            jax.ShapeDtypeStruct((SHARDS, 2 * ROWS, HEAD_DIM), jnp.bfloat16),
            jax.ShapeDtypeStruct((3, ROWS, HEAD_DIM), jnp.float32),
        ],
        in_specs=[hbm, hbm, vmem, hbm, hbm],
        out_specs=[vmem, vmem],
        scratch_shapes=[
            pltpu.VMEM((1, ROWS), jnp.int32),
            pltpu.VMEM((1, ROWS), jnp.int32),
            pltpu.VMEM((ROWS, 2 * HEAD_DIM), jnp.bfloat16),
            pltpu.VMEM((ROWS, 2 * HEAD_DIM), jnp.bfloat16),
            pltpu.SemaphoreType.DMA((4,)),
        ],
        compiler_params=pltpu.CompilerParams(vmem_limit_bytes=KEYS_VMEM),
        name="rotate_keys",
    )(span_place[None, :], span_offset[None, :], lane_frequencies(), key_rows, value_rows)
    own = lax.all_to_all(payload, "uly", split_axis=0, concat_axis=0, tiled=True)

    q_other = pl.pallas_call(
        other_queries_kernel,
        out_shape=jax.ShapeDtypeStruct((HEAD_DIM, WIDTH), jnp.bfloat16),
        compiler_params=VMEM,
        name="rotate_other_queries",
    )(queries, tables)
    partner = [(i, i ^ 2) for i in range(SHARDS)]
    q_partner = lax.ppermute(q_other, "uly", partner)
    split_own, odds, segments = pl.pallas_call(
        own_queries_kernel,
        out_shape=[
            jax.ShapeDtypeStruct((2 * HEAD_DIM, WIDTH), jnp.bfloat16),
            jax.ShapeDtypeStruct((5 * BLOCK, ROWS), jnp.bfloat16),
            jax.ShapeDtypeStruct((5 * SHARDS, 1, ROWS), jnp.int32),
        ],
        in_specs=[vmem, vmem, hbm],
        out_specs=[vmem, vmem, vmem],
        scratch_shapes=[pltpu.SemaphoreType.DMA],
        compiler_params=VMEM,
        name="rotate_own_queries",
    )(queries, tables, segment_number.reshape(BLOCKS * SHARDS, 1, ROWS))
    ready = (own, split_own, q_partner, odds, segments)
    own, split_own, q_partner, odds, segments = lax.optimization_barrier(ready)

    within = range(BLOCKS)
    ahead = [(i + 2 - 4 * (i % 2), i) for i in within if i + 2 - 4 * (i % 2) in within]
    behind = [(i - 2 + 4 * (i % 2), i) for i in within if i - 2 + 4 * (i % 2) in within]
    cores = [(i, i ^ 1) for i in within]
    far = lax.ppermute(own, "blk", ahead)
    back = lax.ppermute(own, "blk", behind)
    near = lax.ppermute(own, "blk", cores)

    run = functools.partial(attend, classes=block_class, segments=segments, odds=odds)
    both = (True, False)
    splits, state, _, _ = run("attend_own", sets=both, splits=(q_partner, split_own), blocks={"own": own})
    far, state = lax.optimization_barrier((far, state))
    late = lax.ppermute(far, "blk", cores)
    theirs = functools.partial(run, sets=both[:1], splits=splits[:1])
    _, passed, laid, _ = theirs("attend_near", state=state[:1], blocks={"near": near, "far": far})
    _, _, rest, to_send = theirs("attend_partner", state=passed, blocks={"late": late, "back": back}, final=True)
    others = lax.ppermute(to_send, "uly", partner)
    mine = run("attend_rest", sets=both[1:], splits=splits[1:], state=state[1:], laid=(laid, rest), final=True)[3]
    return pl.pallas_call(
        combine_kernel,
        out_shape=jax.ShapeDtypeStruct((ROWS, 2 * WIDTH), jnp.bfloat16),
        in_specs=[vmem, vmem],
        out_specs=hbm,
        scratch_shapes=[pltpu.SemaphoreType.DMA((2,))],
        compiler_params=VMEM,
        name="combine",
    )(mine, others)


def solution(mesh):
    rows = P(("blk", "uly"), None)
    line = P(("blk", "uly"))
    return jax.shard_map(
        shards,
        mesh=mesh,
        in_specs=(rows, rows, rows, line, line, P(), P()),
        out_specs=rows,
        check_vma=False,
    )
```

time: 84.2 us -> 74.4 us (0.88)
  the two profiles are of different devices: /device:TPU:19 before, /device:TPU:16 now
where the time goes in v2:
time: 74.4 us; the launch traced here: 74 us
  starting transfers between devices  31.1 us (42%)
  Pallas kernels  22.9 us (31%)
  waiting for transfers between devices  18.8 us (25%)
  local copies, waits for them, and re-layouts  0.93 us (1%)
    pallas_call x4, Pallas kernels, attend(): pl.pallas_call(functools.partial(attend_kernel, sets, roles, len(laid), s...  17.3 us
    ppermute x1, starting transfers between devices, shards(): far = lax.ppermute(own, 'blk', ahead)  11.7 us
    all_to_all x1, starting transfers between devices, shards(): lax.all_to_all(payload, 'uly', split_axis=0, concat_axis=0, tiled=True)  7.78 us
    all_to_all x1, waiting for transfers between devices, shards(): lax.all_to_all(payload, 'uly', split_axis=0, concat_axis=0, tiled=True)  7.72 us
    ppermute x1, waiting for transfers between devices, shards(): q_partner = lax.ppermute(q_other, 'uly', partner)  4.92 us
    ppermute x1, starting transfers between devices, shards(): q_partner = lax.ppermute(q_other, 'uly', partner)  3.93 us
    ppermute x1, waiting for transfers between devices, shards(): others = lax.ppermute(to_send, 'uly', partner)  3.29 us
    ppermute x1, waiting for transfers between devices, shards(): far = lax.ppermute(own, 'blk', ahead)  2.87 us
  transfers between devices with their start and end apart: 7, of which 4 were waited for; matrix products, arithmetic and copies ran while one was open for 0% of the time, Pallas kernels for 21%

profile of v2, /device:TPU:16, one launch (start us, length us, event | category | flops | bytes accessed | tf_op | source)
XLA Modules:
  0.0 74.0 jit_solution(12585118039011787502)
XLA Ops:
  0.0 0.0 copy-start
  0.0 0.0 copy-start.2
  0.0 2.7 %rotate_keys.1 = (bf16[8,256,128]{2,1,0:T(8,128)(2,1)}, f32[3,128,128]{2,1,0:T(8,128)}) custom-call(s32[1,128]{1,0:T(1,128)} %bitcast.4, s32[1,128]{1,0:T(1,128)} %bitcast.5, f32[1,128]{1,0:T(1,128)} %constant.2.clone.frequency, bf16[128,256]{1,0:T(8,128)(2,1)} %keys_in.1, bf16[128,256]{1,0:T(8,128)(2,1)} %values_in.1), custom_call_target="tpu_custom_call" | custom-call | tf_op jit(solution)/shard_map/rotate_keys/pallas_call | solution.py:350
  2.7 0.0 copy-start.3
  2.7 7.8 %all-to-all-start = ((bf16[8,256,128]{2,1,0:T(8,128)(2,1)}), bf16[8,256,128]{2,1,0:T(8,128)(2,1)S(1)}, u32[]{:S(2)}, u32[]{:S(2)}) async-start(bf16[8,256,128]{2,1,0:T(8,128)(2,1)} %get-tuple-element.28), calls=%async_computation | async-start | bytes 1048576 | tf_op jit(solution)/shard_map/all_to_all | solution.py:368
  10.5 0.0 copy-done
  10.5 0.0 copy-start.1
  10.5 0.9 %copy-done.1 = f32[3,128,128]{2,1,0:T(8,128)S(1)} copy-done((f32[3,128,128]{2,1,0:T(8,128)S(1)}, f32[3,128,128]{2,1,0:T(8,128)}, u32[]{:S(2)}) %copy-start.1) | copy-done | bytes 196632
  11.4 0.4 rotate_other_queries.1
  11.9 3.9 %collective-permute-start = (bf16[128,1024]{1,0:T(8,128)(2,1)S(1)}, bf16[128,1024]{1,0:T(8,128)(2,1)S(1)}, u32[]{:S(2)}, u32[]{:S(2)}) collective-permute-start(bf16[128,1024]{1,0:T(8,128)(2,1)S(1)} %rotate_other_queries.1), channel_id=1, source_target_pairs={{0,2},{1,3},{2,0},{3,1},{4,6},{5,7},{6,4},{7,5},{8,10},{9,11},{10,... | collective-permute-start | bytes 786440 | tf_op jit(solution)/shard_map/ppermute | solution.py:377
  15.8 0.0 copy-done.2
  15.8 1.7 %rotate_own_queries.1 = (bf16[256,1024]{1,0:T(8,128)(2,1)S(1)}, bf16[5120,128]{1,0:T(8,128)(2,1)S(1)}, s32[40,1,128]{2,1,0:T(1,128)S(1)}) custom-call(bf16[128,2048]{1,0:T(8,128)(2,1)S(1)} %copy-done, f32[3,128,128]{2,1,0:T(8,128)S(1)} %copy-done.1, s32[512,1,128]{2,1,0:T(1,128)S(1)} %bitcast.3), custom_call_target="tpu_custom_call" | custom-call | tf_op jit(solution)/shard_map/rotate_own_queries/pallas_call | solution.py:378
  17.5 4.9 %collective-permute-done.refs_3_ = bf16[128,1024]{1,0:T(8,128)(2,1)S(1)} collective-permute-done((bf16[128,1024]{1,0:T(8,128)(2,1)S(1)}, bf16[128,1024]{1,0:T(8,128)(2,1)S(1)}, u32[]{:S(2)}, u32[]{:S(2)}) %collective-permute-start) | collective-permute-done | bytes 262176 | tf_op jit(solution)/shard_map/ppermute | solution.py:377
  22.4 7.7 %all-to-all-done.refs_5_ = bf16[8,256,128]{2,1,0:T(8,128)(2,1)S(1)} async-done(((bf16[8,256,128]{2,1,0:T(8,128)(2,1)}), bf16[8,256,128]{2,1,0:T(8,128)(2,1)S(1)}, u32[]{:S(2)}, u32[]{:S(2)}) %all-to-all-start) | async-done | bytes 524320 | tf_op jit(solution)/shard_map/all_to_all | solution.py:368
  30.1 11.7 %collective-permute-start.2 = (bf16[8,256,128]{2,1,0:T(8,128)(2,1)S(1)}, bf16[8,256,128]{2,1,0:T(8,128)(2,1)S(1)}, u32[]{:S(2)}, u32[]{:S(2)}) collective-permute-start(bf16[8,256,128]{2,1,0:T(8,128)(2,1)S(1)} %all-to-all-done.refs_5_), channel_id=1, source_target_pairs={{16,0},{32,16},{8,24},{48,32},{24,40},{64,48},{40,56},{80,64},{56,... | collective-permute-start | bytes 1572872 | tf_op jit(solution)/shard_map/ppermute | solution.py:398
  41.8 1.9 %collective-permute-start.4 = (bf16[8,256,128]{2,1,0:T(8,128)(2,1)S(1)}, bf16[8,256,128]{2,1,0:T(8,128)(2,1)S(1)}, u32[]{:S(2)}, u32[]{:S(2)}) collective-permute-start(bf16[8,256,128]{2,1,0:T(8,128)(2,1)S(1)} %all-to-all-done.refs_5_), channel_id=1, source_target_pairs={{24,8},{0,16},{40,24},{16,32},{56,40},{32,48},{72,56},{48,64},{88,... | collective-permute-start | bytes 1572872 | tf_op jit(solution)/shard_map/ppermute | solution.py:399
  43.8 1.9 %collective-permute-start.1 = (bf16[8,256,128]{2,1,0:T(8,128)(2,1)S(1)}, bf16[8,256,128]{2,1,0:T(8,128)(2,1)S(1)}, u32[]{:S(2)}, u32[]{:S(2)}) collective-permute-start(bf16[8,256,128]{2,1,0:T(8,128)(2,1)S(1)} %all-to-all-done.refs_5_), channel_id=1, source_target_pairs={{0,8},{8,0},{16,24},{24,16},{32,40},{40,32},{48,56},{56,48},{64,72... | collective-permute-start | bytes 1572872 | tf_op jit(solution)/shard_map/ppermute | solution.py:400
  45.7 0.0 copy-done.3
  45.7 4.9 %attend_own.1 = (f32[144,1024]{1,0:T(8,128)S(1)}, f32[144,1024]{1,0:T(8,128)S(1)}, bf16[256,1024]{1,0:T(8,128)(2,1)S(1)}, bf16[1,1024,256]{2,1,0:T(8,128)(2,1)}, bf16[1,128,1024]{2,1,0:T(8,128)(2,1)}) custom-call(s32[64]{0:T(128)S(1)} %copy-done.3, s32[40,1,128]{2,1,0:T(1,128)S(1)} %get-tuple-element.33.refs_1_, ...), custom_call_target="tpu_custom_call" | custom-call | flops 2147483648 | bytes 1048576 | tf_op jit(solution)/shard_map/attend_own/pallas_call | solution.py:329
  50.6 2.9 %collective-permute-done.2.refs_5_ = bf16[8,256,128]{2,1,0:T(8,128)(2,1)S(1)} collective-permute-done((bf16[8,256,128]{2,1,0:T(8,128)(2,1)S(1)}, bf16[8,256,128]{2,1,0:T(8,128)(2,1)S(1)}, u32[]{:S(2)}, u32[]{:S(2)}) %collective-permute-start.2) | collective-permute-done | bytes 524320 | tf_op jit(solution)/shard_map/ppermute | solution.py:398
  53.4 1.9 %collective-permute-start.3 = (bf16[8,256,128]{2,1,0:T(8,128)(2,1)S(1)}, bf16[8,256,128]{2,1,0:T(8,128)(2,1)S(1)}, u32[]{:S(2)}, u32[]{:S(2)}) collective-permute-start(bf16[8,256,128]{2,1,0:T(8,128)(2,1)S(1)} %collective-permute-done.2.refs_5_), channel_id=1, source_target_pairs={{0,8},{8,0},{16,24},{24,16},{32,40},{40,32},{48,56},{56,48},{64,72... | collective-permute-start | bytes 1572872 | tf_op jit(solution)/shard_map/ppermute | solution.py:406
  55.3 0.0 collective-permute-done.1.refs_4_
  55.4 3.2 %attend_near.1 = (f32[144,1024]{1,0:T(8,128)S(1)}, bf16[2,1024,256]{2,1,0:T(8,128)(2,1)S(1)}, bf16[2,128,1024]{2,1,0:T(8,128)(2,1)S(1)}) custom-call(s32[64]{0:T(128)S(1)} %copy-done.3, s32[40,1,128]{2,1,0:T(1,128)S(1)} %get-tuple-element.33.refs_1_, bf16[5120,128]{1,0:T(8,128)(2,1)S(1)} %get-tuple-element.34.refs_2_, ...), custom_call_target="tpu_custom_call" | custom-call | flops 2147483648 | bytes 1048576 | tf_op jit(solution)/shard_map/attend_near/pallas_call | solution.py:329
  58.6 0.0 collective-permute-done.4.refs_5_
  58.6 0.0 collective-permute-done.3.refs_4_
  58.6 3.9 %attend_partner.1 = (f32[144,1024]{1,0:T(8,128)}, bf16[128,1024]{1,0:T(8,128)(2,1)S(1)}, bf16[2,1024,256]{2,1,0:T(8,128)(2,1)S(1)}, bf16[2,128,1024]{2,1,0:T(8,128)(2,1)S(1)}) custom-call(s32[64]{0:T(128)S(1)} %copy-done.3, s32[40,1,128]{2,1,0:T(1,128)S(1)} %get-tuple-element.33.refs_1_, bf16[5120,128]{1,0:T(8,128)(2,1)S(1)} %get-tuple-element.34.refs_2_, ...), custom_call_target="tpu_custom_call" | custom-call | flops 2147483648 | bytes 1048576 | tf_op jit(solution)/shard_map/attend_partner/pallas_call | solution.py:329
  62.4 1.9 %collective-permute-start.5 = (bf16[128,1024]{1,0:T(8,128)(2,1)S(1)}, bf16[128,1024]{1,0:T(8,128)(2,1)S(1)}, u32[]{:S(2)}, u32[]{:S(2)}) collective-permute-start(bf16[128,1024]{1,0:T(8,128)(2,1)S(1)} %get-tuple-element.50), channel_id=1, source_target_pairs={{0,2},{1,3},{2,0},{3,1},{4,6},{5,7},{6,4},{7,5},{8,10},{9,11},{10,... | collective-permute-start | bytes 786440 | tf_op jit(solution)/shard_map/ppermute | solution.py:410
  64.4 5.4 %attend_rest.1 = (f32[144,1024]{1,0:T(8,128)}, bf16[128,1024]{1,0:T(8,128)(2,1)S(1)}) custom-call(s32[64]{0:T(128)S(1)} %copy-done.3, s32[40,1,128]{2,1,0:T(1,128)S(1)} %get-tuple-element.33.refs_1_, bf16[5120,128]{1,0:T(8,128)(2,1)S(1)} %get-tuple-element.34.refs_2_, bf16[2,1024,256]{2,1,0:T(8,128)(2,1)S(1)} %get-tuple-element.43.refs_3_, ...), custom_call_target="tpu_custom_call" | custom-call | flops 4294967296 | bytes 1048576 | tf_op jit(solution)/shard_map/attend_rest/pallas_call | solution.py:329
  69.7 3.3 %collective-permute-done.5.others = bf16[128,1024]{1,0:T(8,128)(2,1)S(1)} collective-permute-done((bf16[128,1024]{1,0:T(8,128)(2,1)S(1)}, bf16[128,1024]{1,0:T(8,128)(2,1)S(1)}, u32[]{:S(2)}, u32[]{:S(2)}) %collective-permute-start.5) | collective-permute-done | bytes 262176 | tf_op jit(solution)/shard_map/ppermute | solution.py:410
  73.0 0.8 %combine.1 = bf16[128,2048]{1,0:T(8,128)(2,1)} custom-call(bf16[128,1024]{1,0:T(8,128)(2,1)S(1)} %get-tuple-element.49.mine, bf16[128,1024]{1,0:T(8,128)(2,1)S(1)} %collective-permute-done.5.others), custom_call_target="tpu_custom_call" | custom-call | tf_op jit(solution)/shard_map/combine/pallas_call | solution.py:412
Async XLA Ops:
  0.0 10.5 %copy-start = (bf16[128,2048]{1,0:T(8,128)(2,1)S(1)}, bf16[128,2048]{1,0:T(8,128)(2,1)}, u32[]{:S(2)}) copy-start(bf16[128,2048]{1,0:T(8,128)(2,1)} %queries.3) | copy-start | bytes 1572868
  0.0 15.8 %copy-start.2 = (s32[65536]{0:T(1024)S(1)}, s32[65536]{0:T(1024)}, u32[]{:S(2)}) copy-start(s32[65536]{0:T(1024)} %param.13) | copy-start | bytes 786436
  2.7 43.0 %copy-start.3 = (s32[64]{0:T(128)S(1)}, s32[64]{0:T(128)}, u32[]{:S(2)}) copy-start(s32[64]{0:T(128)} %refs_0_.7) | copy-start | bytes 772
  2.7 27.4 %all-to-all-start = ((bf16[8,256,128]{2,1,0:T(8,128)(2,1)}), bf16[8,256,128]{2,1,0:T(8,128)(2,1)S(1)}, u32[]{:S(2)}, u32[]{:S(2)}) async-start(bf16[8,256,128]{2,1,0:T(8,128)(2,1)} %get-tuple-element.28), calls=%async_computation | async-start | bytes 1048576 | tf_op jit(solution)/shard_map/all_to_all | solution.py:368
  10.5 0.9 %copy-start.1 = (f32[3,128,128]{2,1,0:T(8,128)S(1)}, f32[3,128,128]{2,1,0:T(8,128)}, u32[]{:S(2)}) copy-start(f32[3,128,128]{2,1,0:T(8,128)} %get-tuple-element.29.tables) | copy-start | bytes 589828
  11.9 10.5 %collective-permute-start = (bf16[128,1024]{1,0:T(8,128)(2,1)S(1)}, bf16[128,1024]{1,0:T(8,128)(2,1)S(1)}, u32[]{:S(2)}, u32[]{:S(2)}) collective-permute-start(bf16[128,1024]{1,0:T(8,128)(2,1)S(1)} %rotate_other_queries.1), channel_id=1, source_target_pairs={{0,2},{1,3},{2,0},{3,1},{4,6},{5,7},{6,4},{7,5},{8,10},{9,11},{10,... | collective-permute-start | bytes 786440 | tf_op jit(solution)/shard_map/ppermute | solution.py:377
  30.1 23.3 %collective-permute-start.2 = (bf16[8,256,128]{2,1,0:T(8,128)(2,1)S(1)}, bf16[8,256,128]{2,1,0:T(8,128)(2,1)S(1)}, u32[]{:S(2)}, u32[]{:S(2)}) collective-permute-start(bf16[8,256,128]{2,1,0:T(8,128)(2,1)S(1)} %all-to-all-done.refs_5_), channel_id=1, source_target_pairs={{16,0},{32,16},{8,24},{48,32},{24,40},{64,48},{40,56},{80,64},{56,... | collective-permute-start | bytes 1572872 | tf_op jit(solution)/shard_map/ppermute | solution.py:398
  41.8 16.7 %collective-permute-start.4 = (bf16[8,256,128]{2,1,0:T(8,128)(2,1)S(1)}, bf16[8,256,128]{2,1,0:T(8,128)(2,1)S(1)}, u32[]{:S(2)}, u32[]{:S(2)}) collective-permute-start(bf16[8,256,128]{2,1,0:T(8,128)(2,1)S(1)} %all-to-all-done.refs_5_), channel_id=1, source_target_pairs={{24,8},{0,16},{40,24},{16,32},{56,40},{32,48},{72,56},{48,64},{88,... | collective-permute-start | bytes 1572872 | tf_op jit(solution)/shard_map/ppermute | solution.py:399
  43.8 11.6 %collective-permute-start.1 = (bf16[8,256,128]{2,1,0:T(8,128)(2,1)S(1)}, bf16[8,256,128]{2,1,0:T(8,128)(2,1)S(1)}, u32[]{:S(2)}, u32[]{:S(2)}) collective-permute-start(bf16[8,256,128]{2,1,0:T(8,128)(2,1)S(1)} %all-to-all-done.refs_5_), channel_id=1, source_target_pairs={{0,8},{8,0},{16,24},{24,16},{32,40},{40,32},{48,56},{56,48},{64,72... | collective-permute-start | bytes 1572872 | tf_op jit(solution)/shard_map/ppermute | solution.py:400
  53.4 5.2 %collective-permute-start.3 = (bf16[8,256,128]{2,1,0:T(8,128)(2,1)S(1)}, bf16[8,256,128]{2,1,0:T(8,128)(2,1)S(1)}, u32[]{:S(2)}, u32[]{:S(2)}) collective-permute-start(bf16[8,256,128]{2,1,0:T(8,128)(2,1)S(1)} %collective-permute-done.2.refs_5_), channel_id=1, source_target_pairs={{0,8},{8,0},{16,24},{24,16},{32,40},{40,32},{48,56},{56,48},{64,72... | collective-permute-start | bytes 1572872 | tf_op jit(solution)/shard_map/ppermute | solution.py:406
  62.4 10.6 %collective-permute-start.5 = (bf16[128,1024]{1,0:T(8,128)(2,1)S(1)}, bf16[128,1024]{1,0:T(8,128)(2,1)S(1)}, u32[]{:S(2)}, u32[]{:S(2)}) collective-permute-start(bf16[128,1024]{1,0:T(8,128)(2,1)S(1)} %get-tuple-element.50), channel_id=1, source_target_pairs={{0,2},{1,3},{2,0},{3,1},{4,6},{5,7},{6,4},{7,5},{8,10},{9,11},{10,... | collective-permute-start | bytes 786440 | tf_op jit(solution)/shard_map/ppermute | solution.py:410

commit v3 on v2

--- a/solution.py
+++ b/solution.py
@@ -15,7 +15,7 @@
 SHARDS = 8
 BLOCK = ROWS * SHARDS
 BLOCKS = 64
-STACK = 4
+STACK = 8
 NEGATIVE = -1e30
 SCALE = HEAD_DIM**-0.5 * 1.4426950408889634
 MAXIMUM = HEAD_DIM + 8
@@ -26,6 +26,10 @@
 def lane_frequencies():
     one = 10000.0 ** (-np.arange(16, dtype=np.float64) / 16)
     return np.concatenate([one, one, one, one, np.zeros(64)]).astype(np.float32)[None, :]
+
+
+def partner_of(block, uly):
+    return uly ^ (2 + 4 * (block % 2))
 
 
 def rotate(x, cosine, minus, plus):
@@ -126,13 +130,16 @@
         splits = [refs.pop(0) for _ in range(count)]
     blocks = [] if pairs else [refs.pop(0) for _ in roles]
     given = [] if start else [refs.pop(0) for _ in range(count)]
-    states = [refs.pop(0) for _ in range(count)]
+    bias = refs.pop(-1) if start else None
+    outs = [refs.pop(0) for _ in range(count)] if final else []
+    if final:
+        states = refs[-count:]
+    else:
+        states = [refs.pop(0) for _ in range(count)]
     if start:
         splits[0] = refs.pop(0)
-    outs = [refs.pop(0) for _ in range(count)] if final else []
     if not pairs:
         laid = [(refs.pop(0), refs.pop(0))]
-    (bias,) = refs
     keys = [pair[0].at[i] for pair in laid for i in range(pair[0].shape[0])]
     values = [pair[1].at[i] for pair in laid for i in range(pair[1].shape[0])]
 
@@ -144,7 +151,7 @@
     square = (ROWS, ROWS)
     lane = lax.broadcasted_iota(jnp.int32, square, 1)
     tip = lax.broadcasted_iota(jnp.int32, square, 0)
-    chunks = [uly ^ 2 if theirs else uly for theirs in sets]
+    chunks = [partner_of(me, uly) if theirs else uly for theirs in sets]
 
     def odd_tokens(s, shape):
         segment = segments[(me - base) * SHARDS + chunks[s]]
@@ -191,12 +198,13 @@
 
     def take(which, masked):
         steps = [(j, s, cols) for j in which for s, cols in items]
+        tops = [states[s][MAXIMUM : MAXIMUM + 1, :] for s in range(count)]
         ahead = scores(*steps[0])
         for i, (j, s, cols) in enumerate(steps):
             now, ahead = ahead, scores(*steps[i + 1]) if i + 1 < len(steps) else None
             if masked:
                 now = now + jnp.concatenate([bias[s]] * STACK, axis=1)
-            weights = jnp.exp2(now - states[s][MAXIMUM : MAXIMUM + 1, cols])
+            weights = jnp.exp2(now - tops[s][:, cols])
             part = jnp.dot(values[j][...], weights.astype(jnp.bfloat16), preferred_element_type=jnp.float32)
             states[s][:HEAD_DIM, cols] += part
             states[s][HEAD_DIM : HEAD_DIM + 1, cols] += jnp.sum(weights, axis=0, keepdims=True)
@@ -292,10 +300,10 @@
             each_block(take_largest)
 
     for s, out in enumerate(outs):
+        share = 1.0 / states[s][HEAD_DIM : HEAD_DIM + 1, :]
         for head in range(HEADS_PER_GROUP):
             cols = slice(head * ROWS, (head + 1) * ROWS)
-            value = states[s][:HEAD_DIM, cols] / states[s][HEAD_DIM : HEAD_DIM + 1, cols]
-            out[:, cols] = value.T.astype(jnp.bfloat16)
+            out[:, cols] = (states[s][:HEAD_DIM, cols] * share[:, cols]).T.astype(jnp.bfloat16)
 
 
 def combine_kernel(mine, others, out, sems):
@@ -310,19 +318,28 @@
         copy.wait()
 
 
-def attend(name, classes, segments, odds, sets, splits, blocks=None, laid=(), state=None, final=False):
+def attend(name, classes, segments, odds, sets, splits, blocks=None, laid=(), state=None, keep=True, final=False):
     roles = tuple(blocks) if blocks else tuple(role for group in laid for role in group[0])
     count, number = len(sets), len(roles)
     start = state is None
     whole = pl.BlockSpec(memory_space=pltpu.VMEM)
-    shapes = [jax.ShapeDtypeStruct((MAXIMUM + 8, WIDTH), jnp.float32)] * count
-    if start:
-        shapes.append(jax.ShapeDtypeStruct((2 * HEAD_DIM, WIDTH), jnp.bfloat16))
+    state_shape, split_shape = (MAXIMUM + 8, WIDTH), (2 * HEAD_DIM, WIDTH)
+    laid_shapes = [(number, BLOCK, 2 * HEAD_DIM), (number, HEAD_DIM, BLOCK)]
+    shapes, scratch = [], []
     if final:
         shapes.append(jax.ShapeDtypeStruct((ROWS, WIDTH), jnp.bfloat16))
-    if blocks:
-        shapes.append(jax.ShapeDtypeStruct((number, BLOCK, 2 * HEAD_DIM), jnp.bfloat16))
-        shapes.append(jax.ShapeDtypeStruct((number, HEAD_DIM, BLOCK), jnp.bfloat16))
+        laid_out = [jax.ShapeDtypeStruct(shape, jnp.bfloat16) for shape in laid_shapes] if blocks else []
+        scratch += [pltpu.VMEM(state_shape, jnp.float32)] * count
+    else:
+        shapes += [jax.ShapeDtypeStruct(state_shape, jnp.float32)] * count
+        laid_out = [jax.ShapeDtypeStruct(shape, jnp.bfloat16) for shape in laid_shapes] if blocks else []
+        if start or not keep:
+            scratch += [pltpu.VMEM(shape, jnp.bfloat16) for shape in laid_shapes]
+            laid_out = []
+        if start:
+            shapes.append(jax.ShapeDtypeStruct(split_shape, jnp.bfloat16))
+            scratch.append(pltpu.VMEM((count, BLOCK, ROWS), jnp.float32))
+    shapes += laid_out
     given = [odds, *(x for group in laid for x in group[1:]), *splits, *(blocks or {}).values(), *(state or ())]
     pairs = count * number * HEADS_PER_GROUP * ROWS * BLOCK
     results = list(
@@ -331,18 +348,17 @@
             out_shape=shapes,
             in_specs=[pl.BlockSpec(memory_space=pltpu.SMEM)] + [whole] * (1 + len(given)),
             out_specs=[whole] * len(shapes),
-            scratch_shapes=[pltpu.VMEM((count, BLOCK if start else 8, ROWS), jnp.float32)],
+            scratch_shapes=scratch,
             compiler_params=VMEM,
             cost_estimate=pl.CostEstimate(flops=8 * pairs * HEAD_DIM, bytes_accessed=2**20, transcendentals=pairs),
             name=name,
         )(classes, segments, *given)
     )
-    if blocks:
+    if laid_out:
         laid = (roles, *results[-2:])
-    states = results[:count]
     if start:
         splits = [results[count], splits[1]]
-    return splits, states, laid, results[count] if final else None
+    return splits, results[:count], laid, results[0] if final else None
 
 
 def shards(queries, key_rows, value_rows, span_place, span_offset, segment_number, block_class):
@@ -373,8 +389,9 @@
         compiler_params=VMEM,
         name="rotate_other_queries",
     )(queries, tables)
-    partner = [(i, i ^ 2) for i in range(SHARDS)]
-    q_partner = lax.ppermute(q_other, "uly", partner)
+    every = [(b, u) for b in range(BLOCKS) for u in range(SHARDS)]
+    partners = [(b * SHARDS + u, b * SHARDS + partner_of(b, u)) for b, u in every]
+    q_partner = lax.ppermute(q_other, ("blk", "uly"), partners)
     split_own, odds, segments = pl.pallas_call(
         own_queries_kernel,
         out_shape=[
@@ -402,12 +419,13 @@
     run = functools.partial(attend, classes=block_class, segments=segments, odds=odds)
     both = (True, False)
     splits, state, _, _ = run("attend_own", sets=both, splits=(q_partner, split_own), blocks={"own": own})
+    _, state, _, _ = run("attend_near", sets=both, splits=splits, state=state, blocks={"near": near}, keep=False)
     far, state = lax.optimization_barrier((far, state))
     late = lax.ppermute(far, "blk", cores)
     theirs = functools.partial(run, sets=both[:1], splits=splits[:1])
-    _, passed, laid, _ = theirs("attend_near", state=state[:1], blocks={"near": near, "far": far})
-    _, _, rest, to_send = theirs("attend_partner", state=passed, blocks={"late": late, "back": back}, final=True)
-    others = lax.ppermute(to_send, "uly", partner)
+    _, passed, laid, _ = theirs("attend_far", state=state[:1], blocks={"far": far, "back": back})
+    _, _, rest, to_send = theirs("attend_partner", state=passed, blocks={"late": late}, final=True)
+    others = lax.ppermute(to_send, ("blk", "uly"), partners)
     mine = run("attend_rest", sets=both[1:], splits=splits[1:], state=state[1:], laid=(laid, rest), final=True)[3]
     return pl.pallas_call(
         combine_kernel,

time: 74.4 us -> 72 us (0.968)
  Pallas kernels: 22.9 us -> 20.8 us
  waiting for transfers between devices: 18.8 us -> 17.9 us
    pallas_call x4 -> x5, Pallas kernels: 17.3 us -> 15.2 us  [attend(): pl.pallas_call(functools.partial(attend_kernel, sets, roles, len(laid), s...]
    ppermute x2, waiting for transfers between devices: 8.21 us -> 6.26 us  [the longest x1 3.52 us: shards(): q_partner = lax.ppermute(q_other, ('blk', 'uly'), partners)]
    all_to_all x1, waiting for transfers between devices: 7.72 us -> 9.12 us  [shards(): lax.all_to_all(payload, 'uly', split_axis=0, concat_axis=0, tiled=True)]
  transfers between devices with their start and end apart: 7 -> 7, of which waited for: 4 -> 5; matrix products, arithmetic and copies ran while one was open for 0% -> 0% of each run, Pallas kernels for 21% -> 21%
where the time goes in v3:
time: 72 us; the launch traced here: 71.2 us
  starting transfers between devices  31.3 us (43%)
  Pallas kernels  20.8 us (29%)
  waiting for transfers between devices  17.9 us (25%)
  local copies, waits for them, and re-layouts  0.93 us (1%)
    pallas_call x5, Pallas kernels, attend(): pl.pallas_call(functools.partial(attend_kernel, sets, roles, len(laid), s...  15.2 us
    ppermute x1, starting transfers between devices, shards(): far = lax.ppermute(own, 'blk', ahead)  11.7 us
    all_to_all x1, waiting for transfers between devices, shards(): lax.all_to_all(payload, 'uly', split_axis=0, concat_axis=0, tiled=True)  9.12 us
    all_to_all x1, starting transfers between devices, shards(): lax.all_to_all(payload, 'uly', split_axis=0, concat_axis=0, tiled=True)  7.78 us
    ppermute x1, starting transfers between devices, shards(): q_partner = lax.ppermute(q_other, ('blk', 'uly'), partners)  3.93 us
    ppermute x1, waiting for transfers between devices, shards(): q_partner = lax.ppermute(q_other, ('blk', 'uly'), partners)  3.52 us
    ppermute x1, waiting for transfers between devices, shards(): others = lax.ppermute(to_send, ('blk', 'uly'), partners)  2.73 us
    pallas_call x1, Pallas kernels, shards(): pl.pallas_call(keys_kernel, out_shape=[jax.ShapeDtypeStruct((SHARDS, 2 *...  2.7 us
  transfers between devices with their start and end apart: 7, of which 5 were waited for; matrix products, arithmetic and copies ran while one was open for 0% of the time, Pallas kernels for 21%

profile of v3, /device:TPU:16, one launch (start us, length us, event | category | flops | bytes accessed | tf_op | source)
XLA Modules:
  0.0 71.2 jit_solution(7486092345283436293)
XLA Ops:
  0.0 0.0 copy-start
  0.0 0.0 copy-start.2
  0.0 2.7 %rotate_keys.1 = (bf16[8,256,128]{2,1,0:T(8,128)(2,1)}, f32[3,128,128]{2,1,0:T(8,128)}) custom-call(s32[1,128]{1,0:T(1,128)} %bitcast.4, s32[1,128]{1,0:T(1,128)} %bitcast.5, f32[1,128]{1,0:T(1,128)} %constant.2.clone.frequency, bf16[128,256]{1,0:T(8,128)(2,1)} %keys_in.1, bf16[128,256]{1,0:T(8,128)(2,1)} %values_in.1), custom_call_target="tpu_custom_call" | custom-call | tf_op jit(solution)/shard_map/rotate_keys/pallas_call | solution.py:366
  2.7 0.0 copy-start.3
  2.7 7.8 %all-to-all-start = ((bf16[8,256,128]{2,1,0:T(8,128)(2,1)}), bf16[8,256,128]{2,1,0:T(8,128)(2,1)S(1)}, u32[]{:S(2)}, u32[]{:S(2)}) async-start(bf16[8,256,128]{2,1,0:T(8,128)(2,1)} %get-tuple-element.29), calls=%async_computation | async-start | bytes 1048576 | tf_op jit(solution)/shard_map/all_to_all | solution.py:384
  10.5 0.0 copy-done
  10.5 0.0 copy-start.1
  10.5 0.9 %copy-done.1 = f32[3,128,128]{2,1,0:T(8,128)S(1)} copy-done((f32[3,128,128]{2,1,0:T(8,128)S(1)}, f32[3,128,128]{2,1,0:T(8,128)}, u32[]{:S(2)}) %copy-start.1) | copy-done | bytes 196632
  11.4 0.4 rotate_other_queries.1
  11.9 3.9 %collective-permute-start = (bf16[128,1024]{1,0:T(8,128)(2,1)S(1)}, bf16[128,1024]{1,0:T(8,128)(2,1)S(1)}, u32[]{:S(2)}, u32[]{:S(2)}) collective-permute-start(bf16[128,1024]{1,0:T(8,128)(2,1)S(1)} %rotate_other_queries.1), channel_id=1, source_target_pairs={{0,2},{1,3},{2,0},{3,1},{4,6},{5,7},{6,4},{7,5},{8,14},{9,15},{10,... | collective-permute-start | bytes 786440 | tf_op jit(solution)/shard_map/ppermute | solution.py:394
  15.8 0.0 copy-done.2
  15.8 1.7 %rotate_own_queries.1 = (bf16[256,1024]{1,0:T(8,128)(2,1)S(1)}, bf16[5120,128]{1,0:T(8,128)(2,1)S(1)}, s32[40,1,128]{2,1,0:T(1,128)S(1)}) custom-call(bf16[128,2048]{1,0:T(8,128)(2,1)S(1)} %copy-done, f32[3,128,128]{2,1,0:T(8,128)S(1)} %copy-done.1, s32[512,1,128]{2,1,0:T(1,128)S(1)} %bitcast.3), custom_call_target="tpu_custom_call" | custom-call | tf_op jit(solution)/shard_map/rotate_own_queries/pallas_call | solution.py:395
  17.5 3.5 %collective-permute-done.refs_3_ = bf16[128,1024]{1,0:T(8,128)(2,1)S(1)} collective-permute-done((bf16[128,1024]{1,0:T(8,128)(2,1)S(1)}, bf16[128,1024]{1,0:T(8,128)(2,1)S(1)}, u32[]{:S(2)}, u32[]{:S(2)}) %collective-permute-start) | collective-permute-done | bytes 262176 | tf_op jit(solution)/shard_map/ppermute | solution.py:394
  21.0 9.1 %all-to-all-done.refs_5_ = bf16[8,256,128]{2,1,0:T(8,128)(2,1)S(1)} async-done(((bf16[8,256,128]{2,1,0:T(8,128)(2,1)}), bf16[8,256,128]{2,1,0:T(8,128)(2,1)S(1)}, u32[]{:S(2)}, u32[]{:S(2)}) %all-to-all-start) | async-done | bytes 524320 | tf_op jit(solution)/shard_map/all_to_all | solution.py:384
  30.1 1.9 %collective-permute-start.2 = (bf16[8,256,128]{2,1,0:T(8,128)(2,1)S(1)}, bf16[8,256,128]{2,1,0:T(8,128)(2,1)S(1)}, u32[]{:S(2)}, u32[]{:S(2)}) collective-permute-start(bf16[8,256,128]{2,1,0:T(8,128)(2,1)S(1)} %all-to-all-done.refs_5_), channel_id=1, source_target_pairs={{0,8},{8,0},{16,24},{24,16},{32,40},{40,32},{48,56},{56,48},{64,72... | collective-permute-start | bytes 1572872 | tf_op jit(solution)/shard_map/ppermute | solution.py:417
  32.0 11.7 %collective-permute-start.1 = (bf16[8,256,128]{2,1,0:T(8,128)(2,1)S(1)}, bf16[8,256,128]{2,1,0:T(8,128)(2,1)S(1)}, u32[]{:S(2)}, u32[]{:S(2)}) collective-permute-start(bf16[8,256,128]{2,1,0:T(8,128)(2,1)S(1)} %all-to-all-done.refs_5_), channel_id=1, source_target_pairs={{16,0},{32,16},{8,24},{48,32},{24,40},{64,48},{40,56},{80,64},{56,... | collective-permute-start | bytes 1572872 | tf_op jit(solution)/shard_map/ppermute | solution.py:415
  43.8 1.9 %collective-permute-start.3 = (bf16[8,256,128]{2,1,0:T(8,128)(2,1)S(1)}, bf16[8,256,128]{2,1,0:T(8,128)(2,1)S(1)}, u32[]{:S(2)}, u32[]{:S(2)}) collective-permute-start(bf16[8,256,128]{2,1,0:T(8,128)(2,1)S(1)} %all-to-all-done.refs_5_), channel_id=1, source_target_pairs={{24,8},{0,16},{40,24},{16,32},{56,40},{32,48},{72,56},{48,64},{88,... | collective-permute-start | bytes 1572872 | tf_op jit(solution)/shard_map/ppermute | solution.py:416
  45.7 0.0 copy-done.3
  45.7 3.8 %attend_own.1 = (f32[144,1024]{1,0:T(8,128)S(1)}, f32[144,1024]{1,0:T(8,128)S(1)}, bf16[256,1024]{1,0:T(8,128)(2,1)S(1)}) custom-call(s32[64]{0:T(128)S(1)} %copy-done.3, s32[40,1,128]{2,1,0:T(1,128)S(1)} %get-tuple-element.34.refs_1_, bf16[5120,128]{1,0:T(8,128)(2,1)S(1)} %get-tuple-element.35.refs_2_, bf16[128,1024]{1,0:T(8,128)(2,1)S(1)} %collective-permute-done.refs_3_, ...), custom_call_target="tpu_custom_call" | custom-call | flops 2147483648 | bytes 1048576 | tf_op jit(solution)/shard_map/attend_own/pallas_call | solution.py:346
  49.5 0.0 collective-permute-done.2.refs_5_
  49.5 2.8 %attend_near.1 = (f32[144,1024]{1,0:T(8,128)S(1)}, f32[144,1024]{1,0:T(8,128)S(1)}) custom-call(s32[64]{0:T(128)S(1)} %copy-done.3, s32[40,1,128]{2,1,0:T(1,128)S(1)} %get-tuple-element.34.refs_1_, bf16[5120,128]{1,0:T(8,128)(2,1)S(1)} %get-tuple-element.35.refs_2_, bf16[256,1024]{1,0:T(8,128)(2,1)S(1)} %get-tuple-element.39.refs_3_, ...), custom_call_target="tpu_custom_call" | custom-call | flops 2147483648 | bytes 1048576 | tf_op jit(solution)/shard_map/attend_near/pallas_call | solution.py:346
  52.3 2.2 %collective-permute-done.1.refs_4_ = bf16[8,256,128]{2,1,0:T(8,128)(2,1)S(1)} collective-permute-done((bf16[8,256,128]{2,1,0:T(8,128)(2,1)S(1)}, bf16[8,256,128]{2,1,0:T(8,128)(2,1)S(1)}, u32[]{:S(2)}, u32[]{:S(2)}) %collective-permute-start.1) | collective-permute-done | bytes 524320 | tf_op jit(solution)/shard_map/ppermute | solution.py:415
  54.5 2.1 %collective-permute-start.4 = (bf16[8,256,128]{2,1,0:T(8,128)(2,1)S(1)}, bf16[8,256,128]{2,1,0:T(8,128)(2,1)S(1)}, u32[]{:S(2)}, u32[]{:S(2)}) collective-permute-start(bf16[8,256,128]{2,1,0:T(8,128)(2,1)S(1)} %collective-permute-done.1.refs_4_), channel_id=1, source_target_pairs={{0,8},{8,0},{16,24},{24,16},{32,40},{40,32},{48,56},{56,48},{64,72... | collective-permute-start | bytes 1572872 | tf_op jit(solution)/shard_map/ppermute | solution.py:424
  56.6 0.3 collective-permute-done.3.refs_5_
  57.0 3.0 %attend_far.1 = (f32[144,1024]{1,0:T(8,128)S(1)}, bf16[2,1024,256]{2,1,0:T(8,128)(2,1)S(1)}, bf16[2,128,1024]{2,1,0:T(8,128)(2,1)S(1)}) custom-call(s32[64]{0:T(128)S(1)} %copy-done.3, s32[40,1,128]{2,1,0:T(1,128)S(1)} %get-tuple-element.34.refs_1_, bf16[5120,128]{1,0:T(8,128)(2,1)S(1)} %get-tuple-element.35.refs_2_, ...), custom_call_target="tpu_custom_call" | custom-call | flops 2147483648 | bytes 1048576 | tf_op jit(solution)/shard_map/attend_far/pallas_call | solution.py:346
  59.9 0.0 collective-permute-done.4.refs_4_
  59.9 2.0 %attend_partner.1 = (bf16[128,1024]{1,0:T(8,128)(2,1)S(1)}, bf16[1,1024,256]{2,1,0:T(8,128)(2,1)S(1)}, bf16[1,128,1024]{2,1,0:T(8,128)(2,1)S(1)}) custom-call(s32[64]{0:T(128)S(1)} %copy-done.3, s32[40,1,128]{2,1,0:T(1,128)S(1)} %get-tuple-element.34.refs_1_, bf16[5120,128]{1,0:T(8,128)(2,1)S(1)} %get-tuple-element.35.refs_2_, ...), custom_call_target="tpu_custom_call" | custom-call | flops 1073741824 | bytes 1048576 | tf_op jit(solution)/shard_map/attend_partner/pallas_call | solution.py:346
  62.0 1.9 %collective-permute-start.5 = (bf16[128,1024]{1,0:T(8,128)(2,1)S(1)}, bf16[128,1024]{1,0:T(8,128)(2,1)S(1)}, u32[]{:S(2)}, u32[]{:S(2)}) collective-permute-start(bf16[128,1024]{1,0:T(8,128)(2,1)S(1)} %get-tuple-element.52), channel_id=1, source_target_pairs={{0,2},{1,3},{2,0},{3,1},{4,6},{5,7},{6,4},{7,5},{8,14},{9,15},{10,... | collective-permute-start | bytes 786440 | tf_op jit(solution)/shard_map/ppermute | solution.py:428
  63.9 3.6 %attend_rest.1.mine = bf16[128,1024]{1,0:T(8,128)(2,1)S(1)} custom-call(s32[64]{0:T(128)S(1)} %copy-done.3, s32[40,1,128]{2,1,0:T(1,128)S(1)} %get-tuple-element.34.refs_1_, bf16[5120,128]{1,0:T(8,128)(2,1)S(1)} %get-tuple-element.35.refs_2_, bf16[2,1024,256]{2,1,0:T(8,128)(2,1)S(1)} %get-tuple-element.46.refs_3_, ...), custom_call_target="tpu_custom_call" | custom-call | flops 3221225472 | bytes 1048576 | tf_op jit(solution)/shard_map/attend_rest/pallas_call | solution.py:346
  67.5 2.7 %collective-permute-done.5.others = bf16[128,1024]{1,0:T(8,128)(2,1)S(1)} collective-permute-done((bf16[128,1024]{1,0:T(8,128)(2,1)S(1)}, bf16[128,1024]{1,0:T(8,128)(2,1)S(1)}, u32[]{:S(2)}, u32[]{:S(2)}) %collective-permute-start.5) | collective-permute-done | bytes 262176 | tf_op jit(solution)/shard_map/ppermute | solution.py:428
  70.3 0.8 %combine.1 = bf16[128,2048]{1,0:T(8,128)(2,1)} custom-call(bf16[128,1024]{1,0:T(8,128)(2,1)S(1)} %attend_rest.1.mine, bf16[128,1024]{1,0:T(8,128)(2,1)S(1)} %collective-permute-done.5.others), custom_call_target="tpu_custom_call" | custom-call | tf_op jit(solution)/shard_map/combine/pallas_call | solution.py:430
Async XLA Ops:
  0.0 10.5 %copy-start = (bf16[128,2048]{1,0:T(8,128)(2,1)S(1)}, bf16[128,2048]{1,0:T(8,128)(2,1)}, u32[]{:S(2)}) copy-start(bf16[128,2048]{1,0:T(8,128)(2,1)} %queries.3) | copy-start | bytes 1572868
  0.0 15.8 %copy-start.2 = (s32[65536]{0:T(1024)S(1)}, s32[65536]{0:T(1024)}, u32[]{:S(2)}) copy-start(s32[65536]{0:T(1024)} %param.13) | copy-start | bytes 786436
  2.7 43.0 %copy-start.3 = (s32[64]{0:T(128)S(1)}, s32[64]{0:T(128)}, u32[]{:S(2)}) copy-start(s32[64]{0:T(128)} %refs_0_.9) | copy-start | bytes 772
  2.7 27.4 %all-to-all-start = ((bf16[8,256,128]{2,1,0:T(8,128)(2,1)}), bf16[8,256,128]{2,1,0:T(8,128)(2,1)S(1)}, u32[]{:S(2)}, u32[]{:S(2)}) async-start(bf16[8,256,128]{2,1,0:T(8,128)(2,1)} %get-tuple-element.29), calls=%async_computation | async-start | bytes 1048576 | tf_op jit(solution)/shard_map/all_to_all | solution.py:384
  10.5 0.9 %copy-start.1 = (f32[3,128,128]{2,1,0:T(8,128)S(1)}, f32[3,128,128]{2,1,0:T(8,128)}, u32[]{:S(2)}) copy-start(f32[3,128,128]{2,1,0:T(8,128)} %get-tuple-element.30.tables) | copy-start | bytes 589828
  11.9 9.1 %collective-permute-start = (bf16[128,1024]{1,0:T(8,128)(2,1)S(1)}, bf16[128,1024]{1,0:T(8,128)(2,1)S(1)}, u32[]{:S(2)}, u32[]{:S(2)}) collective-permute-start(bf16[128,1024]{1,0:T(8,128)(2,1)S(1)} %rotate_other_queries.1), channel_id=1, source_target_pairs={{0,2},{1,3},{2,0},{3,1},{4,6},{5,7},{6,4},{7,5},{8,14},{9,15},{10,... | collective-permute-start | bytes 786440 | tf_op jit(solution)/shard_map/ppermute | solution.py:394
  30.1 19.4 %collective-permute-start.2 = (bf16[8,256,128]{2,1,0:T(8,128)(2,1)S(1)}, bf16[8,256,128]{2,1,0:T(8,128)(2,1)S(1)}, u32[]{:S(2)}, u32[]{:S(2)}) collective-permute-start(bf16[8,256,128]{2,1,0:T(8,128)(2,1)S(1)} %all-to-all-done.refs_5_), channel_id=1, source_target_pairs={{0,8},{8,0},{16,24},{24,16},{32,40},{40,32},{48,56},{56,48},{64,72... | collective-permute-start | bytes 1572872 | tf_op jit(solution)/shard_map/ppermute | solution.py:417
  32.0 22.5 %collective-permute-start.1 = (bf16[8,256,128]{2,1,0:T(8,128)(2,1)S(1)}, bf16[8,256,128]{2,1,0:T(8,128)(2,1)S(1)}, u32[]{:S(2)}, u32[]{:S(2)}) collective-permute-start(bf16[8,256,128]{2,1,0:T(8,128)(2,1)S(1)} %all-to-all-done.refs_5_), channel_id=1, source_target_pairs={{16,0},{32,16},{8,24},{48,32},{24,40},{64,48},{40,56},{80,64},{56,... | collective-permute-start | bytes 1572872 | tf_op jit(solution)/shard_map/ppermute | solution.py:415
  43.8 13.2 %collective-permute-start.3 = (bf16[8,256,128]{2,1,0:T(8,128)(2,1)S(1)}, bf16[8,256,128]{2,1,0:T(8,128)(2,1)S(1)}, u32[]{:S(2)}, u32[]{:S(2)}) collective-permute-start(bf16[8,256,128]{2,1,0:T(8,128)(2,1)S(1)} %all-to-all-done.refs_5_), channel_id=1, source_target_pairs={{24,8},{0,16},{40,24},{16,32},{56,40},{32,48},{72,56},{48,64},{88,... | collective-permute-start | bytes 1572872 | tf_op jit(solution)/shard_map/ppermute | solution.py:416
  54.5 5.4 %collective-permute-start.4 = (bf16[8,256,128]{2,1,0:T(8,128)(2,1)S(1)}, bf16[8,256,128]{2,1,0:T(8,128)(2,1)S(1)}, u32[]{:S(2)}, u32[]{:S(2)}) collective-permute-start(bf16[8,256,128]{2,1,0:T(8,128)(2,1)S(1)} %collective-permute-done.1.refs_4_), channel_id=1, source_target_pairs={{0,8},{8,0},{16,24},{24,16},{32,40},{40,32},{48,56},{56,48},{64,72... | collective-permute-start | bytes 1572872 | tf_op jit(solution)/shard_map/ppermute | solution.py:424
  62.0 8.3 %collective-permute-start.5 = (bf16[128,1024]{1,0:T(8,128)(2,1)S(1)}, bf16[128,1024]{1,0:T(8,128)(2,1)S(1)}, u32[]{:S(2)}, u32[]{:S(2)}) collective-permute-start(bf16[128,1024]{1,0:T(8,128)(2,1)S(1)} %get-tuple-element.52), channel_id=1, source_target_pairs={{0,2},{1,3},{2,0},{3,1},{4,6},{5,7},{6,4},{7,5},{8,14},{9,15},{10,... | collective-permute-start | bytes 786440 | tf_op jit(solution)/shard_map/ppermute | solution.py:428

commit v4 on v3

--- a/solution.py
+++ b/solution.py
@@ -40,13 +40,13 @@
     )
 
 
-def keys_kernel(place_in, offset_in, frequency, keys_in, values_in, payload, tables, place, offset, keys, values, sems):
-    copies = [
-        pltpu.make_async_copy(source, target, sems.at[i])
-        for i, (source, target) in enumerate(
-            ((place_in, place), (offset_in, offset), (keys_in, keys), (values_in, values))
-        )
-    ]
+def keys_kernel(*refs):
+    place_in, offset_in, frequency, keys_in, values_in, queries_in = refs[:6]
+    payload, tables, other, place, offset, keys, values, queries, sems = refs[6:]
+    group = 1 - lax.axis_index("uly") // 2 % 2
+    queries_in = queries_in.at[:, pl.ds(pl.multiple_of(group * WIDTH, WIDTH), WIDTH)]
+    pairs = (place_in, place), (offset_in, offset), (keys_in, keys), (values_in, values), (queries_in, queries)
+    copies = [pltpu.make_async_copy(source, target, sems.at[i]) for i, (source, target) in enumerate(pairs)]
     for copy in copies:
         copy.start()
     copies[0].wait()
@@ -71,6 +71,11 @@
             for half in range(2):
                 payload[2 * x + half, :ROWS, :] = turned
                 payload[2 * x + half, ROWS:, :] = across
+    copies[4].wait()
+    for head in range(HEADS_PER_GROUP):
+        cols = slice(head * ROWS, (head + 1) * ROWS)
+        turned = rotate(queries[:, cols].astype(jnp.float32), cosine, minus, plus).astype(jnp.bfloat16)
+        other[:, cols] = turned.astype(jnp.float32).T.astype(jnp.bfloat16)
 
 
 def split_queries(x, odd, tip):
@@ -85,13 +90,6 @@
     start = pl.multiple_of(group * WIDTH + head * HEAD_DIM, HEAD_DIM)
     x = queries[:, pl.ds(start, HEAD_DIM)].astype(jnp.float32)
     return rotate(x, tables[0], tables[1], tables[2]).astype(jnp.bfloat16).astype(jnp.float32).T
-
-
-def other_queries_kernel(queries, tables, other):
-    group = 1 - lax.axis_index("uly") // 2 % 2
-    for head in range(HEADS_PER_GROUP):
-        cols = slice(head * ROWS, (head + 1) * ROWS)
-        other[:, cols] = turn_queries(queries, tables, group, head).astype(jnp.bfloat16)
 
 
 def own_queries_kernel(queries, tables, all_segments, own, odds, segments, sem):
@@ -318,7 +316,7 @@
         copy.wait()
 
 
-def attend(name, classes, segments, odds, sets, splits, blocks=None, laid=(), state=None, keep=True, final=False):
+def attend(name, classes, segments, odds, sets, splits, blocks=None, laid=(), state=None, final=False):
     roles = tuple(blocks) if blocks else tuple(role for group in laid for role in group[0])
     count, number = len(sets), len(roles)
     start = state is None
@@ -333,10 +331,9 @@
     else:
         shapes += [jax.ShapeDtypeStruct(state_shape, jnp.float32)] * count
         laid_out = [jax.ShapeDtypeStruct(shape, jnp.bfloat16) for shape in laid_shapes] if blocks else []
-        if start or not keep:
+        if start:
             scratch += [pltpu.VMEM(shape, jnp.bfloat16) for shape in laid_shapes]
             laid_out = []
-        if start:
             shapes.append(jax.ShapeDtypeStruct(split_shape, jnp.bfloat16))
             scratch.append(pltpu.VMEM((count, BLOCK, ROWS), jnp.float32))
     shapes += laid_out
@@ -363,32 +360,28 @@
 
 def shards(queries, key_rows, value_rows, span_place, span_offset, segment_number, block_class):
     vmem, hbm = pl.BlockSpec(memory_space=pltpu.VMEM), pl.BlockSpec(memory_space=pl.ANY)
-    payload, tables = pl.pallas_call(
+    payload, tables, q_other = pl.pallas_call(
         keys_kernel,
         out_shape=[
             jax.ShapeDtypeStruct((SHARDS, 2 * ROWS, HEAD_DIM), jnp.bfloat16),
             jax.ShapeDtypeStruct((3, ROWS, HEAD_DIM), jnp.float32),
+            jax.ShapeDtypeStruct((HEAD_DIM, WIDTH), jnp.bfloat16),
         ],
-        in_specs=[hbm, hbm, vmem, hbm, hbm],
-        out_specs=[vmem, vmem],
+        in_specs=[hbm, hbm, vmem, hbm, hbm, hbm],
+        out_specs=[vmem, vmem, vmem],
         scratch_shapes=[
             pltpu.VMEM((1, ROWS), jnp.int32),
             pltpu.VMEM((1, ROWS), jnp.int32),
             pltpu.VMEM((ROWS, 2 * HEAD_DIM), jnp.bfloat16),
             pltpu.VMEM((ROWS, 2 * HEAD_DIM), jnp.bfloat16),
-            pltpu.SemaphoreType.DMA((4,)),
+            pltpu.VMEM((ROWS, WIDTH), jnp.bfloat16),
+            pltpu.SemaphoreType.DMA((5,)),
         ],
         compiler_params=pltpu.CompilerParams(vmem_limit_bytes=KEYS_VMEM),
         name="rotate_keys",
-    )(span_place[None, :], span_offset[None, :], lane_frequencies(), key_rows, value_rows)
+    )(span_place[None, :], span_offset[None, :], lane_frequencies(), key_rows, value_rows, queries)
     own = lax.all_to_all(payload, "uly", split_axis=0, concat_axis=0, tiled=True)
 
-    q_other = pl.pallas_call(
-        other_queries_kernel,
-        out_shape=jax.ShapeDtypeStruct((HEAD_DIM, WIDTH), jnp.bfloat16),
-        compiler_params=VMEM,
-        name="rotate_other_queries",
-    )(queries, tables)
     every = [(b, u) for b in range(BLOCKS) for u in range(SHARDS)]
     partners = [(b * SHARDS + u, b * SHARDS + partner_of(b, u)) for b, u in every]
     q_partner = lax.ppermute(q_other, ("blk", "uly"), partners)
@@ -419,12 +412,11 @@
     run = functools.partial(attend, classes=block_class, segments=segments, odds=odds)
     both = (True, False)
     splits, state, _, _ = run("attend_own", sets=both, splits=(q_partner, split_own), blocks={"own": own})
-    _, state, _, _ = run("attend_near", sets=both, splits=splits, state=state, blocks={"near": near}, keep=False)
     far, state = lax.optimization_barrier((far, state))
     late = lax.ppermute(far, "blk", cores)
     theirs = functools.partial(run, sets=both[:1], splits=splits[:1])
-    _, passed, laid, _ = theirs("attend_far", state=state[:1], blocks={"far": far, "back": back})
-    _, _, rest, to_send = theirs("attend_partner", state=passed, blocks={"late": late}, final=True)
+    _, passed, laid, _ = theirs("attend_near", state=state[:1], blocks={"near": near, "far": far})
+    _, _, rest, to_send = theirs("attend_partner", state=passed, blocks={"late": late, "back": back}, final=True)
     others = lax.ppermute(to_send, ("blk", "uly"), partners)
     mine = run("attend_rest", sets=both[1:], splits=splits[1:], state=state[1:], laid=(laid, rest), final=True)[3]
     return pl.pallas_call(

time: 72 us -> 71.8 us (level)
  waiting for transfers between devices: 17.9 us -> 19.5 us
  Pallas kernels: 20.8 us -> 19.3 us
    ppermute x1, waiting for transfers between devices: 2.24 us -> 4.48 us  [shards(): far = lax.ppermute(own, 'blk', ahead)]
    pallas_call x5 -> x4, Pallas kernels: 15.2 us -> 13.8 us  [attend(): pl.pallas_call(functools.partial(attend_kernel, sets, roles, len(laid), s...]
    all_to_all x1, waiting for transfers between devices: 9.12 us -> 10.3 us  [shards(): lax.all_to_all(payload, 'uly', split_axis=0, concat_axis=0, tiled=True)]
    ppermute x1, waiting for transfers between devices: 2.73 us -> 1.89 us  [shards(): others = lax.ppermute(to_send, ('blk', 'uly'), partners)]
  transfers between devices with their start and end apart: 7 -> 7, of which waited for: 5 -> 4; matrix products, arithmetic and copies ran while one was open for 0% -> 0% of each run, Pallas kernels for 21% -> 17%
where the time goes in v4:
time: 71.8 us; the launch traced here: 71.1 us
  starting transfers between devices  31.1 us (43%)
  waiting for transfers between devices  19.5 us (27%)
  Pallas kernels  19.3 us (27%)
  local copies, waits for them, and re-layouts  0.93 us (1%)
    pallas_call x4, Pallas kernels, attend(): pl.pallas_call(functools.partial(attend_kernel, sets, roles, len(laid), s...  13.8 us
    ppermute x1, starting transfers between devices, shards(): far = lax.ppermute(own, 'blk', ahead)  11.7 us
    all_to_all x1, waiting for transfers between devices, shards(): lax.all_to_all(payload, 'uly', split_axis=0, concat_axis=0, tiled=True)  10.3 us
    all_to_all x1, starting transfers between devices, shards(): lax.all_to_all(payload, 'uly', split_axis=0, concat_axis=0, tiled=True)  7.78 us
    ppermute x1, waiting for transfers between devices, shards(): far = lax.ppermute(own, 'blk', ahead)  4.48 us
    ppermute x1, starting transfers between devices, shards(): q_partner = lax.ppermute(q_other, ('blk', 'uly'), partners)  3.92 us
    pallas_call x1, Pallas kernels, shards(): pl.pallas_call(keys_kernel, out_shape=[jax.ShapeDtypeStruct((SHARDS, 2 *...  3.04 us
    ppermute x1, waiting for transfers between devices, shards(): q_partner = lax.ppermute(q_other, ('blk', 'uly'), partners)  2.85 us
  transfers between devices with their start and end apart: 7, of which 4 were waited for; matrix products, arithmetic and copies ran while one was open for 0% of the time, Pallas kernels for 17%

profile of v4, /device:TPU:16, one launch (start us, length us, event | category | flops | bytes accessed | tf_op | source)
XLA Modules:
  0.0 71.1 jit_solution(15598921529242877510)
XLA Ops:
  0.0 0.0 copy-start
  0.0 0.0 copy-start.1
  0.0 0.0 copy-start.3
  0.0 3.0 %rotate_keys.1 = (bf16[8,256,128]{2,1,0:T(8,128)(2,1)}, f32[3,128,128]{2,1,0:T(8,128)}, bf16[128,1024]{1,0:T(8,128)(2,1)}) custom-call(s32[1,128]{1,0:T(1,128)} %bitcast.4, s32[1,128]{1,0:T(1,128)} %bitcast.5, f32[1,128]{1,0:T(1,128)} %constant.2.clone.refs_2_, bf16[128,256]{1,0:T(8,128)(2,1)} %refs_3_.1, bf16[128,256]{1,0:T(8,128)(2,1)} %refs_4_.1, ...), custom_call_target="tpu_custom_call" | custom-call | tf_op jit(solution)/shard_map/rotate_keys/pallas_call | solution.py:363
  3.1 7.8 %all-to-all-start = ((bf16[8,256,128]{2,1,0:T(8,128)(2,1)}), bf16[8,256,128]{2,1,0:T(8,128)(2,1)S(1)}, u32[]{:S(2)}, u32[]{:S(2)}) async-start(bf16[8,256,128]{2,1,0:T(8,128)(2,1)} %get-tuple-element.28), calls=%async_computation | async-start | bytes 1048576 | tf_op jit(solution)/shard_map/all_to_all | solution.py:383
  10.8 3.9 %collective-permute-start = (bf16[128,1024]{1,0:T(8,128)(2,1)}, bf16[128,1024]{1,0:T(8,128)(2,1)S(1)}, u32[]{:S(2)}, u32[]{:S(2)}) collective-permute-start(bf16[128,1024]{1,0:T(8,128)(2,1)} %get-tuple-element.31), channel_id=1, source_target_pairs={{0,2},{1,3},{2,0},{3,1},{4,6},{5,7},{6,4},{7,5},{8,14},{9,15},{10,... | collective-permute-start | bytes 786440 | tf_op jit(solution)/shard_map/ppermute | solution.py:387
  14.8 0.0 copy-done
  14.8 0.0 copy-done.1
  14.8 0.0 copy-start.2
  14.8 0.9 %copy-done.2 = f32[3,128,128]{2,1,0:T(8,128)S(1)} copy-done((f32[3,128,128]{2,1,0:T(8,128)S(1)}, f32[3,128,128]{2,1,0:T(8,128)}, u32[]{:S(2)}) %copy-start.2) | copy-done | bytes 196632
  15.7 1.6 %rotate_own_queries.1 = (bf16[256,1024]{1,0:T(8,128)(2,1)S(1)}, bf16[5120,128]{1,0:T(8,128)(2,1)S(1)}, s32[40,1,128]{2,1,0:T(1,128)S(1)}) custom-call(bf16[128,2048]{1,0:T(8,128)(2,1)S(1)} %copy-done, f32[3,128,128]{2,1,0:T(8,128)S(1)} %copy-done.2, s32[512,1,128]{2,1,0:T(1,128)S(1)} %bitcast.3), custom_call_target="tpu_custom_call" | custom-call | tf_op jit(solution)/shard_map/rotate_own_queries/pallas_call | solution.py:388
  17.3 2.8 %collective-permute-done.refs_3_ = bf16[128,1024]{1,0:T(8,128)(2,1)S(1)} collective-permute-done((bf16[128,1024]{1,0:T(8,128)(2,1)}, bf16[128,1024]{1,0:T(8,128)(2,1)S(1)}, u32[]{:S(2)}, u32[]{:S(2)}) %collective-permute-start) | collective-permute-done | bytes 262176 | tf_op jit(solution)/shard_map/ppermute | solution.py:387
  20.2 10.3 %all-to-all-done.refs_5_ = bf16[8,256,128]{2,1,0:T(8,128)(2,1)S(1)} async-done(((bf16[8,256,128]{2,1,0:T(8,128)(2,1)}), bf16[8,256,128]{2,1,0:T(8,128)(2,1)S(1)}, u32[]{:S(2)}, u32[]{:S(2)}) %all-to-all-start) | async-done | bytes 524320 | tf_op jit(solution)/shard_map/all_to_all | solution.py:383
  30.4 11.7 %collective-permute-start.2 = (bf16[8,256,128]{2,1,0:T(8,128)(2,1)S(1)}, bf16[8,256,128]{2,1,0:T(8,128)(2,1)S(1)}, u32[]{:S(2)}, u32[]{:S(2)}) collective-permute-start(bf16[8,256,128]{2,1,0:T(8,128)(2,1)S(1)} %all-to-all-done.refs_5_), channel_id=1, source_target_pairs={{16,0},{32,16},{8,24},{48,32},{24,40},{64,48},{40,56},{80,64},{56,... | collective-permute-start | bytes 1572872 | tf_op jit(solution)/shard_map/ppermute | solution.py:408
  42.2 1.9 %collective-permute-start.4 = (bf16[8,256,128]{2,1,0:T(8,128)(2,1)S(1)}, bf16[8,256,128]{2,1,0:T(8,128)(2,1)S(1)}, u32[]{:S(2)}, u32[]{:S(2)}) collective-permute-start(bf16[8,256,128]{2,1,0:T(8,128)(2,1)S(1)} %all-to-all-done.refs_5_), channel_id=1, source_target_pairs={{24,8},{0,16},{40,24},{16,32},{56,40},{32,48},{72,56},{48,64},{88,... | collective-permute-start | bytes 1572872 | tf_op jit(solution)/shard_map/ppermute | solution.py:409
  44.1 1.9 %collective-permute-start.1 = (bf16[8,256,128]{2,1,0:T(8,128)(2,1)S(1)}, bf16[8,256,128]{2,1,0:T(8,128)(2,1)S(1)}, u32[]{:S(2)}, u32[]{:S(2)}) collective-permute-start(bf16[8,256,128]{2,1,0:T(8,128)(2,1)S(1)} %all-to-all-done.refs_5_), channel_id=1, source_target_pairs={{0,8},{8,0},{16,24},{24,16},{32,40},{40,32},{48,56},{56,48},{64,72... | collective-permute-start | bytes 1572872 | tf_op jit(solution)/shard_map/ppermute | solution.py:410
  46.0 0.0 copy-done.3
  46.0 3.2 %attend_own.1 = (f32[144,1024]{1,0:T(8,128)S(1)}, f32[144,1024]{1,0:T(8,128)S(1)}, bf16[256,1024]{1,0:T(8,128)(2,1)S(1)}) custom-call(s32[64]{0:T(128)S(1)} %copy-done.3, s32[40,1,128]{2,1,0:T(1,128)S(1)} %get-tuple-element.34.refs_1_, bf16[5120,128]{1,0:T(8,128)(2,1)S(1)} %get-tuple-element.35.refs_2_, bf16[128,1024]{1,0:T(8,128)(2,1)S(1)} %collective-permute-done.refs_3_, ...), custom_call_target="tpu_custom_call" | custom-call | flops 2147483648 | bytes 1048576 | tf_op jit(solution)/shard_map/attend_own/pallas_call | solution.py:343
  49.3 4.5 %collective-permute-done.2.refs_5_ = bf16[8,256,128]{2,1,0:T(8,128)(2,1)S(1)} collective-permute-done((bf16[8,256,128]{2,1,0:T(8,128)(2,1)S(1)}, bf16[8,256,128]{2,1,0:T(8,128)(2,1)S(1)}, u32[]{:S(2)}, u32[]{:S(2)}) %collective-permute-start.2) | collective-permute-done | bytes 524320 | tf_op jit(solution)/shard_map/ppermute | solution.py:408
  53.8 1.9 %collective-permute-start.3 = (bf16[8,256,128]{2,1,0:T(8,128)(2,1)S(1)}, bf16[8,256,128]{2,1,0:T(8,128)(2,1)S(1)}, u32[]{:S(2)}, u32[]{:S(2)}) collective-permute-start(bf16[8,256,128]{2,1,0:T(8,128)(2,1)S(1)} %collective-permute-done.2.refs_5_), channel_id=1, source_target_pairs={{0,8},{8,0},{16,24},{24,16},{32,40},{40,32},{48,56},{56,48},{64,72... | collective-permute-start | bytes 1572872 | tf_op jit(solution)/shard_map/ppermute | solution.py:416
  55.7 0.0 collective-permute-done.1.refs_4_
  55.7 3.1 %attend_near.1 = (f32[144,1024]{1,0:T(8,128)S(1)}, bf16[2,1024,256]{2,1,0:T(8,128)(2,1)S(1)}, bf16[2,128,1024]{2,1,0:T(8,128)(2,1)S(1)}) custom-call(s32[64]{0:T(128)S(1)} %copy-done.3, s32[40,1,128]{2,1,0:T(1,128)S(1)} %get-tuple-element.34.refs_1_, bf16[5120,128]{1,0:T(8,128)(2,1)S(1)} %get-tuple-element.35.refs_2_, ...), custom_call_target="tpu_custom_call" | custom-call | flops 2147483648 | bytes 1048576 | tf_op jit(solution)/shard_map/attend_near/pallas_call | solution.py:343
  58.8 0.0 collective-permute-done.4.refs_5_
  58.8 0.0 collective-permute-done.3.refs_4_
  58.8 3.1 %attend_partner.1 = (bf16[128,1024]{1,0:T(8,128)(2,1)S(1)}, bf16[2,1024,256]{2,1,0:T(8,128)(2,1)S(1)}, bf16[2,128,1024]{2,1,0:T(8,128)(2,1)S(1)}) custom-call(s32[64]{0:T(128)S(1)} %copy-done.3, s32[40,1,128]{2,1,0:T(1,128)S(1)} %get-tuple-element.34.refs_1_, bf16[5120,128]{1,0:T(8,128)(2,1)S(1)} %get-tuple-element.35.refs_2_, ...), custom_call_target="tpu_custom_call" | custom-call | flops 2147483648 | bytes 1048576 | tf_op jit(solution)/shard_map/attend_partner/pallas_call | solution.py:343
  61.9 1.9 %collective-permute-start.5 = (bf16[128,1024]{1,0:T(8,128)(2,1)S(1)}, bf16[128,1024]{1,0:T(8,128)(2,1)S(1)}, u32[]{:S(2)}, u32[]{:S(2)}) collective-permute-start(bf16[128,1024]{1,0:T(8,128)(2,1)S(1)} %get-tuple-element.50), channel_id=1, source_target_pairs={{0,2},{1,3},{2,0},{3,1},{4,6},{5,7},{6,4},{7,5},{8,14},{9,15},{10,... | collective-permute-start | bytes 786440 | tf_op jit(solution)/shard_map/ppermute | solution.py:420
  63.8 4.4 %attend_rest.1.mine = bf16[128,1024]{1,0:T(8,128)(2,1)S(1)} custom-call(s32[64]{0:T(128)S(1)} %copy-done.3, s32[40,1,128]{2,1,0:T(1,128)S(1)} %get-tuple-element.34.refs_1_, bf16[5120,128]{1,0:T(8,128)(2,1)S(1)} %get-tuple-element.35.refs_2_, bf16[2,1024,256]{2,1,0:T(8,128)(2,1)S(1)} %get-tuple-element.44.refs_3_, ...), custom_call_target="tpu_custom_call" | custom-call | flops 4294967296 | bytes 1048576 | tf_op jit(solution)/shard_map/attend_rest/pallas_call | solution.py:343
  68.2 1.9 %collective-permute-done.5.others = bf16[128,1024]{1,0:T(8,128)(2,1)S(1)} collective-permute-done((bf16[128,1024]{1,0:T(8,128)(2,1)S(1)}, bf16[128,1024]{1,0:T(8,128)(2,1)S(1)}, u32[]{:S(2)}, u32[]{:S(2)}) %collective-permute-start.5) | collective-permute-done | bytes 262176 | tf_op jit(solution)/shard_map/ppermute | solution.py:420
  70.1 0.8 %combine.1 = bf16[128,2048]{1,0:T(8,128)(2,1)} custom-call(bf16[128,1024]{1,0:T(8,128)(2,1)S(1)} %attend_rest.1.mine, bf16[128,1024]{1,0:T(8,128)(2,1)S(1)} %collective-permute-done.5.others), custom_call_target="tpu_custom_call" | custom-call | tf_op jit(solution)/shard_map/combine/pallas_call | solution.py:422
Async XLA Ops:
  0.0 14.8 %copy-start = (bf16[128,2048]{1,0:T(8,128)(2,1)S(1)}, bf16[128,2048]{1,0:T(8,128)(2,1)}, u32[]{:S(2)}) copy-start(bf16[128,2048]{1,0:T(8,128)(2,1)} %queries.1) | copy-start | bytes 1572868
  0.0 14.8 %copy-start.1 = (s32[65536]{0:T(1024)S(1)}, s32[65536]{0:T(1024)}, u32[]{:S(2)}) copy-start(s32[65536]{0:T(1024)} %param.13) | copy-start | bytes 786436
  0.0 46.0 %copy-start.3 = (s32[64]{0:T(128)S(1)}, s32[64]{0:T(128)}, u32[]{:S(2)}) copy-start(s32[64]{0:T(128)} %refs_0_.7) | copy-start | bytes 772
  3.1 27.4 %all-to-all-start = ((bf16[8,256,128]{2,1,0:T(8,128)(2,1)}), bf16[8,256,128]{2,1,0:T(8,128)(2,1)S(1)}, u32[]{:S(2)}, u32[]{:S(2)}) async-start(bf16[8,256,128]{2,1,0:T(8,128)(2,1)} %get-tuple-element.28), calls=%async_computation | async-start | bytes 1048576 | tf_op jit(solution)/shard_map/all_to_all | solution.py:383
  10.8 9.3 %collective-permute-start = (bf16[128,1024]{1,0:T(8,128)(2,1)}, bf16[128,1024]{1,0:T(8,128)(2,1)S(1)}, u32[]{:S(2)}, u32[]{:S(2)}) collective-permute-start(bf16[128,1024]{1,0:T(8,128)(2,1)} %get-tuple-element.31), channel_id=1, source_target_pairs={{0,2},{1,3},{2,0},{3,1},{4,6},{5,7},{6,4},{7,5},{8,14},{9,15},{10,... | collective-permute-start | bytes 786440 | tf_op jit(solution)/shard_map/ppermute | solution.py:387
  14.8 0.9 %copy-start.2 = (f32[3,128,128]{2,1,0:T(8,128)S(1)}, f32[3,128,128]{2,1,0:T(8,128)}, u32[]{:S(2)}) copy-start(f32[3,128,128]{2,1,0:T(8,128)} %get-tuple-element.29.tables) | copy-start | bytes 589828
  30.4 23.3 %collective-permute-start.2 = (bf16[8,256,128]{2,1,0:T(8,128)(2,1)S(1)}, bf16[8,256,128]{2,1,0:T(8,128)(2,1)S(1)}, u32[]{:S(2)}, u32[]{:S(2)}) collective-permute-start(bf16[8,256,128]{2,1,0:T(8,128)(2,1)S(1)} %all-to-all-done.refs_5_), channel_id=1, source_target_pairs={{16,0},{32,16},{8,24},{48,32},{24,40},{64,48},{40,56},{80,64},{56,... | collective-permute-start | bytes 1572872 | tf_op jit(solution)/shard_map/ppermute | solution.py:408
  42.2 16.6 %collective-permute-start.4 = (bf16[8,256,128]{2,1,0:T(8,128)(2,1)S(1)}, bf16[8,256,128]{2,1,0:T(8,128)(2,1)S(1)}, u32[]{:S(2)}, u32[]{:S(2)}) collective-permute-start(bf16[8,256,128]{2,1,0:T(8,128)(2,1)S(1)} %all-to-all-done.refs_5_), channel_id=1, source_target_pairs={{24,8},{0,16},{40,24},{16,32},{56,40},{32,48},{72,56},{48,64},{88,... | collective-permute-start | bytes 1572872 | tf_op jit(solution)/shard_map/ppermute | solution.py:409
  44.1 11.6 %collective-permute-start.1 = (bf16[8,256,128]{2,1,0:T(8,128)(2,1)S(1)}, bf16[8,256,128]{2,1,0:T(8,128)(2,1)S(1)}, u32[]{:S(2)}, u32[]{:S(2)}) collective-permute-start(bf16[8,256,128]{2,1,0:T(8,128)(2,1)S(1)} %all-to-all-done.refs_5_), channel_id=1, source_target_pairs={{0,8},{8,0},{16,24},{24,16},{32,40},{40,32},{48,56},{56,48},{64,72... | collective-permute-start | bytes 1572872 | tf_op jit(solution)/shard_map/ppermute | solution.py:410
  53.8 5.0 %collective-permute-start.3 = (bf16[8,256,128]{2,1,0:T(8,128)(2,1)S(1)}, bf16[8,256,128]{2,1,0:T(8,128)(2,1)S(1)}, u32[]{:S(2)}, u32[]{:S(2)}) collective-permute-start(bf16[8,256,128]{2,1,0:T(8,128)(2,1)S(1)} %collective-permute-done.2.refs_5_), channel_id=1, source_target_pairs={{0,8},{8,0},{16,24},{24,16},{32,40},{40,32},{48,56},{56,48},{64,72... | collective-permute-start | bytes 1572872 | tf_op jit(solution)/shard_map/ppermute | solution.py:416
  61.9 8.3 %collective-permute-start.5 = (bf16[128,1024]{1,0:T(8,128)(2,1)S(1)}, bf16[128,1024]{1,0:T(8,128)(2,1)S(1)}, u32[]{:S(2)}, u32[]{:S(2)}) collective-permute-start(bf16[128,1024]{1,0:T(8,128)(2,1)S(1)} %get-tuple-element.50), channel_id=1, source_target_pairs={{0,2},{1,3},{2,0},{3,1},{4,6},{5,7},{6,4},{7,5},{8,14},{9,15},{10,... | collective-permute-start | bytes 786440 | tf_op jit(solution)/shard_map/ppermute | solution.py:420

commit v5 on v4

--- a/solution.py
+++ b/solution.py
@@ -406,12 +406,13 @@
     behind = [(i - 2 + 4 * (i % 2), i) for i in within if i - 2 + 4 * (i % 2) in within]
     cores = [(i, i ^ 1) for i in within]
     far = lax.ppermute(own, "blk", ahead)
-    back = lax.ppermute(own, "blk", behind)
     near = lax.ppermute(own, "blk", cores)
 
     run = functools.partial(attend, classes=block_class, segments=segments, odds=odds)
     both = (True, False)
     splits, state, _, _ = run("attend_own", sets=both, splits=(q_partner, split_own), blocks={"own": own})
+    own, state = lax.optimization_barrier((own, state))
+    back = lax.ppermute(own, "blk", behind)
     far, state = lax.optimization_barrier((far, state))
     late = lax.ppermute(far, "blk", cores)
     theirs = functools.partial(run, sets=both[:1], splits=splits[:1])

time: 71.8 us -> 73.7 us (1.026)
  waiting for transfers between devices: 19.5 us -> 20.5 us
    ppermute x1, waiting for transfers between devices: 0.01 us -> 5.48 us  [shards(): back = lax.ppermute(own, 'blk', behind)]
    ppermute x1, waiting for transfers between devices: 4.48 us -> 0.01 us  [shards(): far = lax.ppermute(own, 'blk', ahead)]
    ppermute x1, starting transfers between devices: 1.91 us -> 2.67 us  [shards(): late = lax.ppermute(far, 'blk', cores)]
  transfers between devices with their start and end apart: 7 -> 7, of which waited for: 4 -> 4; matrix products, arithmetic and copies ran while one was open for 0% -> 0% of each run, Pallas kernels for 17% -> 18%
where the time goes in v5:
time: 73.7 us; the launch traced here: 73.3 us
  starting transfers between devices  31.8 us (43%)
  waiting for transfers between devices  20.5 us (28%)
  Pallas kernels  19.7 us (27%)
  local copies, waits for them, and re-layouts  0.93 us (1%)
    pallas_call x4, Pallas kernels, attend(): pl.pallas_call(functools.partial(attend_kernel, sets, roles, len(laid), s...  14.3 us
    ppermute x1, starting transfers between devices, shards(): far = lax.ppermute(own, 'blk', ahead)  11.7 us
    all_to_all x1, waiting for transfers between devices, shards(): lax.all_to_all(payload, 'uly', split_axis=0, concat_axis=0, tiled=True)  10.3 us
    all_to_all x1, starting transfers between devices, shards(): lax.all_to_all(payload, 'uly', split_axis=0, concat_axis=0, tiled=True)  7.78 us
    ppermute x1, waiting for transfers between devices, shards(): back = lax.ppermute(own, 'blk', behind)  5.48 us
    ppermute x1, starting transfers between devices, shards(): q_partner = lax.ppermute(q_other, ('blk', 'uly'), partners)  3.92 us
    pallas_call x1, Pallas kernels, shards(): pl.pallas_call(keys_kernel, out_shape=[jax.ShapeDtypeStruct((SHARDS, 2 *...  3.04 us
    ppermute x1, waiting for transfers between devices, shards(): q_partner = lax.ppermute(q_other, ('blk', 'uly'), partners)  2.85 us
  transfers between devices with their start and end apart: 7, of which 4 were waited for; matrix products, arithmetic and copies ran while one was open for 0% of the time, Pallas kernels for 18%

profile of v5, /device:TPU:16, one launch (start us, length us, event | category | flops | bytes accessed | tf_op | source)
XLA Modules:
  0.0 73.3 jit_solution(3281610362109729200)
XLA Ops:
  0.0 0.0 copy-start
  0.0 0.0 copy-start.1
  0.0 0.0 copy-start.3
  0.0 3.0 %rotate_keys.1 = (bf16[8,256,128]{2,1,0:T(8,128)(2,1)}, f32[3,128,128]{2,1,0:T(8,128)}, bf16[128,1024]{1,0:T(8,128)(2,1)}) custom-call(s32[1,128]{1,0:T(1,128)} %bitcast.4, s32[1,128]{1,0:T(1,128)} %bitcast.5, f32[1,128]{1,0:T(1,128)} %constant.2.clone.refs_2_, bf16[128,256]{1,0:T(8,128)(2,1)} %refs_3_.1, bf16[128,256]{1,0:T(8,128)(2,1)} %refs_4_.1, ...), custom_call_target="tpu_custom_call" | custom-call | tf_op jit(solution)/shard_map/rotate_keys/pallas_call | solution.py:363
  3.1 7.8 %all-to-all-start = ((bf16[8,256,128]{2,1,0:T(8,128)(2,1)}), bf16[8,256,128]{2,1,0:T(8,128)(2,1)S(1)}, u32[]{:S(2)}, u32[]{:S(2)}) async-start(bf16[8,256,128]{2,1,0:T(8,128)(2,1)} %get-tuple-element.31), calls=%async_computation | async-start | bytes 1048576 | tf_op jit(solution)/shard_map/all_to_all | solution.py:383
  10.8 3.9 %collective-permute-start = (bf16[128,1024]{1,0:T(8,128)(2,1)}, bf16[128,1024]{1,0:T(8,128)(2,1)S(1)}, u32[]{:S(2)}, u32[]{:S(2)}) collective-permute-start(bf16[128,1024]{1,0:T(8,128)(2,1)} %get-tuple-element.34), channel_id=1, source_target_pairs={{0,2},{1,3},{2,0},{3,1},{4,6},{5,7},{6,4},{7,5},{8,14},{9,15},{10,... | collective-permute-start | bytes 786440 | tf_op jit(solution)/shard_map/ppermute | solution.py:387
  14.8 0.0 copy-done
  14.8 0.0 copy-done.1
  14.8 0.0 copy-start.2
  14.8 0.9 %copy-done.2 = f32[3,128,128]{2,1,0:T(8,128)S(1)} copy-done((f32[3,128,128]{2,1,0:T(8,128)S(1)}, f32[3,128,128]{2,1,0:T(8,128)}, u32[]{:S(2)}) %copy-start.2) | copy-done | bytes 196632
  15.7 1.6 %rotate_own_queries.1 = (bf16[256,1024]{1,0:T(8,128)(2,1)S(1)}, bf16[5120,128]{1,0:T(8,128)(2,1)S(1)}, s32[40,1,128]{2,1,0:T(1,128)S(1)}) custom-call(bf16[128,2048]{1,0:T(8,128)(2,1)S(1)} %copy-done, f32[3,128,128]{2,1,0:T(8,128)S(1)} %copy-done.2, s32[512,1,128]{2,1,0:T(1,128)S(1)} %bitcast.3), custom_call_target="tpu_custom_call" | custom-call | tf_op jit(solution)/shard_map/rotate_own_queries/pallas_call | solution.py:388
  17.3 2.8 %collective-permute-done.refs_3_ = bf16[128,1024]{1,0:T(8,128)(2,1)S(1)} collective-permute-done((bf16[128,1024]{1,0:T(8,128)(2,1)}, bf16[128,1024]{1,0:T(8,128)(2,1)S(1)}, u32[]{:S(2)}, u32[]{:S(2)}) %collective-permute-start) | collective-permute-done | bytes 262176 | tf_op jit(solution)/shard_map/ppermute | solution.py:387
  20.2 10.3 %all-to-all-done.refs_5_ = bf16[8,256,128]{2,1,0:T(8,128)(2,1)S(1)} async-done(((bf16[8,256,128]{2,1,0:T(8,128)(2,1)}), bf16[8,256,128]{2,1,0:T(8,128)(2,1)S(1)}, u32[]{:S(2)}, u32[]{:S(2)}) %all-to-all-start) | async-done | bytes 524320 | tf_op jit(solution)/shard_map/all_to_all | solution.py:383
  30.4 11.7 %collective-permute-start.2 = (bf16[8,256,128]{2,1,0:T(8,128)(2,1)S(1)}, bf16[8,256,128]{2,1,0:T(8,128)(2,1)S(1)}, u32[]{:S(2)}, u32[]{:S(2)}) collective-permute-start(bf16[8,256,128]{2,1,0:T(8,128)(2,1)S(1)} %all-to-all-done.refs_5_), channel_id=1, source_target_pairs={{16,0},{32,16},{8,24},{48,32},{24,40},{64,48},{40,56},{80,64},{56,... | collective-permute-start | bytes 1572872 | tf_op jit(solution)/shard_map/ppermute | solution.py:408
  42.2 1.9 %collective-permute-start.1 = (bf16[8,256,128]{2,1,0:T(8,128)(2,1)S(1)}, bf16[8,256,128]{2,1,0:T(8,128)(2,1)S(1)}, u32[]{:S(2)}, u32[]{:S(2)}) collective-permute-start(bf16[8,256,128]{2,1,0:T(8,128)(2,1)S(1)} %all-to-all-done.refs_5_), channel_id=1, source_target_pairs={{0,8},{8,0},{16,24},{24,16},{32,40},{40,32},{48,56},{56,48},{64,72... | collective-permute-start | bytes 1572872 | tf_op jit(solution)/shard_map/ppermute | solution.py:409
  44.1 0.0 copy-done.3
  44.1 3.7 %attend_own.1 = (f32[144,1024]{1,0:T(8,128)S(1)}, f32[144,1024]{1,0:T(8,128)S(1)}, bf16[256,1024]{1,0:T(8,128)(2,1)S(1)}) custom-call(s32[64]{0:T(128)S(1)} %copy-done.3, s32[40,1,128]{2,1,0:T(1,128)S(1)} %get-tuple-element.37.refs_1_, bf16[5120,128]{1,0:T(8,128)(2,1)S(1)} %get-tuple-element.38.refs_2_, bf16[128,1024]{1,0:T(8,128)(2,1)S(1)} %collective-permute-done.refs_3_, ...), custom_call_target="tpu_custom_call" | custom-call | flops 2147483648 | bytes 1048576 | tf_op jit(solution)/shard_map/attend_own/pallas_call | solution.py:343
  47.9 1.9 %collective-permute-start.4 = (bf16[8,256,128]{2,1,0:T(8,128)(2,1)S(1)}, bf16[8,256,128]{2,1,0:T(8,128)(2,1)S(1)}, u32[]{:S(2)}, u32[]{:S(2)}) collective-permute-start(bf16[8,256,128]{2,1,0:T(8,128)(2,1)S(1)} %all-to-all-done.refs_5_), channel_id=1, source_target_pairs={{24,8},{0,16},{40,24},{16,32},{56,40},{32,48},{72,56},{48,64},{88,... | collective-permute-start | bytes 1572872 | tf_op jit(solution)/shard_map/ppermute | solution.py:415
  49.8 0.0 collective-permute-done.2.refs_5_
  49.8 2.7 %collective-permute-start.3 = (bf16[8,256,128]{2,1,0:T(8,128)(2,1)S(1)}, bf16[8,256,128]{2,1,0:T(8,128)(2,1)S(1)}, u32[]{:S(2)}, u32[]{:S(2)}) collective-permute-start(bf16[8,256,128]{2,1,0:T(8,128)(2,1)S(1)} %collective-permute-done.2.refs_5_), channel_id=1, source_target_pairs={{0,8},{8,0},{16,24},{24,16},{32,40},{40,32},{48,56},{56,48},{64,72... | collective-permute-start | bytes 1572872 | tf_op jit(solution)/shard_map/ppermute | solution.py:417
  52.5 0.0 collective-permute-done.1.refs_4_
  52.5 3.1 %attend_near.1 = (f32[144,1024]{1,0:T(8,128)S(1)}, bf16[2,1024,256]{2,1,0:T(8,128)(2,1)S(1)}, bf16[2,128,1024]{2,1,0:T(8,128)(2,1)S(1)}) custom-call(s32[64]{0:T(128)S(1)} %copy-done.3, s32[40,1,128]{2,1,0:T(1,128)S(1)} %get-tuple-element.37.refs_1_, bf16[5120,128]{1,0:T(8,128)(2,1)S(1)} %get-tuple-element.38.refs_2_, ...), custom_call_target="tpu_custom_call" | custom-call | flops 2147483648 | bytes 1048576 | tf_op jit(solution)/shard_map/attend_near/pallas_call | solution.py:343
  55.6 5.5 %collective-permute-done.4.refs_5_ = bf16[8,256,128]{2,1,0:T(8,128)(2,1)S(1)} collective-permute-done((bf16[8,256,128]{2,1,0:T(8,128)(2,1)S(1)}, bf16[8,256,128]{2,1,0:T(8,128)(2,1)S(1)}, u32[]{:S(2)}, u32[]{:S(2)}) %collective-permute-start.4) | collective-permute-done | bytes 524320 | tf_op jit(solution)/shard_map/ppermute | solution.py:415
  61.0 0.0 collective-permute-done.3.refs_4_
  61.0 3.0 %attend_partner.1 = (bf16[128,1024]{1,0:T(8,128)(2,1)S(1)}, bf16[2,1024,256]{2,1,0:T(8,128)(2,1)S(1)}, bf16[2,128,1024]{2,1,0:T(8,128)(2,1)S(1)}) custom-call(s32[64]{0:T(128)S(1)} %copy-done.3, s32[40,1,128]{2,1,0:T(1,128)S(1)} %get-tuple-element.37.refs_1_, bf16[5120,128]{1,0:T(8,128)(2,1)S(1)} %get-tuple-element.38.refs_2_, ...), custom_call_target="tpu_custom_call" | custom-call | flops 2147483648 | bytes 1048576 | tf_op jit(solution)/shard_map/attend_partner/pallas_call | solution.py:343
  64.1 1.9 %collective-permute-start.5 = (bf16[128,1024]{1,0:T(8,128)(2,1)S(1)}, bf16[128,1024]{1,0:T(8,128)(2,1)S(1)}, u32[]{:S(2)}, u32[]{:S(2)}) collective-permute-start(bf16[128,1024]{1,0:T(8,128)(2,1)S(1)} %get-tuple-element.56), channel_id=1, source_target_pairs={{0,2},{1,3},{2,0},{3,1},{4,6},{5,7},{6,4},{7,5},{8,14},{9,15},{10,... | collective-permute-start | bytes 786440 | tf_op jit(solution)/shard_map/ppermute | solution.py:421
  66.0 4.4 %attend_rest.1.mine = bf16[128,1024]{1,0:T(8,128)(2,1)S(1)} custom-call(s32[64]{0:T(128)S(1)} %copy-done.3, s32[40,1,128]{2,1,0:T(1,128)S(1)} %get-tuple-element.37.refs_1_, bf16[5120,128]{1,0:T(8,128)(2,1)S(1)} %get-tuple-element.38.refs_2_, bf16[2,1024,256]{2,1,0:T(8,128)(2,1)S(1)} %get-tuple-element.49.refs_3_, ...), custom_call_target="tpu_custom_call" | custom-call | flops 4294967296 | bytes 1048576 | tf_op jit(solution)/shard_map/attend_rest/pallas_call | solution.py:343
  70.4 1.9 %collective-permute-done.5.others = bf16[128,1024]{1,0:T(8,128)(2,1)S(1)} collective-permute-done((bf16[128,1024]{1,0:T(8,128)(2,1)S(1)}, bf16[128,1024]{1,0:T(8,128)(2,1)S(1)}, u32[]{:S(2)}, u32[]{:S(2)}) %collective-permute-start.5) | collective-permute-done | bytes 262176 | tf_op jit(solution)/shard_map/ppermute | solution.py:421
  72.4 0.8 %combine.1 = bf16[128,2048]{1,0:T(8,128)(2,1)} custom-call(bf16[128,1024]{1,0:T(8,128)(2,1)S(1)} %attend_rest.1.mine, bf16[128,1024]{1,0:T(8,128)(2,1)S(1)} %collective-permute-done.5.others), custom_call_target="tpu_custom_call" | custom-call | tf_op jit(solution)/shard_map/combine/pallas_call | solution.py:423
Async XLA Ops:
  0.0 14.8 %copy-start = (bf16[128,2048]{1,0:T(8,128)(2,1)S(1)}, bf16[128,2048]{1,0:T(8,128)(2,1)}, u32[]{:S(2)}) copy-start(bf16[128,2048]{1,0:T(8,128)(2,1)} %queries.1) | copy-start | bytes 1572868
  0.0 14.8 %copy-start.1 = (s32[65536]{0:T(1024)S(1)}, s32[65536]{0:T(1024)}, u32[]{:S(2)}) copy-start(s32[65536]{0:T(1024)} %param.13) | copy-start | bytes 786436
  0.0 44.1 %copy-start.3 = (s32[64]{0:T(128)S(1)}, s32[64]{0:T(128)}, u32[]{:S(2)}) copy-start(s32[64]{0:T(128)} %refs_0_.7) | copy-start | bytes 772
  3.1 27.4 %all-to-all-start = ((bf16[8,256,128]{2,1,0:T(8,128)(2,1)}), bf16[8,256,128]{2,1,0:T(8,128)(2,1)S(1)}, u32[]{:S(2)}, u32[]{:S(2)}) async-start(bf16[8,256,128]{2,1,0:T(8,128)(2,1)} %get-tuple-element.31), calls=%async_computation | async-start | bytes 1048576 | tf_op jit(solution)/shard_map/all_to_all | solution.py:383
  10.8 9.3 %collective-permute-start = (bf16[128,1024]{1,0:T(8,128)(2,1)}, bf16[128,1024]{1,0:T(8,128)(2,1)S(1)}, u32[]{:S(2)}, u32[]{:S(2)}) collective-permute-start(bf16[128,1024]{1,0:T(8,128)(2,1)} %get-tuple-element.34), channel_id=1, source_target_pairs={{0,2},{1,3},{2,0},{3,1},{4,6},{5,7},{6,4},{7,5},{8,14},{9,15},{10,... | collective-permute-start | bytes 786440 | tf_op jit(solution)/shard_map/ppermute | solution.py:387
  14.8 0.9 %copy-start.2 = (f32[3,128,128]{2,1,0:T(8,128)S(1)}, f32[3,128,128]{2,1,0:T(8,128)}, u32[]{:S(2)}) copy-start(f32[3,128,128]{2,1,0:T(8,128)} %get-tuple-element.32.tables) | copy-start | bytes 589828
  30.4 19.3 %collective-permute-start.2 = (bf16[8,256,128]{2,1,0:T(8,128)(2,1)S(1)}, bf16[8,256,128]{2,1,0:T(8,128)(2,1)S(1)}, u32[]{:S(2)}, u32[]{:S(2)}) collective-permute-start(bf16[8,256,128]{2,1,0:T(8,128)(2,1)S(1)} %all-to-all-done.refs_5_), channel_id=1, source_target_pairs={{16,0},{32,16},{8,24},{48,32},{24,40},{64,48},{40,56},{80,64},{56,... | collective-permute-start | bytes 1572872 | tf_op jit(solution)/shard_map/ppermute | solution.py:408
  42.2 10.3 %collective-permute-start.1 = (bf16[8,256,128]{2,1,0:T(8,128)(2,1)S(1)}, bf16[8,256,128]{2,1,0:T(8,128)(2,1)S(1)}, u32[]{:S(2)}, u32[]{:S(2)}) collective-permute-start(bf16[8,256,128]{2,1,0:T(8,128)(2,1)S(1)} %all-to-all-done.refs_5_), channel_id=1, source_target_pairs={{0,8},{8,0},{16,24},{24,16},{32,40},{40,32},{48,56},{56,48},{64,72... | collective-permute-start | bytes 1572872 | tf_op jit(solution)/shard_map/ppermute | solution.py:409
  47.9 13.2 %collective-permute-start.4 = (bf16[8,256,128]{2,1,0:T(8,128)(2,1)S(1)}, bf16[8,256,128]{2,1,0:T(8,128)(2,1)S(1)}, u32[]{:S(2)}, u32[]{:S(2)}) collective-permute-start(bf16[8,256,128]{2,1,0:T(8,128)(2,1)S(1)} %all-to-all-done.refs_5_), channel_id=1, source_target_pairs={{24,8},{0,16},{40,24},{16,32},{56,40},{32,48},{72,56},{48,64},{88,... | collective-permute-start | bytes 1572872 | tf_op jit(solution)/shard_map/ppermute | solution.py:415
  49.8 11.2 %collective-permute-start.3 = (bf16[8,256,128]{2,1,0:T(8,128)(2,1)S(1)}, bf16[8,256,128]{2,1,0:T(8,128)(2,1)S(1)}, u32[]{:S(2)}, u32[]{:S(2)}) collective-permute-start(bf16[8,256,128]{2,1,0:T(8,128)(2,1)S(1)} %collective-permute-done.2.refs_5_), channel_id=1, source_target_pairs={{0,8},{8,0},{16,24},{24,16},{32,40},{40,32},{48,56},{56,48},{64,72... | collective-permute-start | bytes 1572872 | tf_op jit(solution)/shard_map/ppermute | solution.py:417
  64.1 8.3 %collective-permute-start.5 = (bf16[128,1024]{1,0:T(8,128)(2,1)S(1)}, bf16[128,1024]{1,0:T(8,128)(2,1)S(1)}, u32[]{:S(2)}, u32[]{:S(2)}) collective-permute-start(bf16[128,1024]{1,0:T(8,128)(2,1)S(1)} %get-tuple-element.56), channel_id=1, source_target_pairs={{0,2},{1,3},{2,0},{3,1},{4,6},{5,7},{6,4},{7,5},{8,14},{9,15},{10,... | collective-permute-start | bytes 786440 | tf_op jit(solution)/shard_map/ppermute | solution.py:421

commit v6 on v5

--- a/solution.py
+++ b/solution.py
@@ -406,13 +406,13 @@
     behind = [(i - 2 + 4 * (i % 2), i) for i in within if i - 2 + 4 * (i % 2) in within]
     cores = [(i, i ^ 1) for i in within]
     far = lax.ppermute(own, "blk", ahead)
-    near = lax.ppermute(own, "blk", cores)
 
     run = functools.partial(attend, classes=block_class, segments=segments, odds=odds)
     both = (True, False)
     splits, state, _, _ = run("attend_own", sets=both, splits=(q_partner, split_own), blocks={"own": own})
     own, state = lax.optimization_barrier((own, state))
     back = lax.ppermute(own, "blk", behind)
+    near = lax.ppermute(own, "blk", cores)
     far, state = lax.optimization_barrier((far, state))
     late = lax.ppermute(far, "blk", cores)
     theirs = functools.partial(run, sets=both[:1], splits=splits[:1])

time: 73.7 us -> 73.7 us (level)
  waiting for transfers between devices: 20.5 us -> 23.9 us
  Pallas kernels: 19.7 us -> 16.4 us
    pallas_call x4, Pallas kernels: 14.3 us -> 10.9 us  [attend(): pl.pallas_call(functools.partial(attend_kernel, sets, roles, len(laid), s...]
    ppermute x1, waiting for transfers between devices: 5.48 us -> 7.31 us  [shards(): back = lax.ppermute(own, 'blk', behind)]
    ppermute x1, waiting for transfers between devices: 1.93 us -> 3.45 us  [shards(): others = lax.ppermute(to_send, ('blk', 'uly'), partners)]
  transfers between devices with their start and end apart: 7 -> 7, of which waited for: 4 -> 4; matrix products, arithmetic and copies ran while one was open for 0% -> 0% of each run, Pallas kernels for 18% -> 13%
where the time goes in v6:
time: 73.7 us; the launch traced here: 73.3 us
  starting transfers between devices  31.8 us (43%)
  waiting for transfers between devices  23.9 us (32%)
  Pallas kernels  16.4 us (22%)
  local copies, waits for them, and re-layouts  0.93 us (1%)
    ppermute x1, starting transfers between devices, shards(): far = lax.ppermute(own, 'blk', ahead)  11.7 us
    pallas_call x4, Pallas kernels, attend(): pl.pallas_call(functools.partial(attend_kernel, sets, roles, len(laid), s...  10.9 us
    all_to_all x1, waiting for transfers between devices, shards(): lax.all_to_all(payload, 'uly', split_axis=0, concat_axis=0, tiled=True)  10.3 us
    all_to_all x1, starting transfers between devices, shards(): lax.all_to_all(payload, 'uly', split_axis=0, concat_axis=0, tiled=True)  7.78 us
    ppermute x1, waiting for transfers between devices, shards(): back = lax.ppermute(own, 'blk', behind)  7.31 us
    ppermute x1, starting transfers between devices, shards(): q_partner = lax.ppermute(q_other, ('blk', 'uly'), partners)  3.92 us
    ppermute x1, waiting for transfers between devices, shards(): others = lax.ppermute(to_send, ('blk', 'uly'), partners)  3.45 us
    pallas_call x1, Pallas kernels, shards(): pl.pallas_call(keys_kernel, out_shape=[jax.ShapeDtypeStruct((SHARDS, 2 *...  3.04 us
  transfers between devices with their start and end apart: 7, of which 4 were waited for; matrix products, arithmetic and copies ran while one was open for 0% of the time, Pallas kernels for 13%

profile of v6, /device:TPU:16, one launch (start us, length us, event | category | flops | bytes accessed | tf_op | source)
XLA Modules:
  0.0 73.3 jit_solution(2431051361153087146)
XLA Ops:
  0.0 0.0 copy-start
  0.0 0.0 copy-start.1
  0.0 0.0 copy-start.3
  0.0 3.0 %rotate_keys.1 = (bf16[8,256,128]{2,1,0:T(8,128)(2,1)}, f32[3,128,128]{2,1,0:T(8,128)}, bf16[128,1024]{1,0:T(8,128)(2,1)}) custom-call(s32[1,128]{1,0:T(1,128)} %bitcast.4, s32[1,128]{1,0:T(1,128)} %bitcast.5, f32[1,128]{1,0:T(1,128)} %constant.2.clone.refs_2_, bf16[128,256]{1,0:T(8,128)(2,1)} %refs_3_.1, bf16[128,256]{1,0:T(8,128)(2,1)} %refs_4_.1, ...), custom_call_target="tpu_custom_call" | custom-call | tf_op jit(solution)/shard_map/rotate_keys/pallas_call | solution.py:363
  3.1 7.8 %all-to-all-start = ((bf16[8,256,128]{2,1,0:T(8,128)(2,1)}), bf16[8,256,128]{2,1,0:T(8,128)(2,1)S(1)}, u32[]{:S(2)}, u32[]{:S(2)}) async-start(bf16[8,256,128]{2,1,0:T(8,128)(2,1)} %get-tuple-element.31), calls=%async_computation | async-start | bytes 1048576 | tf_op jit(solution)/shard_map/all_to_all | solution.py:383
  10.8 3.9 %collective-permute-start = (bf16[128,1024]{1,0:T(8,128)(2,1)}, bf16[128,1024]{1,0:T(8,128)(2,1)S(1)}, u32[]{:S(2)}, u32[]{:S(2)}) collective-permute-start(bf16[128,1024]{1,0:T(8,128)(2,1)} %get-tuple-element.34), channel_id=1, source_target_pairs={{0,2},{1,3},{2,0},{3,1},{4,6},{5,7},{6,4},{7,5},{8,14},{9,15},{10,... | collective-permute-start | bytes 786440 | tf_op jit(solution)/shard_map/ppermute | solution.py:387
  14.8 0.0 copy-done
  14.8 0.0 copy-done.1
  14.8 0.0 copy-start.2
  14.8 0.9 %copy-done.2 = f32[3,128,128]{2,1,0:T(8,128)S(1)} copy-done((f32[3,128,128]{2,1,0:T(8,128)S(1)}, f32[3,128,128]{2,1,0:T(8,128)}, u32[]{:S(2)}) %copy-start.2) | copy-done | bytes 196632
  15.7 1.6 %rotate_own_queries.1 = (bf16[256,1024]{1,0:T(8,128)(2,1)S(1)}, bf16[5120,128]{1,0:T(8,128)(2,1)S(1)}, s32[40,1,128]{2,1,0:T(1,128)S(1)}) custom-call(bf16[128,2048]{1,0:T(8,128)(2,1)S(1)} %copy-done, f32[3,128,128]{2,1,0:T(8,128)S(1)} %copy-done.2, s32[512,1,128]{2,1,0:T(1,128)S(1)} %bitcast.3), custom_call_target="tpu_custom_call" | custom-call | tf_op jit(solution)/shard_map/rotate_own_queries/pallas_call | solution.py:388
  17.3 2.8 %collective-permute-done.refs_3_ = bf16[128,1024]{1,0:T(8,128)(2,1)S(1)} collective-permute-done((bf16[128,1024]{1,0:T(8,128)(2,1)}, bf16[128,1024]{1,0:T(8,128)(2,1)S(1)}, u32[]{:S(2)}, u32[]{:S(2)}) %collective-permute-start) | collective-permute-done | bytes 262176 | tf_op jit(solution)/shard_map/ppermute | solution.py:387
  20.2 10.3 %all-to-all-done.refs_5_ = bf16[8,256,128]{2,1,0:T(8,128)(2,1)S(1)} async-done(((bf16[8,256,128]{2,1,0:T(8,128)(2,1)}), bf16[8,256,128]{2,1,0:T(8,128)(2,1)S(1)}, u32[]{:S(2)}, u32[]{:S(2)}) %all-to-all-start) | async-done | bytes 524320 | tf_op jit(solution)/shard_map/all_to_all | solution.py:383
  30.4 11.7 %collective-permute-start.2 = (bf16[8,256,128]{2,1,0:T(8,128)(2,1)S(1)}, bf16[8,256,128]{2,1,0:T(8,128)(2,1)S(1)}, u32[]{:S(2)}, u32[]{:S(2)}) collective-permute-start(bf16[8,256,128]{2,1,0:T(8,128)(2,1)S(1)} %all-to-all-done.refs_5_), channel_id=1, source_target_pairs={{16,0},{32,16},{8,24},{48,32},{24,40},{64,48},{40,56},{80,64},{56,... | collective-permute-start | bytes 1572872 | tf_op jit(solution)/shard_map/ppermute | solution.py:408
  42.2 0.0 copy-done.3
  42.2 3.8 %attend_own.1 = (f32[144,1024]{1,0:T(8,128)S(1)}, f32[144,1024]{1,0:T(8,128)S(1)}, bf16[256,1024]{1,0:T(8,128)(2,1)S(1)}) custom-call(s32[64]{0:T(128)S(1)} %copy-done.3, s32[40,1,128]{2,1,0:T(1,128)S(1)} %get-tuple-element.37.refs_1_, bf16[5120,128]{1,0:T(8,128)(2,1)S(1)} %get-tuple-element.38.refs_2_, bf16[128,1024]{1,0:T(8,128)(2,1)S(1)} %collective-permute-done.refs_3_, ...), custom_call_target="tpu_custom_call" | custom-call | flops 2147483648 | bytes 1048576 | tf_op jit(solution)/shard_map/attend_own/pallas_call | solution.py:343
  45.9 1.9 %collective-permute-start.1 = (bf16[8,256,128]{2,1,0:T(8,128)(2,1)S(1)}, bf16[8,256,128]{2,1,0:T(8,128)(2,1)S(1)}, u32[]{:S(2)}, u32[]{:S(2)}) collective-permute-start(bf16[8,256,128]{2,1,0:T(8,128)(2,1)S(1)} %all-to-all-done.refs_5_), channel_id=1, source_target_pairs={{0,8},{8,0},{16,24},{24,16},{32,40},{40,32},{48,56},{56,48},{64,72... | collective-permute-start | bytes 1572872 | tf_op jit(solution)/shard_map/ppermute | solution.py:415
  47.9 1.9 %collective-permute-start.4 = (bf16[8,256,128]{2,1,0:T(8,128)(2,1)S(1)}, bf16[8,256,128]{2,1,0:T(8,128)(2,1)S(1)}, u32[]{:S(2)}, u32[]{:S(2)}) collective-permute-start(bf16[8,256,128]{2,1,0:T(8,128)(2,1)S(1)} %all-to-all-done.refs_5_), channel_id=1, source_target_pairs={{24,8},{0,16},{40,24},{16,32},{56,40},{32,48},{72,56},{48,64},{88,... | collective-permute-start | bytes 1572872 | tf_op jit(solution)/shard_map/ppermute | solution.py:414
  49.8 0.0 collective-permute-done.2.refs_5_
  49.8 2.7 %collective-permute-start.3 = (bf16[8,256,128]{2,1,0:T(8,128)(2,1)S(1)}, bf16[8,256,128]{2,1,0:T(8,128)(2,1)S(1)}, u32[]{:S(2)}, u32[]{:S(2)}) collective-permute-start(bf16[8,256,128]{2,1,0:T(8,128)(2,1)S(1)} %collective-permute-done.2.refs_5_), channel_id=1, source_target_pairs={{0,8},{8,0},{16,24},{24,16},{32,40},{40,32},{48,56},{56,48},{64,72... | collective-permute-start | bytes 1572872 | tf_op jit(solution)/shard_map/ppermute | solution.py:417
  52.5 0.0 collective-permute-done.1.refs_4_
  52.5 1.2 %attend_near.1 = (f32[144,1024]{1,0:T(8,128)S(1)}, bf16[2,1024,256]{2,1,0:T(8,128)(2,1)S(1)}, bf16[2,128,1024]{2,1,0:T(8,128)(2,1)S(1)}) custom-call(s32[64]{0:T(128)S(1)} %copy-done.3, s32[40,1,128]{2,1,0:T(1,128)S(1)} %get-tuple-element.37.refs_1_, bf16[5120,128]{1,0:T(8,128)(2,1)S(1)} %get-tuple-element.38.refs_2_, ...), custom_call_target="tpu_custom_call" | custom-call | flops 2147483648 | bytes 1048576 | tf_op jit(solution)/shard_map/attend_near/pallas_call | solution.py:343
  53.8 7.3 %collective-permute-done.4.refs_5_ = bf16[8,256,128]{2,1,0:T(8,128)(2,1)S(1)} collective-permute-done((bf16[8,256,128]{2,1,0:T(8,128)(2,1)S(1)}, bf16[8,256,128]{2,1,0:T(8,128)(2,1)S(1)}, u32[]{:S(2)}, u32[]{:S(2)}) %collective-permute-start.4) | collective-permute-done | bytes 524320 | tf_op jit(solution)/shard_map/ppermute | solution.py:414
  61.1 0.0 collective-permute-done.3.refs_4_
  61.1 3.0 %attend_partner.1 = (bf16[128,1024]{1,0:T(8,128)(2,1)S(1)}, bf16[2,1024,256]{2,1,0:T(8,128)(2,1)S(1)}, bf16[2,128,1024]{2,1,0:T(8,128)(2,1)S(1)}) custom-call(s32[64]{0:T(128)S(1)} %copy-done.3, s32[40,1,128]{2,1,0:T(1,128)S(1)} %get-tuple-element.37.refs_1_, bf16[5120,128]{1,0:T(8,128)(2,1)S(1)} %get-tuple-element.38.refs_2_, ...), custom_call_target="tpu_custom_call" | custom-call | flops 2147483648 | bytes 1048576 | tf_op jit(solution)/shard_map/attend_partner/pallas_call | solution.py:343
  64.1 1.9 %collective-permute-start.5 = (bf16[128,1024]{1,0:T(8,128)(2,1)S(1)}, bf16[128,1024]{1,0:T(8,128)(2,1)S(1)}, u32[]{:S(2)}, u32[]{:S(2)}) collective-permute-start(bf16[128,1024]{1,0:T(8,128)(2,1)S(1)} %get-tuple-element.56), channel_id=1, source_target_pairs={{0,2},{1,3},{2,0},{3,1},{4,6},{5,7},{6,4},{7,5},{8,14},{9,15},{10,... | collective-permute-start | bytes 786440 | tf_op jit(solution)/shard_map/ppermute | solution.py:421
  66.0 2.9 %attend_rest.1.mine = bf16[128,1024]{1,0:T(8,128)(2,1)S(1)} custom-call(s32[64]{0:T(128)S(1)} %copy-done.3, s32[40,1,128]{2,1,0:T(1,128)S(1)} %get-tuple-element.37.refs_1_, bf16[5120,128]{1,0:T(8,128)(2,1)S(1)} %get-tuple-element.38.refs_2_, bf16[2,1024,256]{2,1,0:T(8,128)(2,1)S(1)} %get-tuple-element.50.refs_3_, ...), custom_call_target="tpu_custom_call" | custom-call | flops 4294967296 | bytes 1048576 | tf_op jit(solution)/shard_map/attend_rest/pallas_call | solution.py:343
  68.9 3.4 %collective-permute-done.5.others = bf16[128,1024]{1,0:T(8,128)(2,1)S(1)} collective-permute-done((bf16[128,1024]{1,0:T(8,128)(2,1)S(1)}, bf16[128,1024]{1,0:T(8,128)(2,1)S(1)}, u32[]{:S(2)}, u32[]{:S(2)}) %collective-permute-start.5) | collective-permute-done | bytes 262176 | tf_op jit(solution)/shard_map/ppermute | solution.py:421
  72.4 0.8 %combine.1 = bf16[128,2048]{1,0:T(8,128)(2,1)} custom-call(bf16[128,1024]{1,0:T(8,128)(2,1)S(1)} %attend_rest.1.mine, bf16[128,1024]{1,0:T(8,128)(2,1)S(1)} %collective-permute-done.5.others), custom_call_target="tpu_custom_call" | custom-call | tf_op jit(solution)/shard_map/combine/pallas_call | solution.py:423
Async XLA Ops:
  0.0 14.8 %copy-start = (bf16[128,2048]{1,0:T(8,128)(2,1)S(1)}, bf16[128,2048]{1,0:T(8,128)(2,1)}, u32[]{:S(2)}) copy-start(bf16[128,2048]{1,0:T(8,128)(2,1)} %queries.1) | copy-start | bytes 1572868
  0.0 14.8 %copy-start.1 = (s32[65536]{0:T(1024)S(1)}, s32[65536]{0:T(1024)}, u32[]{:S(2)}) copy-start(s32[65536]{0:T(1024)} %param.13) | copy-start | bytes 786436
  0.0 42.2 %copy-start.3 = (s32[64]{0:T(128)S(1)}, s32[64]{0:T(128)}, u32[]{:S(2)}) copy-start(s32[64]{0:T(128)} %refs_0_.7) | copy-start | bytes 772
  3.1 27.4 %all-to-all-start = ((bf16[8,256,128]{2,1,0:T(8,128)(2,1)}), bf16[8,256,128]{2,1,0:T(8,128)(2,1)S(1)}, u32[]{:S(2)}, u32[]{:S(2)}) async-start(bf16[8,256,128]{2,1,0:T(8,128)(2,1)} %get-tuple-element.31), calls=%async_computation | async-start | bytes 1048576 | tf_op jit(solution)/shard_map/all_to_all | solution.py:383
  10.8 9.3 %collective-permute-start = (bf16[128,1024]{1,0:T(8,128)(2,1)}, bf16[128,1024]{1,0:T(8,128)(2,1)S(1)}, u32[]{:S(2)}, u32[]{:S(2)}) collective-permute-start(bf16[128,1024]{1,0:T(8,128)(2,1)} %get-tuple-element.34), channel_id=1, source_target_pairs={{0,2},{1,3},{2,0},{3,1},{4,6},{5,7},{6,4},{7,5},{8,14},{9,15},{10,... | collective-permute-start | bytes 786440 | tf_op jit(solution)/shard_map/ppermute | solution.py:387
  14.8 0.9 %copy-start.2 = (f32[3,128,128]{2,1,0:T(8,128)S(1)}, f32[3,128,128]{2,1,0:T(8,128)}, u32[]{:S(2)}) copy-start(f32[3,128,128]{2,1,0:T(8,128)} %get-tuple-element.32.tables) | copy-start | bytes 589828
  30.4 19.4 %collective-permute-start.2 = (bf16[8,256,128]{2,1,0:T(8,128)(2,1)S(1)}, bf16[8,256,128]{2,1,0:T(8,128)(2,1)S(1)}, u32[]{:S(2)}, u32[]{:S(2)}) collective-permute-start(bf16[8,256,128]{2,1,0:T(8,128)(2,1)S(1)} %all-to-all-done.refs_5_), channel_id=1, source_target_pairs={{16,0},{32,16},{8,24},{48,32},{24,40},{64,48},{40,56},{80,64},{56,... | collective-permute-start | bytes 1572872 | tf_op jit(solution)/shard_map/ppermute | solution.py:408
  45.9 6.5 %collective-permute-start.1 = (bf16[8,256,128]{2,1,0:T(8,128)(2,1)S(1)}, bf16[8,256,128]{2,1,0:T(8,128)(2,1)S(1)}, u32[]{:S(2)}, u32[]{:S(2)}) collective-permute-start(bf16[8,256,128]{2,1,0:T(8,128)(2,1)S(1)} %all-to-all-done.refs_5_), channel_id=1, source_target_pairs={{0,8},{8,0},{16,24},{24,16},{32,40},{40,32},{48,56},{56,48},{64,72... | collective-permute-start | bytes 1572872 | tf_op jit(solution)/shard_map/ppermute | solution.py:415
  47.9 13.2 %collective-permute-start.4 = (bf16[8,256,128]{2,1,0:T(8,128)(2,1)S(1)}, bf16[8,256,128]{2,1,0:T(8,128)(2,1)S(1)}, u32[]{:S(2)}, u32[]{:S(2)}) collective-permute-start(bf16[8,256,128]{2,1,0:T(8,128)(2,1)S(1)} %all-to-all-done.refs_5_), channel_id=1, source_target_pairs={{24,8},{0,16},{40,24},{16,32},{56,40},{32,48},{72,56},{48,64},{88,... | collective-permute-start | bytes 1572872 | tf_op jit(solution)/shard_map/ppermute | solution.py:414
  49.8 11.2 %collective-permute-start.3 = (bf16[8,256,128]{2,1,0:T(8,128)(2,1)S(1)}, bf16[8,256,128]{2,1,0:T(8,128)(2,1)S(1)}, u32[]{:S(2)}, u32[]{:S(2)}) collective-permute-start(bf16[8,256,128]{2,1,0:T(8,128)(2,1)S(1)} %collective-permute-done.2.refs_5_), channel_id=1, source_target_pairs={{0,8},{8,0},{16,24},{24,16},{32,40},{40,32},{48,56},{56,48},{64,72... | collective-permute-start | bytes 1572872 | tf_op jit(solution)/shard_map/ppermute | solution.py:417
  64.1 8.3 %collective-permute-start.5 = (bf16[128,1024]{1,0:T(8,128)(2,1)S(1)}, bf16[128,1024]{1,0:T(8,128)(2,1)S(1)}, u32[]{:S(2)}, u32[]{:S(2)}) collective-permute-start(bf16[128,1024]{1,0:T(8,128)(2,1)S(1)} %get-tuple-element.56), channel_id=1, source_target_pairs={{0,2},{1,3},{2,0},{3,1},{4,6},{5,7},{6,4},{7,5},{8,14},{9,15},{10,... | collective-permute-start | bytes 786440 | tf_op jit(solution)/shard_map/ppermute | solution.py:421

commit v7 on v4

--- a/solution.py
+++ b/solution.py
@@ -398,8 +398,7 @@
         compiler_params=VMEM,
         name="rotate_own_queries",
     )(queries, tables, segment_number.reshape(BLOCKS * SHARDS, 1, ROWS))
-    ready = (own, split_own, q_partner, odds, segments)
-    own, split_own, q_partner, odds, segments = lax.optimization_barrier(ready)
+    own, split_own, odds, segments = lax.optimization_barrier((own, split_own, odds, segments))
 
     within = range(BLOCKS)
     ahead = [(i + 2 - 4 * (i % 2), i) for i in within if i + 2 - 4 * (i % 2) in within]

time: 71.8 us -> 72.9 us (1.015)
  starting transfers between devices: 31.1 us -> 29.3 us
  waiting for transfers between devices: 19.5 us -> 21.3 us
    all_to_all x1, waiting for transfers between devices: 10.3 us -> 17 us  [shards(): lax.all_to_all(payload, 'uly', split_axis=0, concat_axis=0, tiled=True)]
    ppermute x1, waiting for transfers between devices: 4.48 us -> 0.01 us  [shards(): far = lax.ppermute(own, 'blk', ahead)]
    ppermute x1, starting transfers between devices: 3.92 us -> 1.92 us  [shards(): q_partner = lax.ppermute(q_other, ('blk', 'uly'), partners)]
  transfers between devices with their start and end apart: 7 -> 7, of which waited for: 4 -> 3; matrix products, arithmetic and copies ran while one was open for 0% -> 0% of each run, Pallas kernels for 17% -> 18%
where the time goes in v7:
time: 72.9 us; the launch traced here: 71.8 us
  starting transfers between devices  29.3 us (40%)
  waiting for transfers between devices  21.3 us (29%)
  Pallas kernels  19.9 us (27%)
  local copies, waits for them, and re-layouts  0.94 us (1%)
    all_to_all x1, waiting for transfers between devices, shards(): lax.all_to_all(payload, 'uly', split_axis=0, concat_axis=0, tiled=True)  17 us
    pallas_call x4, Pallas kernels, attend(): pl.pallas_call(functools.partial(attend_kernel, sets, roles, len(laid), s...  14.5 us
    ppermute x1, starting transfers between devices, shards(): far = lax.ppermute(own, 'blk', ahead)  11.7 us
    all_to_all x1, starting transfers between devices, shards(): lax.all_to_all(payload, 'uly', split_axis=0, concat_axis=0, tiled=True)  7.91 us
    pallas_call x1, Pallas kernels, shards(): pl.pallas_call(keys_kernel, out_shape=[jax.ShapeDtypeStruct((SHARDS, 2 *...  3.03 us
    ppermute x1, waiting for transfers between devices, shards(): q_partner = lax.ppermute(q_other, ('blk', 'uly'), partners)  2.42 us
    ppermute x1, starting transfers between devices, shards(): near = lax.ppermute(own, 'blk', cores)  1.98 us
    ppermute x1, starting transfers between devices, shards(): others = lax.ppermute(to_send, ('blk', 'uly'), partners)  1.94 us
  transfers between devices with their start and end apart: 7, of which 3 were waited for; matrix products, arithmetic and copies ran while one was open for 0% of the time, Pallas kernels for 18%

profile of v7, /device:TPU:16, one launch (start us, length us, event | category | flops | bytes accessed | tf_op | source)
XLA Modules:
  0.0 71.8 jit_solution(10347512978473247570)
XLA Ops:
  0.0 0.0 copy-start
  0.0 0.0 copy-start.1
  0.0 0.0 copy-start.3
  0.0 3.0 %rotate_keys.1 = (bf16[8,256,128]{2,1,0:T(8,128)(2,1)}, f32[3,128,128]{2,1,0:T(8,128)}, bf16[128,1024]{1,0:T(8,128)(2,1)}) custom-call(s32[1,128]{1,0:T(1,128)} %bitcast.4, s32[1,128]{1,0:T(1,128)} %bitcast.5, f32[1,128]{1,0:T(1,128)} %constant.2.clone.refs_2_, bf16[128,256]{1,0:T(8,128)(2,1)} %refs_3_.1, bf16[128,256]{1,0:T(8,128)(2,1)} %refs_4_.1, ...), custom_call_target="tpu_custom_call" | custom-call | tf_op jit(solution)/shard_map/rotate_keys/pallas_call | solution.py:363
  3.1 0.0 copy-start.4
  3.1 7.9 %all-to-all-start = ((bf16[8,256,128]{2,1,0:T(8,128)(2,1)}), bf16[8,256,128]{2,1,0:T(8,128)(2,1)S(1)}, u32[]{:S(2)}, u32[]{:S(2)}) async-start(bf16[8,256,128]{2,1,0:T(8,128)(2,1)} %get-tuple-element.27), calls=%async_computation | async-start | bytes 1048576 | tf_op jit(solution)/shard_map/all_to_all | solution.py:383
  11.0 0.0 copy-done
  11.0 0.0 copy-done.1
  11.0 0.0 copy-start.2
  11.0 0.9 %copy-done.2 = f32[3,128,128]{2,1,0:T(8,128)S(1)} copy-done((f32[3,128,128]{2,1,0:T(8,128)S(1)}, f32[3,128,128]{2,1,0:T(8,128)}, u32[]{:S(2)}) %copy-start.2) | copy-done | bytes 196632
  11.9 1.6 %rotate_own_queries.1 = (bf16[256,1024]{1,0:T(8,128)(2,1)S(1)}, bf16[5120,128]{1,0:T(8,128)(2,1)S(1)}, s32[40,1,128]{2,1,0:T(1,128)S(1)}) custom-call(bf16[128,2048]{1,0:T(8,128)(2,1)S(1)} %copy-done, f32[3,128,128]{2,1,0:T(8,128)S(1)} %copy-done.2, s32[512,1,128]{2,1,0:T(1,128)S(1)} %bitcast.3), custom_call_target="tpu_custom_call" | custom-call | tf_op jit(solution)/shard_map/rotate_own_queries/pallas_call | solution.py:388
  13.5 17.0 %all-to-all-done.refs_5_ = bf16[8,256,128]{2,1,0:T(8,128)(2,1)S(1)} async-done(((bf16[8,256,128]{2,1,0:T(8,128)(2,1)}), bf16[8,256,128]{2,1,0:T(8,128)(2,1)S(1)}, u32[]{:S(2)}, u32[]{:S(2)}) %all-to-all-start) | async-done | bytes 524320 | tf_op jit(solution)/shard_map/all_to_all | solution.py:383
  30.6 11.7 %collective-permute-start.2 = (bf16[8,256,128]{2,1,0:T(8,128)(2,1)S(1)}, bf16[8,256,128]{2,1,0:T(8,128)(2,1)S(1)}, u32[]{:S(2)}, u32[]{:S(2)}) collective-permute-start(bf16[8,256,128]{2,1,0:T(8,128)(2,1)S(1)} %all-to-all-done.refs_5_), channel_id=1, source_target_pairs={{16,0},{32,16},{8,24},{48,32},{24,40},{64,48},{40,56},{80,64},{56,... | collective-permute-start | bytes 1572872 | tf_op jit(solution)/shard_map/ppermute | solution.py:407
  42.3 0.0 copy-done.4
  42.3 1.9 %collective-permute-start = (bf16[128,1024]{1,0:T(8,128)(2,1)S(1)}, bf16[128,1024]{1,0:T(8,128)(2,1)S(1)}, u32[]{:S(2)}, u32[]{:S(2)}) collective-permute-start(bf16[128,1024]{1,0:T(8,128)(2,1)S(1)} %copy-done.4), channel_id=1, source_target_pairs={{0,2},{1,3},{2,0},{3,1},{4,6},{5,7},{6,4},{7,5},{8,14},{9,15},{10,... | collective-permute-start | bytes 786440 | tf_op jit(solution)/shard_map/ppermute | solution.py:387
  44.2 1.9 %collective-permute-start.4 = (bf16[8,256,128]{2,1,0:T(8,128)(2,1)S(1)}, bf16[8,256,128]{2,1,0:T(8,128)(2,1)S(1)}, u32[]{:S(2)}, u32[]{:S(2)}) collective-permute-start(bf16[8,256,128]{2,1,0:T(8,128)(2,1)S(1)} %all-to-all-done.refs_5_), channel_id=1, source_target_pairs={{24,8},{0,16},{40,24},{16,32},{56,40},{32,48},{72,56},{48,64},{88,... | collective-permute-start | bytes 1572872 | tf_op jit(solution)/shard_map/ppermute | solution.py:408
  46.2 2.0 %collective-permute-start.1 = (bf16[8,256,128]{2,1,0:T(8,128)(2,1)S(1)}, bf16[8,256,128]{2,1,0:T(8,128)(2,1)S(1)}, u32[]{:S(2)}, u32[]{:S(2)}) collective-permute-start(bf16[8,256,128]{2,1,0:T(8,128)(2,1)S(1)} %all-to-all-done.refs_5_), channel_id=1, source_target_pairs={{0,8},{8,0},{16,24},{24,16},{32,40},{40,32},{48,56},{56,48},{64,72... | collective-permute-start | bytes 1572872 | tf_op jit(solution)/shard_map/ppermute | solution.py:409
  48.2 2.4 %collective-permute-done.refs_3_ = bf16[128,1024]{1,0:T(8,128)(2,1)S(1)} collective-permute-done((bf16[128,1024]{1,0:T(8,128)(2,1)S(1)}, bf16[128,1024]{1,0:T(8,128)(2,1)S(1)}, u32[]{:S(2)}, u32[]{:S(2)}) %collective-permute-start) | collective-permute-done | bytes 262176 | tf_op jit(solution)/shard_map/ppermute | solution.py:387
  50.6 0.0 copy-done.3
  50.6 3.8 %attend_own.1 = (f32[144,1024]{1,0:T(8,128)S(1)}, f32[144,1024]{1,0:T(8,128)S(1)}, bf16[256,1024]{1,0:T(8,128)(2,1)S(1)}) custom-call(s32[64]{0:T(128)S(1)} %copy-done.3, s32[40,1,128]{2,1,0:T(1,128)S(1)} %get-tuple-element.32.refs_1_, bf16[5120,128]{1,0:T(8,128)(2,1)S(1)} %get-tuple-element.33.refs_2_, bf16[128,1024]{1,0:T(8,128)(2,1)S(1)} %collective-permute-done.refs_3_, ...), custom_call_target="tpu_custom_call" | custom-call | flops 2147483648 | bytes 1048576 | tf_op jit(solution)/shard_map/attend_own/pallas_call | solution.py:343
  54.4 0.0 collective-permute-done.2.refs_5_
  54.4 1.9 %collective-permute-start.3 = (bf16[8,256,128]{2,1,0:T(8,128)(2,1)S(1)}, bf16[8,256,128]{2,1,0:T(8,128)(2,1)S(1)}, u32[]{:S(2)}, u32[]{:S(2)}) collective-permute-start(bf16[8,256,128]{2,1,0:T(8,128)(2,1)S(1)} %collective-permute-done.2.refs_5_), channel_id=1, source_target_pairs={{0,8},{8,0},{16,24},{24,16},{32,40},{40,32},{48,56},{56,48},{64,72... | collective-permute-start | bytes 1572872 | tf_op jit(solution)/shard_map/ppermute | solution.py:415
  56.3 0.0 collective-permute-done.1.refs_4_
  56.3 3.2 %attend_near.1 = (f32[144,1024]{1,0:T(8,128)S(1)}, bf16[2,1024,256]{2,1,0:T(8,128)(2,1)S(1)}, bf16[2,128,1024]{2,1,0:T(8,128)(2,1)S(1)}) custom-call(s32[64]{0:T(128)S(1)} %copy-done.3, s32[40,1,128]{2,1,0:T(1,128)S(1)} %get-tuple-element.32.refs_1_, bf16[5120,128]{1,0:T(8,128)(2,1)S(1)} %get-tuple-element.33.refs_2_, ...), custom_call_target="tpu_custom_call" | custom-call | flops 2147483648 | bytes 1048576 | tf_op jit(solution)/shard_map/attend_near/pallas_call | solution.py:343
  59.5 0.0 collective-permute-done.4.refs_5_
  59.5 0.0 collective-permute-done.3.refs_4_
  59.5 3.1 %attend_partner.1 = (bf16[128,1024]{1,0:T(8,128)(2,1)S(1)}, bf16[2,1024,256]{2,1,0:T(8,128)(2,1)S(1)}, bf16[2,128,1024]{2,1,0:T(8,128)(2,1)S(1)}) custom-call(s32[64]{0:T(128)S(1)} %copy-done.3, s32[40,1,128]{2,1,0:T(1,128)S(1)} %get-tuple-element.32.refs_1_, bf16[5120,128]{1,0:T(8,128)(2,1)S(1)} %get-tuple-element.33.refs_2_, ...), custom_call_target="tpu_custom_call" | custom-call | flops 2147483648 | bytes 1048576 | tf_op jit(solution)/shard_map/attend_partner/pallas_call | solution.py:343
  62.6 1.9 %collective-permute-start.5 = (bf16[128,1024]{1,0:T(8,128)(2,1)S(1)}, bf16[128,1024]{1,0:T(8,128)(2,1)S(1)}, u32[]{:S(2)}, u32[]{:S(2)}) collective-permute-start(bf16[128,1024]{1,0:T(8,128)(2,1)S(1)} %get-tuple-element.48), channel_id=1, source_target_pairs={{0,2},{1,3},{2,0},{3,1},{4,6},{5,7},{6,4},{7,5},{8,14},{9,15},{10,... | collective-permute-start | bytes 786440 | tf_op jit(solution)/shard_map/ppermute | solution.py:419
  64.5 4.5 %attend_rest.1.mine = bf16[128,1024]{1,0:T(8,128)(2,1)S(1)} custom-call(s32[64]{0:T(128)S(1)} %copy-done.3, s32[40,1,128]{2,1,0:T(1,128)S(1)} %get-tuple-element.32.refs_1_, bf16[5120,128]{1,0:T(8,128)(2,1)S(1)} %get-tuple-element.33.refs_2_, bf16[2,1024,256]{2,1,0:T(8,128)(2,1)S(1)} %get-tuple-element.42.refs_3_, ...), custom_call_target="tpu_custom_call" | custom-call | flops 4294967296 | bytes 1048576 | tf_op jit(solution)/shard_map/attend_rest/pallas_call | solution.py:343
  69.0 1.8 %collective-permute-done.5.others = bf16[128,1024]{1,0:T(8,128)(2,1)S(1)} collective-permute-done((bf16[128,1024]{1,0:T(8,128)(2,1)S(1)}, bf16[128,1024]{1,0:T(8,128)(2,1)S(1)}, u32[]{:S(2)}, u32[]{:S(2)}) %collective-permute-start.5) | collective-permute-done | bytes 262176 | tf_op jit(solution)/shard_map/ppermute | solution.py:419
  70.8 0.8 %combine.1 = bf16[128,2048]{1,0:T(8,128)(2,1)} custom-call(bf16[128,1024]{1,0:T(8,128)(2,1)S(1)} %attend_rest.1.mine, bf16[128,1024]{1,0:T(8,128)(2,1)S(1)} %collective-permute-done.5.others), custom_call_target="tpu_custom_call" | custom-call | tf_op jit(solution)/shard_map/combine/pallas_call | solution.py:421
Async XLA Ops:
  0.0 11.0 %copy-start = (bf16[128,2048]{1,0:T(8,128)(2,1)S(1)}, bf16[128,2048]{1,0:T(8,128)(2,1)}, u32[]{:S(2)}) copy-start(bf16[128,2048]{1,0:T(8,128)(2,1)} %queries.1) | copy-start | bytes 1572868
  0.0 11.0 %copy-start.1 = (s32[65536]{0:T(1024)S(1)}, s32[65536]{0:T(1024)}, u32[]{:S(2)}) copy-start(s32[65536]{0:T(1024)} %param.13) | copy-start | bytes 786436
  0.0 50.6 %copy-start.3 = (s32[64]{0:T(128)S(1)}, s32[64]{0:T(128)}, u32[]{:S(2)}) copy-start(s32[64]{0:T(128)} %refs_0_.7) | copy-start | bytes 772
  3.1 39.3 %copy-start.4 = (bf16[128,1024]{1,0:T(8,128)(2,1)S(1)}, bf16[128,1024]{1,0:T(8,128)(2,1)}, u32[]{:S(2)}) copy-start(bf16[128,1024]{1,0:T(8,128)(2,1)} %get-tuple-element.34) | copy-start | bytes 786436
  3.1 27.5 %all-to-all-start = ((bf16[8,256,128]{2,1,0:T(8,128)(2,1)}), bf16[8,256,128]{2,1,0:T(8,128)(2,1)S(1)}, u32[]{:S(2)}, u32[]{:S(2)}) async-start(bf16[8,256,128]{2,1,0:T(8,128)(2,1)} %get-tuple-element.27), calls=%async_computation | async-start | bytes 1048576 | tf_op jit(solution)/shard_map/all_to_all | solution.py:383
  11.0 0.9 %copy-start.2 = (f32[3,128,128]{2,1,0:T(8,128)S(1)}, f32[3,128,128]{2,1,0:T(8,128)}, u32[]{:S(2)}) copy-start(f32[3,128,128]{2,1,0:T(8,128)} %get-tuple-element.28.tables) | copy-start | bytes 589828
  30.6 23.8 %collective-permute-start.2 = (bf16[8,256,128]{2,1,0:T(8,128)(2,1)S(1)}, bf16[8,256,128]{2,1,0:T(8,128)(2,1)S(1)}, u32[]{:S(2)}, u32[]{:S(2)}) collective-permute-start(bf16[8,256,128]{2,1,0:T(8,128)(2,1)S(1)} %all-to-all-done.refs_5_), channel_id=1, source_target_pairs={{16,0},{32,16},{8,24},{48,32},{24,40},{64,48},{40,56},{80,64},{56,... | collective-permute-start | bytes 1572872 | tf_op jit(solution)/shard_map/ppermute | solution.py:407
  42.3 8.3 %collective-permute-start = (bf16[128,1024]{1,0:T(8,128)(2,1)S(1)}, bf16[128,1024]{1,0:T(8,128)(2,1)S(1)}, u32[]{:S(2)}, u32[]{:S(2)}) collective-permute-start(bf16[128,1024]{1,0:T(8,128)(2,1)S(1)} %copy-done.4), channel_id=1, source_target_pairs={{0,2},{1,3},{2,0},{3,1},{4,6},{5,7},{6,4},{7,5},{8,14},{9,15},{10,... | collective-permute-start | bytes 786440 | tf_op jit(solution)/shard_map/ppermute | solution.py:387
  44.2 15.2 %collective-permute-start.4 = (bf16[8,256,128]{2,1,0:T(8,128)(2,1)S(1)}, bf16[8,256,128]{2,1,0:T(8,128)(2,1)S(1)}, u32[]{:S(2)}, u32[]{:S(2)}) collective-permute-start(bf16[8,256,128]{2,1,0:T(8,128)(2,1)S(1)} %all-to-all-done.refs_5_), channel_id=1, source_target_pairs={{24,8},{0,16},{40,24},{16,32},{56,40},{32,48},{72,56},{48,64},{88,... | collective-permute-start | bytes 1572872 | tf_op jit(solution)/shard_map/ppermute | solution.py:408
  46.2 10.1 %collective-permute-start.1 = (bf16[8,256,128]{2,1,0:T(8,128)(2,1)S(1)}, bf16[8,256,128]{2,1,0:T(8,128)(2,1)S(1)}, u32[]{:S(2)}, u32[]{:S(2)}) collective-permute-start(bf16[8,256,128]{2,1,0:T(8,128)(2,1)S(1)} %all-to-all-done.refs_5_), channel_id=1, source_target_pairs={{0,8},{8,0},{16,24},{24,16},{32,40},{40,32},{48,56},{56,48},{64,72... | collective-permute-start | bytes 1572872 | tf_op jit(solution)/shard_map/ppermute | solution.py:409
  54.4 5.1 %collective-permute-start.3 = (bf16[8,256,128]{2,1,0:T(8,128)(2,1)S(1)}, bf16[8,256,128]{2,1,0:T(8,128)(2,1)S(1)}, u32[]{:S(2)}, u32[]{:S(2)}) collective-permute-start(bf16[8,256,128]{2,1,0:T(8,128)(2,1)S(1)} %collective-permute-done.2.refs_5_), channel_id=1, source_target_pairs={{0,8},{8,0},{16,24},{24,16},{32,40},{40,32},{48,56},{56,48},{64,72... | collective-permute-start | bytes 1572872 | tf_op jit(solution)/shard_map/ppermute | solution.py:415
  62.6 8.3 %collective-permute-start.5 = (bf16[128,1024]{1,0:T(8,128)(2,1)S(1)}, bf16[128,1024]{1,0:T(8,128)(2,1)S(1)}, u32[]{:S(2)}, u32[]{:S(2)}) collective-permute-start(bf16[128,1024]{1,0:T(8,128)(2,1)S(1)} %get-tuple-element.48), channel_id=1, source_target_pairs={{0,2},{1,3},{2,0},{3,1},{4,6},{5,7},{6,4},{7,5},{8,14},{9,15},{10,... | collective-permute-start | bytes 786440 | tf_op jit(solution)/shard_map/ppermute | solution.py:419

commit v8 on v4

--- a/solution.py
+++ b/solution.py
@@ -42,7 +42,7 @@
 
 def keys_kernel(*refs):
     place_in, offset_in, frequency, keys_in, values_in, queries_in = refs[:6]
-    payload, tables, other, place, offset, keys, values, queries, sems = refs[6:]
+    payload, tables, other, place, offset, keys, values, queries, staged, sems = refs[6:]
     group = 1 - lax.axis_index("uly") // 2 % 2
     queries_in = queries_in.at[:, pl.ds(pl.multiple_of(group * WIDTH, WIDTH), WIDTH)]
     pairs = (place_in, place), (offset_in, offset), (keys_in, keys), (values_in, values), (queries_in, queries)
@@ -63,19 +63,22 @@
     tables[0], tables[1], tables[2] = cosine, minus, plus
     copies[2].wait()
     copies[3].wait()
+    sent = []
     for group in range(2):
         lanes = slice(group * HEAD_DIM, (group + 1) * HEAD_DIM)
-        turned = rotate(keys[:, lanes].astype(jnp.float32), cosine, minus, plus).astype(jnp.bfloat16)
-        across = values[:, lanes].astype(jnp.float32).T.astype(jnp.bfloat16)
-        for x in (group, group + 2):
-            for half in range(2):
-                payload[2 * x + half, :ROWS, :] = turned
-                payload[2 * x + half, ROWS:, :] = across
+        turned = rotate(keys[:, lanes].astype(jnp.float32), cosine, minus, plus)
+        staged[group, :ROWS, :] = turned.astype(jnp.bfloat16)
+        staged[group, ROWS:, :] = values[:, lanes].astype(jnp.float32).T.astype(jnp.bfloat16)
+        for peer in (2 * group, 2 * group + 1, 2 * group + 4, 2 * group + 5):
+            sent.append(pltpu.make_async_copy(staged.at[group], payload.at[peer], sems.at[5 + len(sent)]))
+            sent[-1].start()
     copies[4].wait()
     for head in range(HEADS_PER_GROUP):
         cols = slice(head * ROWS, (head + 1) * ROWS)
         turned = rotate(queries[:, cols].astype(jnp.float32), cosine, minus, plus).astype(jnp.bfloat16)
         other[:, cols] = turned.astype(jnp.float32).T.astype(jnp.bfloat16)
+    for copy in sent:
+        copy.wait()
 
 
 def split_queries(x, odd, tip):
@@ -368,14 +371,15 @@
             jax.ShapeDtypeStruct((HEAD_DIM, WIDTH), jnp.bfloat16),
         ],
         in_specs=[hbm, hbm, vmem, hbm, hbm, hbm],
-        out_specs=[vmem, vmem, vmem],
+        out_specs=[hbm, vmem, vmem],
         scratch_shapes=[
             pltpu.VMEM((1, ROWS), jnp.int32),
             pltpu.VMEM((1, ROWS), jnp.int32),
             pltpu.VMEM((ROWS, 2 * HEAD_DIM), jnp.bfloat16),
             pltpu.VMEM((ROWS, 2 * HEAD_DIM), jnp.bfloat16),
             pltpu.VMEM((ROWS, WIDTH), jnp.bfloat16),
-            pltpu.SemaphoreType.DMA((5,)),
+            pltpu.VMEM((2, 2 * ROWS, HEAD_DIM), jnp.bfloat16),
+            pltpu.SemaphoreType.DMA((13,)),
         ],
         compiler_params=pltpu.CompilerParams(vmem_limit_bytes=KEYS_VMEM),
         name="rotate_keys",

time: 71.8 us -> 72.7 us (1.013)
  Pallas kernels: 19.3 us -> 20.3 us
  transfers between devices with their start and end apart: 7 -> 7, of which waited for: 4 -> 4; matrix products, arithmetic and copies ran while one was open for 0% -> 0% of each run, Pallas kernels for 17% -> 18%
where the time goes in v8:
time: 72.7 us; the launch traced here: 71.6 us
  starting transfers between devices  31.1 us (43%)
  Pallas kernels  20.3 us (28%)
  waiting for transfers between devices  19 us (26%)
  local copies, waits for them, and re-layouts  0.93 us (1%)
    pallas_call x4, Pallas kernels, attend(): pl.pallas_call(functools.partial(attend_kernel, sets, roles, len(laid), s...  14.3 us
    ppermute x1, starting transfers between devices, shards(): far = lax.ppermute(own, 'blk', ahead)  11.7 us
    all_to_all x1, waiting for transfers between devices, shards(): lax.all_to_all(payload, 'uly', split_axis=0, concat_axis=0, tiled=True)  10.3 us
    all_to_all x1, starting transfers between devices, shards(): lax.all_to_all(payload, 'uly', split_axis=0, concat_axis=0, tiled=True)  7.78 us
    ppermute x1, waiting for transfers between devices, shards(): far = lax.ppermute(own, 'blk', ahead)  3.97 us
    ppermute x1, starting transfers between devices, shards(): q_partner = lax.ppermute(q_other, ('blk', 'uly'), partners)  3.92 us
    pallas_call x1, Pallas kernels, shards(): pl.pallas_call(keys_kernel, out_shape=[jax.ShapeDtypeStruct((SHARDS, 2 *...  3.51 us
    ppermute x1, waiting for transfers between devices, shards(): q_partner = lax.ppermute(q_other, ('blk', 'uly'), partners)  2.85 us
  transfers between devices with their start and end apart: 7, of which 4 were waited for; matrix products, arithmetic and copies ran while one was open for 0% of the time, Pallas kernels for 18%

profile of v8, /device:TPU:16, one launch (start us, length us, event | category | flops | bytes accessed | tf_op | source)
XLA Modules:
  0.0 71.6 jit_solution(9761561538817766436)
XLA Ops:
  0.0 0.0 copy-start
  0.0 0.0 copy-start.1
  0.0 0.0 copy-start.3
  0.0 3.5 %rotate_keys.1 = (bf16[8,256,128]{2,1,0:T(8,128)(2,1)}, f32[3,128,128]{2,1,0:T(8,128)}, bf16[128,1024]{1,0:T(8,128)(2,1)}) custom-call(s32[1,128]{1,0:T(1,128)} %bitcast.4, s32[1,128]{1,0:T(1,128)} %bitcast.5, f32[1,128]{1,0:T(1,128)} %constant.2.clone.refs_2_, bf16[128,256]{1,0:T(8,128)(2,1)} %refs_3_.1, bf16[128,256]{1,0:T(8,128)(2,1)} %refs_4_.1, ...), custom_call_target="tpu_custom_call" | custom-call | tf_op jit(solution)/shard_map/rotate_keys/pallas_call | solution.py:366
  3.5 7.8 %all-to-all-start = ((bf16[8,256,128]{2,1,0:T(8,128)(2,1)}), bf16[8,256,128]{2,1,0:T(8,128)(2,1)S(1)}, u32[]{:S(2)}, u32[]{:S(2)}) async-start(bf16[8,256,128]{2,1,0:T(8,128)(2,1)} %get-tuple-element.28), calls=%async_computation | async-start | bytes 1048576 | tf_op jit(solution)/shard_map/all_to_all | solution.py:387
  11.3 3.9 %collective-permute-start = (bf16[128,1024]{1,0:T(8,128)(2,1)}, bf16[128,1024]{1,0:T(8,128)(2,1)S(1)}, u32[]{:S(2)}, u32[]{:S(2)}) collective-permute-start(bf16[128,1024]{1,0:T(8,128)(2,1)} %get-tuple-element.31), channel_id=1, source_target_pairs={{0,2},{1,3},{2,0},{3,1},{4,6},{5,7},{6,4},{7,5},{8,14},{9,15},{10,... | collective-permute-start | bytes 786440 | tf_op jit(solution)/shard_map/ppermute | solution.py:391
  15.2 0.0 copy-done
  15.2 0.0 copy-done.1
  15.3 0.0 copy-start.2
  15.3 0.9 %copy-done.2 = f32[3,128,128]{2,1,0:T(8,128)S(1)} copy-done((f32[3,128,128]{2,1,0:T(8,128)S(1)}, f32[3,128,128]{2,1,0:T(8,128)}, u32[]{:S(2)}) %copy-start.2) | copy-done | bytes 196632
  16.2 1.6 %rotate_own_queries.1 = (bf16[256,1024]{1,0:T(8,128)(2,1)S(1)}, bf16[5120,128]{1,0:T(8,128)(2,1)S(1)}, s32[40,1,128]{2,1,0:T(1,128)S(1)}) custom-call(bf16[128,2048]{1,0:T(8,128)(2,1)S(1)} %copy-done, f32[3,128,128]{2,1,0:T(8,128)S(1)} %copy-done.2, s32[512,1,128]{2,1,0:T(1,128)S(1)} %bitcast.3), custom_call_target="tpu_custom_call" | custom-call | tf_op jit(solution)/shard_map/rotate_own_queries/pallas_call | solution.py:392
  17.8 2.8 %collective-permute-done.refs_3_ = bf16[128,1024]{1,0:T(8,128)(2,1)S(1)} collective-permute-done((bf16[128,1024]{1,0:T(8,128)(2,1)}, bf16[128,1024]{1,0:T(8,128)(2,1)S(1)}, u32[]{:S(2)}, u32[]{:S(2)}) %collective-permute-start) | collective-permute-done | bytes 262176 | tf_op jit(solution)/shard_map/ppermute | solution.py:391
  20.6 10.3 %all-to-all-done.refs_5_ = bf16[8,256,128]{2,1,0:T(8,128)(2,1)S(1)} async-done(((bf16[8,256,128]{2,1,0:T(8,128)(2,1)}), bf16[8,256,128]{2,1,0:T(8,128)(2,1)S(1)}, u32[]{:S(2)}, u32[]{:S(2)}) %all-to-all-start) | async-done | bytes 524320 | tf_op jit(solution)/shard_map/all_to_all | solution.py:387
  30.9 11.7 %collective-permute-start.2 = (bf16[8,256,128]{2,1,0:T(8,128)(2,1)S(1)}, bf16[8,256,128]{2,1,0:T(8,128)(2,1)S(1)}, u32[]{:S(2)}, u32[]{:S(2)}) collective-permute-start(bf16[8,256,128]{2,1,0:T(8,128)(2,1)S(1)} %all-to-all-done.refs_5_), channel_id=1, source_target_pairs={{16,0},{32,16},{8,24},{48,32},{24,40},{64,48},{40,56},{80,64},{56,... | collective-permute-start | bytes 1572872 | tf_op jit(solution)/shard_map/ppermute | solution.py:412
  42.6 1.9 %collective-permute-start.4 = (bf16[8,256,128]{2,1,0:T(8,128)(2,1)S(1)}, bf16[8,256,128]{2,1,0:T(8,128)(2,1)S(1)}, u32[]{:S(2)}, u32[]{:S(2)}) collective-permute-start(bf16[8,256,128]{2,1,0:T(8,128)(2,1)S(1)} %all-to-all-done.refs_5_), channel_id=1, source_target_pairs={{24,8},{0,16},{40,24},{16,32},{56,40},{32,48},{72,56},{48,64},{88,... | collective-permute-start | bytes 1572872 | tf_op jit(solution)/shard_map/ppermute | solution.py:413
  44.6 1.9 %collective-permute-start.1 = (bf16[8,256,128]{2,1,0:T(8,128)(2,1)S(1)}, bf16[8,256,128]{2,1,0:T(8,128)(2,1)S(1)}, u32[]{:S(2)}, u32[]{:S(2)}) collective-permute-start(bf16[8,256,128]{2,1,0:T(8,128)(2,1)S(1)} %all-to-all-done.refs_5_), channel_id=1, source_target_pairs={{0,8},{8,0},{16,24},{24,16},{32,40},{40,32},{48,56},{56,48},{64,72... | collective-permute-start | bytes 1572872 | tf_op jit(solution)/shard_map/ppermute | solution.py:414
  46.5 0.0 copy-done.3
  46.5 3.7 %attend_own.1 = (f32[144,1024]{1,0:T(8,128)S(1)}, f32[144,1024]{1,0:T(8,128)S(1)}, bf16[256,1024]{1,0:T(8,128)(2,1)S(1)}) custom-call(s32[64]{0:T(128)S(1)} %copy-done.3, s32[40,1,128]{2,1,0:T(1,128)S(1)} %get-tuple-element.34.refs_1_, bf16[5120,128]{1,0:T(8,128)(2,1)S(1)} %get-tuple-element.35.refs_2_, bf16[128,1024]{1,0:T(8,128)(2,1)S(1)} %collective-permute-done.refs_3_, ...), custom_call_target="tpu_custom_call" | custom-call | flops 2147483648 | bytes 1048576 | tf_op jit(solution)/shard_map/attend_own/pallas_call | solution.py:346
  50.3 4.0 %collective-permute-done.2.refs_5_ = bf16[8,256,128]{2,1,0:T(8,128)(2,1)S(1)} collective-permute-done((bf16[8,256,128]{2,1,0:T(8,128)(2,1)S(1)}, bf16[8,256,128]{2,1,0:T(8,128)(2,1)S(1)}, u32[]{:S(2)}, u32[]{:S(2)}) %collective-permute-start.2) | collective-permute-done | bytes 524320 | tf_op jit(solution)/shard_map/ppermute | solution.py:412
  54.2 1.9 %collective-permute-start.3 = (bf16[8,256,128]{2,1,0:T(8,128)(2,1)S(1)}, bf16[8,256,128]{2,1,0:T(8,128)(2,1)S(1)}, u32[]{:S(2)}, u32[]{:S(2)}) collective-permute-start(bf16[8,256,128]{2,1,0:T(8,128)(2,1)S(1)} %collective-permute-done.2.refs_5_), channel_id=1, source_target_pairs={{0,8},{8,0},{16,24},{24,16},{32,40},{40,32},{48,56},{56,48},{64,72... | collective-permute-start | bytes 1572872 | tf_op jit(solution)/shard_map/ppermute | solution.py:420
  56.1 0.0 collective-permute-done.1.refs_4_
  56.2 3.1 %attend_near.1 = (f32[144,1024]{1,0:T(8,128)S(1)}, bf16[2,1024,256]{2,1,0:T(8,128)(2,1)S(1)}, bf16[2,128,1024]{2,1,0:T(8,128)(2,1)S(1)}) custom-call(s32[64]{0:T(128)S(1)} %copy-done.3, s32[40,1,128]{2,1,0:T(1,128)S(1)} %get-tuple-element.34.refs_1_, bf16[5120,128]{1,0:T(8,128)(2,1)S(1)} %get-tuple-element.35.refs_2_, ...), custom_call_target="tpu_custom_call" | custom-call | flops 2147483648 | bytes 1048576 | tf_op jit(solution)/shard_map/attend_near/pallas_call | solution.py:346
  59.2 0.0 collective-permute-done.4.refs_5_
  59.3 0.0 collective-permute-done.3.refs_4_
  59.3 3.1 %attend_partner.1 = (bf16[128,1024]{1,0:T(8,128)(2,1)S(1)}, bf16[2,1024,256]{2,1,0:T(8,128)(2,1)S(1)}, bf16[2,128,1024]{2,1,0:T(8,128)(2,1)S(1)}) custom-call(s32[64]{0:T(128)S(1)} %copy-done.3, s32[40,1,128]{2,1,0:T(1,128)S(1)} %get-tuple-element.34.refs_1_, bf16[5120,128]{1,0:T(8,128)(2,1)S(1)} %get-tuple-element.35.refs_2_, ...), custom_call_target="tpu_custom_call" | custom-call | flops 2147483648 | bytes 1048576 | tf_op jit(solution)/shard_map/attend_partner/pallas_call | solution.py:346
  62.3 1.9 %collective-permute-start.5 = (bf16[128,1024]{1,0:T(8,128)(2,1)S(1)}, bf16[128,1024]{1,0:T(8,128)(2,1)S(1)}, u32[]{:S(2)}, u32[]{:S(2)}) collective-permute-start(bf16[128,1024]{1,0:T(8,128)(2,1)S(1)} %get-tuple-element.50), channel_id=1, source_target_pairs={{0,2},{1,3},{2,0},{3,1},{4,6},{5,7},{6,4},{7,5},{8,14},{9,15},{10,... | collective-permute-start | bytes 786440 | tf_op jit(solution)/shard_map/ppermute | solution.py:424
  64.3 4.4 %attend_rest.1.mine = bf16[128,1024]{1,0:T(8,128)(2,1)S(1)} custom-call(s32[64]{0:T(128)S(1)} %copy-done.3, s32[40,1,128]{2,1,0:T(1,128)S(1)} %get-tuple-element.34.refs_1_, bf16[5120,128]{1,0:T(8,128)(2,1)S(1)} %get-tuple-element.35.refs_2_, bf16[2,1024,256]{2,1,0:T(8,128)(2,1)S(1)} %get-tuple-element.44.refs_3_, ...), custom_call_target="tpu_custom_call" | custom-call | flops 4294967296 | bytes 1048576 | tf_op jit(solution)/shard_map/attend_rest/pallas_call | solution.py:346
  68.7 1.9 %collective-permute-done.5.others = bf16[128,1024]{1,0:T(8,128)(2,1)S(1)} collective-permute-done((bf16[128,1024]{1,0:T(8,128)(2,1)S(1)}, bf16[128,1024]{1,0:T(8,128)(2,1)S(1)}, u32[]{:S(2)}, u32[]{:S(2)}) %collective-permute-start.5) | collective-permute-done | bytes 262176 | tf_op jit(solution)/shard_map/ppermute | solution.py:424
  70.6 0.8 %combine.1 = bf16[128,2048]{1,0:T(8,128)(2,1)} custom-call(bf16[128,1024]{1,0:T(8,128)(2,1)S(1)} %attend_rest.1.mine, bf16[128,1024]{1,0:T(8,128)(2,1)S(1)} %collective-permute-done.5.others), custom_call_target="tpu_custom_call" | custom-call | tf_op jit(solution)/shard_map/combine/pallas_call | solution.py:426
Async XLA Ops:
  0.0 15.2 %copy-start = (bf16[128,2048]{1,0:T(8,128)(2,1)S(1)}, bf16[128,2048]{1,0:T(8,128)(2,1)}, u32[]{:S(2)}) copy-start(bf16[128,2048]{1,0:T(8,128)(2,1)} %queries.1) | copy-start | bytes 1572868
  0.0 15.2 %copy-start.1 = (s32[65536]{0:T(1024)S(1)}, s32[65536]{0:T(1024)}, u32[]{:S(2)}) copy-start(s32[65536]{0:T(1024)} %param.13) | copy-start | bytes 786436
  0.0 46.5 %copy-start.3 = (s32[64]{0:T(128)S(1)}, s32[64]{0:T(128)}, u32[]{:S(2)}) copy-start(s32[64]{0:T(128)} %refs_0_.7) | copy-start | bytes 772
  3.5 27.4 %all-to-all-start = ((bf16[8,256,128]{2,1,0:T(8,128)(2,1)}), bf16[8,256,128]{2,1,0:T(8,128)(2,1)S(1)}, u32[]{:S(2)}, u32[]{:S(2)}) async-start(bf16[8,256,128]{2,1,0:T(8,128)(2,1)} %get-tuple-element.28), calls=%async_computation | async-start | bytes 1048576 | tf_op jit(solution)/shard_map/all_to_all | solution.py:387
  11.3 9.3 %collective-permute-start = (bf16[128,1024]{1,0:T(8,128)(2,1)}, bf16[128,1024]{1,0:T(8,128)(2,1)S(1)}, u32[]{:S(2)}, u32[]{:S(2)}) collective-permute-start(bf16[128,1024]{1,0:T(8,128)(2,1)} %get-tuple-element.31), channel_id=1, source_target_pairs={{0,2},{1,3},{2,0},{3,1},{4,6},{5,7},{6,4},{7,5},{8,14},{9,15},{10,... | collective-permute-start | bytes 786440 | tf_op jit(solution)/shard_map/ppermute | solution.py:391
  15.3 0.9 %copy-start.2 = (f32[3,128,128]{2,1,0:T(8,128)S(1)}, f32[3,128,128]{2,1,0:T(8,128)}, u32[]{:S(2)}) copy-start(f32[3,128,128]{2,1,0:T(8,128)} %get-tuple-element.29.tables) | copy-start | bytes 589828
  30.9 23.3 %collective-permute-start.2 = (bf16[8,256,128]{2,1,0:T(8,128)(2,1)S(1)}, bf16[8,256,128]{2,1,0:T(8,128)(2,1)S(1)}, u32[]{:S(2)}, u32[]{:S(2)}) collective-permute-start(bf16[8,256,128]{2,1,0:T(8,128)(2,1)S(1)} %all-to-all-done.refs_5_), channel_id=1, source_target_pairs={{16,0},{32,16},{8,24},{48,32},{24,40},{64,48},{40,56},{80,64},{56,... | collective-permute-start | bytes 1572872 | tf_op jit(solution)/shard_map/ppermute | solution.py:412
  42.6 16.6 %collective-permute-start.4 = (bf16[8,256,128]{2,1,0:T(8,128)(2,1)S(1)}, bf16[8,256,128]{2,1,0:T(8,128)(2,1)S(1)}, u32[]{:S(2)}, u32[]{:S(2)}) collective-permute-start(bf16[8,256,128]{2,1,0:T(8,128)(2,1)S(1)} %all-to-all-done.refs_5_), channel_id=1, source_target_pairs={{24,8},{0,16},{40,24},{16,32},{56,40},{32,48},{72,56},{48,64},{88,... | collective-permute-start | bytes 1572872 | tf_op jit(solution)/shard_map/ppermute | solution.py:413
  44.6 11.6 %collective-permute-start.1 = (bf16[8,256,128]{2,1,0:T(8,128)(2,1)S(1)}, bf16[8,256,128]{2,1,0:T(8,128)(2,1)S(1)}, u32[]{:S(2)}, u32[]{:S(2)}) collective-permute-start(bf16[8,256,128]{2,1,0:T(8,128)(2,1)S(1)} %all-to-all-done.refs_5_), channel_id=1, source_target_pairs={{0,8},{8,0},{16,24},{24,16},{32,40},{40,32},{48,56},{56,48},{64,72... | collective-permute-start | bytes 1572872 | tf_op jit(solution)/shard_map/ppermute | solution.py:414
  54.2 5.0 %collective-permute-start.3 = (bf16[8,256,128]{2,1,0:T(8,128)(2,1)S(1)}, bf16[8,256,128]{2,1,0:T(8,128)(2,1)S(1)}, u32[]{:S(2)}, u32[]{:S(2)}) collective-permute-start(bf16[8,256,128]{2,1,0:T(8,128)(2,1)S(1)} %collective-permute-done.2.refs_5_), channel_id=1, source_target_pairs={{0,8},{8,0},{16,24},{24,16},{32,40},{40,32},{48,56},{56,48},{64,72... | collective-permute-start | bytes 1572872 | tf_op jit(solution)/shard_map/ppermute | solution.py:420
  62.3 8.3 %collective-permute-start.5 = (bf16[128,1024]{1,0:T(8,128)(2,1)S(1)}, bf16[128,1024]{1,0:T(8,128)(2,1)S(1)}, u32[]{:S(2)}, u32[]{:S(2)}) collective-permute-start(bf16[128,1024]{1,0:T(8,128)(2,1)S(1)} %get-tuple-element.50), channel_id=1, source_target_pairs={{0,2},{1,3},{2,0},{3,1},{4,6},{5,7},{6,4},{7,5},{8,14},{9,15},{10,... | collective-permute-start | bytes 786440 | tf_op jit(solution)/shard_map/ppermute | solution.py:424
